TPU v7x, 128 devices: a whole 4x4x4 slice. The times are simulated.
128 devices in a mesh: ctx: 32 (over y, z, x_lo), wt: 4 (over x_hi, core).
Axes of the slice: x: 4 (x_hi: 2, x_lo: 2; x = x_hi * 2 + x_lo), y: 4, z: 4, core: 2. Of those that a mesh axis runs over, the one named last changes fastest.
Arguments:
- inputs: bfloat16 [4, 4096, 1600], P('wt', 'ctx'), may hold values from -6 to 6
- block_order: int32 [4, 32], P('wt'), may hold values from 0 to 31, as said below
- cotangent: bfloat16 [4, 4096, 1600], P('wt', 'ctx'), may hold values from -6 to 6
- ln1_gain: bfloat16 [1600], P('wt'), may hold values from 0.5 to 1.5
- ln1_bias: bfloat16 [1600], P('wt'), may hold values from -1.25 to 1.25
- w_qkv: bfloat16 [1600, 4800], P('wt'), may hold values from -0.15625 to 0.15625
- bias_q: bfloat16 [1600], P('wt'), may hold values from -1.25 to 1.25
- bias_v: bfloat16 [1600], P('wt'), may hold values from -1.25 to 1.25
- w_out: bfloat16 [1600, 1600], P('wt'), may hold values from -2.5 to 2.5
- bias_out: bfloat16 [1600], P('wt'), may hold values from -1.25 to 1.25
- ln2_gain: bfloat16 [1600], P('wt'), may hold values from 0.5 to 1.5
- ln2_bias: bfloat16 [1600], P('wt'), may hold values from -1.25 to 1.25
- w_fc: bfloat16 [1600, 6400], P('wt'), may hold values from -0.15625 to 0.15625
- bias_fc: bfloat16 [6400], P('wt'), may hold values from -1.25 to 1.25
- w_proj: bfloat16 [6400, 1600], P('wt'), may hold values from -0.078125 to 0.078125
- bias_proj: bfloat16 [1600], P('wt'), may hold values from -1.25 to 1.25
Outputs:
- outputs: bfloat16 [4, 4096, 1600], P('wt', 'ctx')
- grad_inputs: float32 [4, 4096, 1600], P('wt', 'ctx')
- grad_ln1_gain: float32 [1600], P('wt')
- grad_ln1_bias: float32 [1600], P('wt')
- grad_w_qkv: float32 [1600, 4800], P('wt')
- grad_bias_q: float32 [1600], P('wt')
- grad_bias_v: float32 [1600], P('wt')
- grad_w_out: float32 [1600, 1600], P('wt')
- grad_bias_out: float32 [1600], P('wt')
- grad_ln2_gain: float32 [1600], P('wt')
- grad_ln2_bias: float32 [1600], P('wt')
- grad_w_fc: float32 [1600, 6400], P('wt')
- grad_bias_fc: float32 [6400], P('wt')
- grad_w_proj: float32 [6400, 1600], P('wt')
- grad_bias_proj: float32 [1600], P('wt')
Inputs may be any that keep to these rules, and one draw needn't show every extreme that they name: Each row of block_order names every block place 0 to 31 exactly once.
All inputs are finite; a program needn't handle non-finite values.
Results may differ from a plain program's by a relative error of at most 0.028.
Values may be sent and summed in bfloat16 or wider, within the bound.
A program may use at most 320 MiB of HBM per device.

v0:
```python
import math

import jax
import jax.numpy as jnp
from jax import lax
from jax.sharding import PartitionSpec as P

HEADS = 25
HEAD_DIM = 64


EPS = 1e-05
NEG = -1e30


def passed_along(value, axis, steps):
    count = lax.axis_size(axis)
    pairs = [(source, (source + steps) % count) for source in range(count)]
    return lax.ppermute(value, axis, pairs)


def layer_norm(values, gain_row, shift_row):
    centered = values - jnp.mean(values, axis=-1, keepdims=True)
    variance = jnp.mean(centered * centered, axis=-1, keepdims=True)
    return centered * lax.rsqrt(variance + EPS) * gain_row + shift_row


def gelu_tanh(values):
    return jax.nn.gelu(values, approximate=True)


def contract_rows(left, right):
    return lax.dot_general(
        left, right, (((0,), (0,)), ((), ())), preferred_element_type=jnp.float32
    )


def contract_cols(left, right):
    return lax.dot_general(
        left, right, (((1,), (1,)), ((), ())), preferred_element_type=jnp.float32
    )


def split_heads(values):
    return values.reshape(values.shape[0], HEADS, values.shape[1] // HEADS)


def places(layout, first_row, piece_rows, shard_rows):
    row_ids = first_row + jnp.arange(piece_rows, dtype=jnp.int32)
    owners = row_ids // shard_rows
    slot_ids = jnp.arange(layout.shape[0], dtype=jnp.int32)
    picked = jnp.sum(jnp.where(owners[:, None] == slot_ids[None, :], layout[None, :], 0), axis=1)
    return picked * shard_rows + row_ids % shard_rows


def by_blocks(step_fn, carried, pieces):
    length = pieces[0].shape[0]
    step_rows = math.gcd(length, 512)

    def one_block(block_index, current):
        pieces_now = tuple(
            (
                lax.dynamic_slice_in_dim(member, block_index * step_rows, step_rows, 0)
                for member in pieces
            )
        )
        return step_fn(current, pieces_now, block_index * step_rows)

    return lax.fori_loop(0, length // step_rows, one_block, carried)


def reduce_grads(first_matrix, second_matrix, vectors):
    wt_count = lax.axis_size("wt")
    vector_rows = jnp.concatenate([member.reshape(wt_count, -1) for member in vectors], axis=1)
    owned_part = (
        lax.psum_scatter(
            first_matrix.astype(jnp.bfloat16), "wt", scatter_dimension=0, tiled=True
        ).astype(jnp.float32),
        lax.psum_scatter(
            second_matrix.astype(jnp.bfloat16), "wt", scatter_dimension=0, tiled=True
        ).astype(jnp.float32),
        lax.psum_scatter(
            vector_rows.astype(jnp.bfloat16), "wt", scatter_dimension=0, tiled=True
        ).astype(jnp.float32),
    )
    summed = (
        lax.psum(owned_part[0].astype(jnp.bfloat16), "ctx").astype(jnp.float32),
        lax.psum(owned_part[1].astype(jnp.bfloat16), "ctx").astype(jnp.float32),
        lax.psum(owned_part[2].astype(jnp.bfloat16), "ctx").astype(jnp.float32),
    )
    first_sum = summed[0]
    second_sum = summed[1]
    vector_sum = summed[2].reshape(-1)
    vector_out = []
    offset = 0
    for member in vectors:
        extent = member.shape[0] // wt_count
        vector_out.append(vector_sum[offset : offset + extent])
        offset = offset + extent
    return (first_sum, second_sum, vector_out)


def unpack(gathered):
    return tuple(
        (member.astype(jnp.float32) if member.ndim == 1 else member for member in gathered)
    )


def local(
    inputs,
    block_order,
    cotangent,
    ln1_gain,
    ln1_bias,
    w_qkv,
    bias_q,
    bias_v,
    w_out,
    bias_out,
    ln2_gain,
    ln2_bias,
    w_fc,
    bias_fc,
    w_proj,
    bias_proj,
):
    gathered = unpack(
        (
            lax.all_gather(ln1_gain, "wt", axis=0, tiled=True),
            lax.all_gather(ln1_bias, "wt", axis=0, tiled=True),
            lax.all_gather(w_qkv, "wt", axis=0, tiled=True),
            lax.all_gather(bias_q, "wt", axis=0, tiled=True),
            lax.all_gather(bias_v, "wt", axis=0, tiled=True),
            lax.all_gather(w_out, "wt", axis=0, tiled=True),
            lax.all_gather(bias_out, "wt", axis=0, tiled=True),
            lax.all_gather(ln2_gain, "wt", axis=0, tiled=True),
            lax.all_gather(ln2_bias, "wt", axis=0, tiled=True),
            lax.all_gather(w_fc, "wt", axis=0, tiled=True),
            lax.all_gather(bias_fc, "wt", axis=0, tiled=True),
            lax.all_gather(w_proj, "wt", axis=0, tiled=True),
            lax.all_gather(bias_proj, "wt", axis=0, tiled=True),
        )
    )
    (
        gain_one,
        shift_one,
        full_qkv,
        full_bq,
        full_bv,
        full_out,
        full_bout,
        gain_two,
        shift_two,
        full_fc,
        full_bfc,
        full_proj,
        full_bproj,
    ) = gathered
    shard_rows = inputs.shape[1]
    features = inputs.shape[2]
    head_width = features // HEADS
    scale = HEAD_DIM ** (-0.5)
    layout = block_order[0]
    own_place = places(layout, lax.axis_index("ctx") * shard_rows, shard_rows, shard_rows)
    tokens = inputs[0].astype(jnp.float32)
    normed_one = layer_norm(tokens, gain_one, shift_one).astype(jnp.bfloat16)
    projected = jnp.dot(normed_one, full_qkv, preferred_element_type=jnp.float32)
    query_rows = (projected[:, :features] + full_bq).astype(jnp.bfloat16)
    key_rows = projected[:, features : 2 * features].astype(jnp.bfloat16)
    value_rows = (projected[:, 2 * features :] + full_bv).astype(jnp.bfloat16)
    query_heads = split_heads(query_rows)

    def forward_step(carried, pieces_now, first_row):
        row_peak, total_mass, accumulated = carried
        key_part, value_part = pieces_now
        visible = (
            places(layout, first_row, key_part.shape[0], shard_rows)[None, :] <= own_place[:, None]
        )[None]
        scores = (
            jnp.einsum(
                "qhd,khd->hqk",
                query_heads,
                split_heads(key_part),
                preferred_element_type=jnp.float32,
            )
            * scale
        )
        scores = jnp.where(visible, scores, NEG)
        new_peak = jnp.maximum(row_peak, jnp.max(scores, axis=-1))
        factor = jnp.exp(row_peak - new_peak)
        attn_weights = jnp.where(visible, jnp.exp(scores - new_peak[:, :, None]), 0.0)
        total_mass = total_mass * factor + jnp.sum(attn_weights, axis=-1)
        accumulated = accumulated * factor.T[:, :, None] + jnp.einsum(
            "hqk,khd->qhd",
            attn_weights.astype(jnp.bfloat16),
            split_heads(value_part),
            preferred_element_type=jnp.float32,
        )
        return (new_peak, total_mass, accumulated)

    start_state = (
        jnp.full((HEADS, shard_rows), NEG, jnp.float32),
        jnp.zeros((HEADS, shard_rows), jnp.float32),
        jnp.zeros((shard_rows, HEADS, head_width), jnp.float32),
    )
    row_peak, total_mass, accumulated = by_blocks(
        forward_step,
        start_state,
        (
            lax.all_gather(key_rows, "ctx", axis=0, tiled=True),
            lax.all_gather(value_rows, "ctx", axis=0, tiled=True),
        ),
    )
    attended = accumulated / total_mass.T[:, :, None]
    log_mass = row_peak + jnp.log(total_mass)
    attended_low = attended.reshape(shard_rows, features).astype(jnp.bfloat16)
    middle = (
        tokens + jnp.dot(attended_low, full_out, preferred_element_type=jnp.float32) + full_bout
    )
    normed_two = layer_norm(middle, gain_two, shift_two).astype(jnp.bfloat16)
    hidden_pre = jnp.dot(normed_two, full_fc, preferred_element_type=jnp.float32) + full_bfc
    hidden_low = gelu_tanh(hidden_pre).astype(jnp.bfloat16)
    outputs = (
        middle + jnp.dot(hidden_low, full_proj, preferred_element_type=jnp.float32) + full_bproj
    )
    (
        gain_one,
        shift_one,
        full_qkv,
        full_bq,
        full_bv,
        full_out,
        full_bout,
        gain_two,
        shift_two,
        full_fc,
        full_bfc,
        full_proj,
        full_bproj,
    ) = gathered
    upstream = cotangent[0]
    upstream_float = upstream.astype(jnp.float32)
    grad_bproj = jnp.sum(upstream_float, axis=0)
    grad_proj = contract_rows(hidden_low, upstream)
    hidden_grad = contract_cols(upstream, full_proj)
    unused_gelu, gelu_back = jax.vjp(gelu_tanh, hidden_pre)
    pre_grad = gelu_back(hidden_grad)[0].astype(jnp.bfloat16)
    grad_bfc = jnp.sum(pre_grad.astype(jnp.float32), axis=0)
    grad_fc = contract_rows(normed_two, pre_grad)
    normed_two_grad = contract_cols(pre_grad, full_fc)
    unused_norm, norm_back = jax.vjp(layer_norm, middle, gain_two, shift_two)
    middle_part, grad_gain_two, grad_shift_two = norm_back(normed_two_grad)
    middle_grad = upstream_float + middle_part
    sum_fc, sum_proj, mlp_vectors = reduce_grads(
        grad_fc, grad_proj, (grad_gain_two, grad_shift_two, grad_bfc, grad_bproj)
    )
    branch_grad = middle_grad.astype(jnp.bfloat16)
    grad_bout = jnp.sum(branch_grad.astype(jnp.float32), axis=0)
    grad_out = contract_rows(attended_low, branch_grad)
    attended_grad = contract_cols(branch_grad, full_out).astype(jnp.bfloat16)
    grad_heads = split_heads(attended_grad)
    delta_rows = jnp.sum(grad_heads.astype(jnp.float32) * attended, axis=-1)
    delta_heads = delta_rows.T
    zero_heads = jnp.zeros((shard_rows, HEADS, head_width), jnp.float32)
    ctx_count = lax.axis_size("ctx")
    own_index = lax.axis_index("ctx")

    def cycle_pair(pair_index, state):
        for half in range(2):
            grad_query, kv_pair, grad_pair = state
            turn = pair_index * 2 + half
            source = (own_index - turn) % ctx_count
            first_row = source * shard_rows
            key_heads = split_heads(kv_pair[0])
            value_heads = split_heads(kv_pair[1])
            visible = (
                places(layout, first_row, shard_rows, shard_rows)[None, :] <= own_place[:, None]
            )[None]
            scores = (
                jnp.einsum(
                    "qhd,khd->hqk", query_heads, key_heads, preferred_element_type=jnp.float32
                )
                * scale
            )
            attn_weights = jnp.where(visible, jnp.exp(scores - log_mass[:, :, None]), 0.0)
            prob_grad = jnp.einsum(
                "qhd,khd->hqk", grad_heads, value_heads, preferred_element_type=jnp.float32
            )
            score_grad = (attn_weights * (prob_grad - delta_heads[:, :, None])).astype(jnp.bfloat16)
            grad_query = (
                grad_query
                + jnp.einsum(
                    "hqk,khd->qhd", score_grad, key_heads, preferred_element_type=jnp.float32
                )
                * scale
            )
            key_added = (
                jnp.einsum(
                    "hqk,qhd->khd", score_grad, query_heads, preferred_element_type=jnp.float32
                )
                * scale
            )
            value_added = jnp.einsum(
                "hqk,qhd->khd",
                attn_weights.astype(jnp.bfloat16),
                grad_heads,
                preferred_element_type=jnp.float32,
            )
            grad_pair = grad_pair + jnp.stack([key_added, value_added])
            kv_pair = passed_along(kv_pair, "ctx", 1)
            grad_pair = passed_along(grad_pair.astype(jnp.bfloat16), "ctx", 1).astype(
                grad_pair.dtype
            )
            state = (grad_query, kv_pair, grad_pair)
        return state

    start_cycle = (
        zero_heads,
        jnp.stack([key_rows, value_rows]),
        jnp.zeros((2, shard_rows, HEADS, head_width), jnp.float32),
    )
    grad_query, unused_pair, grad_pair = lax.fori_loop(0, ctx_count // 2, cycle_pair, start_cycle)
    grad_key = grad_pair[0]
    grad_value = grad_pair[1]
    query_low = grad_query.reshape(shard_rows, features).astype(jnp.bfloat16)
    key_low = grad_key.reshape(shard_rows, features).astype(jnp.bfloat16)
    value_low = grad_value.reshape(shard_rows, features).astype(jnp.bfloat16)
    stacked = jnp.concatenate([query_low, key_low, value_low], axis=1)
    grad_bq = jnp.sum(query_low.astype(jnp.float32), axis=0)
    grad_bv = jnp.sum(value_low.astype(jnp.float32), axis=0)
    grad_qkv = contract_rows(normed_one, stacked)
    normed_one_grad = contract_cols(stacked, full_qkv)
    unused_first, first_back = jax.vjp(layer_norm, tokens, gain_one, shift_one)
    input_part, grad_gain_one, grad_shift_one = first_back(normed_one_grad)
    input_grad = middle_grad + input_part
    sum_qkv, sum_out, attn_vectors = reduce_grads(
        grad_qkv, grad_out, (grad_gain_one, grad_shift_one, grad_bq, grad_bv, grad_bout)
    )
    return (
        outputs.astype(jnp.bfloat16)[None],
        input_grad[None],
        attn_vectors[0],
        attn_vectors[1],
        sum_qkv,
        attn_vectors[2],
        attn_vectors[3],
        sum_out,
        attn_vectors[4],
        mlp_vectors[0],
        mlp_vectors[1],
        sum_fc,
        mlp_vectors[2],
        sum_proj,
        mlp_vectors[3],
    )


def solution(mesh):
    placed = (
        P("wt", "ctx", None),
        P("wt", None),
        P("wt", "ctx", None),
        P("wt"),
        P("wt"),
        P("wt", None),
        P("wt"),
        P("wt"),
        P("wt", None),
        P("wt"),
        P("wt"),
        P("wt"),
        P("wt", None),
        P("wt"),
        P("wt", None),
        P("wt"),
    )
    return jax.shard_map(
        local,
        mesh=mesh,
        in_specs=placed,
        out_specs=(
            P("wt", "ctx", None),
            P("wt", "ctx", None),
            P("wt"),
            P("wt"),
            P("wt", None),
            P("wt"),
            P("wt"),
            P("wt", None),
            P("wt"),
            P("wt"),
            P("wt"),
            P("wt", None),
            P("wt"),
            P("wt", None),
            P("wt"),
        ),
        check_vma=False,
    )
```

profile of v0, /device:TPU:1, one launch (start us, length us, event | category | flops | bytes accessed | tf_op | source)
XLA Modules:
  0.0 3485.1 jit_solution(9939901539169866123)
XLA Ops:
  27.1 89.4 %all-gather.7.cloned.1.call-done = bf16[1600,4800]{1,0:T(8,128)(2,1)} async-done(((bf16[400,4800]{1,0:T(8,128)(2,1)}), bf16[1600,4800]{1,0:T(8,128)(2,1)}) %all-gather.7.cloned.1.call-update) | async-done | bytes 15360016 | tf_op jit(solution)/shard_map/all_gather | solution.py:131
  133.7 272.9 %all-gather.9.cloned.1.call-done = bf16[4096,1600]{0,1:T(8,128)(2,1)} async-done(((bf16[128,1600]{0,1:T(8,128)(2,1)}), bf16[4096,1600]{0,1:T(8,128)(2,1)}) %all-gather.9.cloned.1.call-update) | async-done | bytes 13107216 | tf_op jit(solution)/shard_map/all_gather | solution.py:210
  406.5 288.5 %all-gather.11.cloned.1.call-done = bf16[4096,1600]{0,1:T(8,128)(2,1)} async-done(((bf16[128,1600]{0,1:T(8,128)(2,1)}), bf16[4096,1600]{0,1:T(8,128)(2,1)}) %all-gather.11.cloned.1.call-update) | async-done | bytes 13107216 | tf_op jit(solution)/shard_map/all_gather | solution.py:211
  695.0 139.2 %while.41 = (s32[]{:T(128)}, f32[25,128]{1,0:T(8,128)S(1)}, f32[25,128]{1,0:T(8,128)S(1)}, f32[128,25,64]{0,2,1:T(8,128)}, s32[1,32]{1,0:T(1,128)S(1)}, /*index=...) while((s32[]{:T(128)}, f32[25,128]{1,0:T(8,128)S(1)}, ...), condition=%wide.region_7.8_spmd.clone, body=%wide.region_3.7_spmd.clone.sunk | while | flops 441492736 | bytes 58233700 | solution.py:69
  841.3 41.4 %all-gather.15.cloned.1.call-done = bf16[1600,6400]{1,0:T(8,128)(2,1)} async-done(((bf16[400,6400]{1,0:T(8,128)(2,1)}), bf16[1600,6400]{1,0:T(8,128)(2,1)}) %all-gather.15.cloned.1.call-update) | async-done | bytes 20480016 | tf_op jit(solution)/shard_map/all_gather | solution.py:138
  894.7 126.5 %all-gather.17.cloned.1.call-done = bf16[6400,1600]{1,0:T(8,128)(2,1)} async-done(((bf16[1600,1600]{1,0:T(8,128)(2,1)}), bf16[6400,1600]{1,0:T(8,128)(2,1)}) %all-gather.17.cloned.1.call-update) | async-done | bytes 20480016 | tf_op jit(solution)/shard_map/all_gather | solution.py:140
  1055.0 1215.2 %while.42 = (s32[]{:T(128)}, f32[128,25,64]{0,2,1:T(8,128)}, bf16[2,128,1600]{1,2,0:T(8,128)(2,1)}, f32[2,128,25,64]{1,3,2,0:T(8,128)S(1)}, s32[]{:T(128)}, /*in...) while((s32[]{:T(128)}, f32[128,25,64]{0,2,1:T(8,128)}, ...), condition=%wide.region_16.17_spmd.clone, body=%wide.region_13.16_spmd.clone.sunk | while | flops 535207200 | bytes 56649008 | solution.py:322
  1083.1 24.3 collective-permute-done.2
  1111.4 31.4 collective-permute-done.3
  1166.2 17.1 collective-permute-done
  1205.3 18.6 collective-permute-done.3
  1284.5 16.7 collective-permute-done.3
  1707.2 17.9 collective-permute-done.3
  1742.8 17.4 collective-permute-done
  1775.8 19.5 collective-permute-done.3
  1811.4 19.0 collective-permute-done
  1844.4 21.3 collective-permute-done.3
  1880.2 19.0 collective-permute-done
  1914.2 21.3 collective-permute-done.3
  1952.2 19.0 collective-permute-done
  1988.4 21.3 collective-permute-done.3
  2028.5 19.0 collective-permute-done
  2066.8 21.3 collective-permute-done.3
  2109.1 18.9 collective-permute-done
  2149.9 21.2 collective-permute-done.3
  2194.1 17.0 collective-permute-done
  2233.2 19.6 collective-permute-done.3
  2308.9 123.9 %reduce-scatter.5.cloned.1.call-done = bf16[400,4800]{1,0:T(8,128)(2,1)} async-done(((bf16[1600,4800]{1,0:T(8,128)(2,1)}), bf16[400,4800]{1,0:T(8,128)(2,1)}) %reduce-scatter.5.cloned.1.call-update) | async-done | bytes 3840016 | tf_op jit(solution)/shard_map/reduce_scatter | solution.py:76
  2432.8 166.4 %reduce-scatter.9.cloned.1.call-done = bf16[400,6400]{1,0:T(8,128)(2,1)} async-done(((bf16[1600,6400]{1,0:T(8,128)(2,1)}), bf16[400,6400]{1,0:T(8,128)(2,1)}) %reduce-scatter.9.cloned.1.call-update) | async-done | bytes 5120016 | tf_op jit(solution)/shard_map/reduce_scatter | solution.py:76
  2599.3 164.2 %reduce-scatter.11.cloned.1.call-done = bf16[1600,1600]{1,0:T(8,128)(2,1)} async-done(((bf16[6400,1600]{1,0:T(8,128)(2,1)}), bf16[1600,1600]{1,0:T(8,128)(2,1)}) %reduce-scatter.11.cloned.1.call-update) | async-done | bytes 5120016 | tf_op jit(solution)/shard_map/reduce_scatter | solution.py:79
  2791.6 146.9 %all-reduce.11 = (bf16[1,2000]{1,0:T(2,128)(2,1)S(1)}, bf16[1,2800]{1,0:T(2,128)(2,1)S(1)}) all-reduce(bf16[1,2000]{1,0:T(2,128)(2,1)S(1)} %constant_dynamic-slice_fusion.3, bf16[1,2800]{1,0:T(2,128)(2,1)S(1)} %constant_dynamic-slice_fusion.2), channel_id=1, replica_groups=mesh['ctx'=32,'wt'=4] {'ctx'}, use_global_device_ids=true, to_apply=%region_25.26 | all-reduce | flops 4800 | bytes 19200 | tf_op jit(solution)/shard_map/psum | solution.py:89
  2955.9 505.0 %all-reduce.17.cloned.1.call-done = (bf16[400,4800]{1,0:T(8,128)(2,1)}, bf16[400,1600]{1,0:T(8,128)(2,1)}, bf16[400,6400]{1,0:T(8,128)(2,1)}, bf16[1600,1600]{1,0:T(8,128)(2,1)}) async-done(((bf16[400,4800]{1,0:T(8,128)(2,1)}, bf16[400,1600]{1,0:T(8,128)(2,1)}, bf16[400,6400]{1,0:T(8,128)(2,1)}, bf16[1600,1600]{1,0:T(8,128)(2,1)}), (bf16[400,4800]{1,0:T(8,128)(2,1)}, bf16[400,1600]{1,0:T(8,128)(2,1)}, ...) | async-done | bytes 15360016 | tf_op jit(solution)/shard_map/psum | solution.py:87
  (803 shorter events, 1140.8 us)
Async XLA Ops:
  7.3 109.2 %all-gather.7.cloned.1.call-start = ((), (), s32[]{:S(2)}) async-start(), calls=%async_computation.4 | async-start | bytes 19456000 | tf_op jit(solution)/shard_map/all_gather | solution.py:131
  8.0 398.5 %all-gather.9.cloned.1.call-start = ((), (), s32[]{:S(2)}) async-start(), calls=%async_computation.5 | async-start | bytes 13516800 | tf_op jit(solution)/shard_map/all_gather | solution.py:210
  127.9 567.1 %all-gather.11.cloned.1.call-start = ((), (), s32[]{:S(2)}) async-start(), calls=%async_computation.6 | async-start | bytes 13516800 | tf_op jit(solution)/shard_map/all_gather | solution.py:211
  129.3 706.9 %all-gather.13.cloned.1.call-start = ((), (), s32[]{:S(2)}) async-start(), calls=%async_computation.7 | async-start | bytes 6656000 | tf_op jit(solution)/shard_map/all_gather | solution.py:134
  129.8 752.8 %all-gather.15.cloned.1.call-start = ((), (), s32[]{:S(2)}) async-start(), calls=%async_computation.8 | async-start | bytes 25600000 | tf_op jit(solution)/shard_map/all_gather | solution.py:138
  130.5 890.7 %all-gather.17.cloned.1.call-start = ((), (), s32[]{:S(2)}) async-start(), calls=%async_computation.9 | async-start | bytes 26624000 | tf_op jit(solution)/shard_map/all_gather | solution.py:140
  131.0 2177.9 %reduce-scatter.7.cloned.1.call-start = ((), (), s32[]{:S(2)}) async-start(), calls=%async_computation.11 | async-start | bytes 6656000 | tf_op jit(solution)/shard_map/reduce_scatter | solution.py:79
  1054.9 1377.9 %reduce-scatter.5.cloned.1.call-start = ((), (), s32[]{:S(2)}) async-start(), calls=%async_computation.10 | async-start | bytes 19456000 | tf_op jit(solution)/shard_map/reduce_scatter | solution.py:76
  1061.3 46.1 %collective-permute-start.2 = (bf16[2,128,25,64]{1,3,2,0:T(8,128)(2,1)S(1)}, bf16[2,128,25,64]{1,3,2,0:T(8,128)(2,1)S(1)}, u32[]{:S(2)}, u32[]{:S(2)}) collective-permute-start(bf16[2,128,25,64]{1,3,2,0:T(8,128)(2,1)S(1)} %fusion.199), channel_id=1, source_target_pairs={{0,4},{4,8},{8,12},{12,16},{16,20},{20,24},{24,28},{28,32},{32,36}... | collective-permute-start | bytes 2457608 | tf_op jit(solution)/shard_map/while/body/eval_jaxpr/ppermute | solution.py:19
  1108.5 34.2 collective-permute-start.3
  1108.5 51.8 %collective-permute-start.1 = (bf16[2,128,1600]{1,2,0:T(8,128)(2,1)}, bf16[2,128,1600]{1,2,0:T(8,128)(2,1)}, u32[]{:S(2)}, u32[]{:S(2)}) collective-permute-start(bf16[2,128,1600]{1,2,0:T(8,128)(2,1)} %collective-permute-done), channel_id=1, source_target_pairs={{0,4},{4,8},{8,12},{12,16},{16,20},{20,24},{24,28},{28,32},{32,36}... | collective-permute-start | bytes 2457608 | tf_op jit(solution)/shard_map/while/body/eval_jaxpr/ppermute | solution.py:19
  1166.1 34.6 collective-permute-start.2
  1201.8 39.6 %collective-permute-start.1 = (bf16[2,128,1600]{1,2,0:T(8,128)(2,1)}, bf16[2,128,1600]{1,2,0:T(8,128)(2,1)}, u32[]{:S(2)}, u32[]{:S(2)}) collective-permute-start(bf16[2,128,1600]{1,2,0:T(8,128)(2,1)} %collective-permute-done), channel_id=1, source_target_pairs={{0,4},{4,8},{8,12},{12,16},{16,20},{20,24},{24,28},{28,32},{32,36}... | collective-permute-start | bytes 2457608 | tf_op jit(solution)/shard_map/while/body/eval_jaxpr/ppermute | solution.py:19
  1281.1 37.7 %collective-permute-start.1 = (bf16[2,128,1600]{1,2,0:T(8,128)(2,1)}, bf16[2,128,1600]{1,2,0:T(8,128)(2,1)}, u32[]{:S(2)}, u32[]{:S(2)}) collective-permute-start(bf16[2,128,1600]{1,2,0:T(8,128)(2,1)} %collective-permute-done), channel_id=1, source_target_pairs={{0,4},{4,8},{8,12},{12,16},{16,20},{20,24},{24,28},{28,32},{32,36}... | collective-permute-start | bytes 2457608 | tf_op jit(solution)/shard_map/while/body/eval_jaxpr/ppermute | solution.py:19
  1356.6 35.9 %collective-permute-start.1 = (bf16[2,128,1600]{1,2,0:T(8,128)(2,1)}, bf16[2,128,1600]{1,2,0:T(8,128)(2,1)}, u32[]{:S(2)}, u32[]{:S(2)}) collective-permute-start(bf16[2,128,1600]{1,2,0:T(8,128)(2,1)} %collective-permute-done), channel_id=1, source_target_pairs={{0,4},{4,8},{8,12},{12,16},{16,20},{20,24},{24,28},{28,32},{32,36}... | collective-permute-start | bytes 2457608 | tf_op jit(solution)/shard_map/while/body/eval_jaxpr/ppermute | solution.py:19
  1428.5 34.0 collective-permute-start.1
  1497.9 33.2 collective-permute-start.1
  1566.5 33.2 collective-permute-start.1
  1635.1 33.2 collective-permute-start.1
  1703.7 33.2 collective-permute-start.1
  1841.0 33.3 collective-permute-start.1
  1910.8 35.5 %collective-permute-start.1 = (bf16[2,128,1600]{1,2,0:T(8,128)(2,1)}, bf16[2,128,1600]{1,2,0:T(8,128)(2,1)}, u32[]{:S(2)}, u32[]{:S(2)}) collective-permute-start(bf16[2,128,1600]{1,2,0:T(8,128)(2,1)} %collective-permute-done), channel_id=1, source_target_pairs={{0,4},{4,8},{8,12},{12,16},{16,20},{20,24},{24,28},{28,32},{32,36}... | collective-permute-start | bytes 2457608 | tf_op jit(solution)/shard_map/while/body/eval_jaxpr/ppermute | solution.py:19
  1984.9 37.7 %collective-permute-start.1 = (bf16[2,128,1600]{1,2,0:T(8,128)(2,1)}, bf16[2,128,1600]{1,2,0:T(8,128)(2,1)}, u32[]{:S(2)}, u32[]{:S(2)}) collective-permute-start(bf16[2,128,1600]{1,2,0:T(8,128)(2,1)} %collective-permute-done), channel_id=1, source_target_pairs={{0,4},{4,8},{8,12},{12,16},{16,20},{20,24},{24,28},{28,32},{32,36}... | collective-permute-start | bytes 2457608 | tf_op jit(solution)/shard_map/while/body/eval_jaxpr/ppermute | solution.py:19
  2028.4 33.9 collective-permute-start.2
  2063.4 39.8 %collective-permute-start.1 = (bf16[2,128,1600]{1,2,0:T(8,128)(2,1)}, bf16[2,128,1600]{1,2,0:T(8,128)(2,1)}, u32[]{:S(2)}, u32[]{:S(2)}) collective-permute-start(bf16[2,128,1600]{1,2,0:T(8,128)(2,1)} %collective-permute-done), channel_id=1, source_target_pairs={{0,4},{4,8},{8,12},{12,16},{16,20},{20,24},{24,28},{28,32},{32,36}... | collective-permute-start | bytes 2457608 | tf_op jit(solution)/shard_map/while/body/eval_jaxpr/ppermute | solution.py:19
  2109.0 36.3 %collective-permute-start.2 = (bf16[2,128,25,64]{1,3,2,0:T(8,128)(2,1)S(1)}, bf16[2,128,25,64]{1,3,2,0:T(8,128)(2,1)S(1)}, u32[]{:S(2)}, u32[]{:S(2)}) collective-permute-start(bf16[2,128,25,64]{1,3,2,0:T(8,128)(2,1)S(1)} %fusion.199), channel_id=1, source_target_pairs={{0,4},{4,8},{8,12},{12,16},{16,20},{20,24},{24,28},{28,32},{32,36}... | collective-permute-start | bytes 2457608 | tf_op jit(solution)/shard_map/while/body/eval_jaxpr/ppermute | solution.py:19
  2146.5 41.8 %collective-permute-start.1 = (bf16[2,128,1600]{1,2,0:T(8,128)(2,1)}, bf16[2,128,1600]{1,2,0:T(8,128)(2,1)}, u32[]{:S(2)}, u32[]{:S(2)}) collective-permute-start(bf16[2,128,1600]{1,2,0:T(8,128)(2,1)} %collective-permute-done), channel_id=1, source_target_pairs={{0,4},{4,8},{8,12},{12,16},{16,20},{20,24},{24,28},{28,32},{32,36}... | collective-permute-start | bytes 2457608 | tf_op jit(solution)/shard_map/while/body/eval_jaxpr/ppermute | solution.py:19
  2194.0 34.6 collective-permute-start.2
  2229.8 40.5 %collective-permute-start.1 = (bf16[2,128,1600]{1,2,0:T(8,128)(2,1)}, bf16[2,128,1600]{1,2,0:T(8,128)(2,1)}, u32[]{:S(2)}, u32[]{:S(2)}) collective-permute-start(bf16[2,128,1600]{1,2,0:T(8,128)(2,1)} %collective-permute-done), channel_id=1, source_target_pairs={{0,4},{4,8},{8,12},{12,16},{16,20},{20,24},{24,28},{28,32},{32,36}... | collective-permute-start | bytes 2457608 | tf_op jit(solution)/shard_map/while/body/eval_jaxpr/ppermute | solution.py:19
  2284.2 315.1 %reduce-scatter.9.cloned.1.call-start = ((), (), s32[]{:S(2)}) async-start(), calls=%async_computation.12 | async-start | bytes 25600000 | tf_op jit(solution)/shard_map/reduce_scatter | solution.py:76
  2296.2 467.3 %reduce-scatter.11.cloned.1.call-start = ((), (), s32[]{:S(2)}) async-start(), calls=%async_computation.13 | async-start | bytes 26624000 | tf_op jit(solution)/shard_map/reduce_scatter | solution.py:79
  2308.8 1152.1 %all-reduce.17.cloned.1.call-start = ((), (), s32[]{:S(2)}) async-start(), calls=%async_computation.14 | async-start | bytes 31334400 | tf_op jit(solution)/shard_map/psum | solution.py:87
  (126 other events, 7395.2 us)
Sparse Core Ops, SparseCore 0:
  9.8 106.6 all-gather.6
  128.1 278.4 all-gather.8
  408.7 286.2 all-gather.10
  696.5 52.1 all-gather.12
  750.3 132.3 all-gather.14
  884.2 136.8 all-gather.16
  1055.0 80.6 reduce-scatter.6
  2284.3 148.4 reduce-scatter.4
  2435.8 163.4 reduce-scatter.8
  2601.8 161.5 reduce-scatter.10
  2766.5 694.3 all-reduce.16
where the time goes:
time: 3490 us
  waiting for transfers between devices  2750 us (79%)
  matrix products  330 us (9%)
  blocking collectives  176 us (5%)
  other arithmetic  114 us (3%)
  local copies, waits for them, and re-layouts  92.1 us (3%)
    ppermute x64, waiting for transfers between devices, passed_along(): return lax.ppermute(value, axis, pairs)  969 us
    psum x1, waiting for transfers between devices, reduce_grads(): lax.psum(owned_part[0].astype(jnp.bfloat16), 'ctx').astype(jnp.float32)  505 us
    reduce_scatter x2, waiting for transfers between devices, reduce_grads(): lax.psum_scatter(first_matrix.astype(jnp.bfloat16), 'wt', scatter_dimensi...  290 us
    all_gather x1, waiting for transfers between devices, local(): lax.all_gather(value_rows, 'ctx', axis=0, tiled=True)  288 us
    all_gather x1, waiting for transfers between devices, local(): lax.all_gather(key_rows, 'ctx', axis=0, tiled=True)  273 us
    reduce_scatter x2, waiting for transfers between devices, reduce_grads(): lax.psum_scatter(second_matrix.astype(jnp.bfloat16), 'wt', scatter_dimens...  164 us
    psum x1, blocking collectives, reduce_grads(): lax.psum(owned_part[2].astype(jnp.bfloat16), 'ctx').astype(jnp.float32)  147 us
    all_gather x1, waiting for transfers between devices, local(): lax.all_gather(w_proj, 'wt', axis=0, tiled=True)  126 us
  transfers between devices with their start and end apart: 75, of which 73 were waited for; matrix products, arithmetic and copies ran while one was open for 13% of the time, Pallas kernels for 0%

commit v1 on v0

v1 whole, which is shorter than its diff:
```python
import math

import jax
import jax.numpy as jnp
from jax import lax
from jax.experimental import pallas as pl
from jax.experimental.pallas import tpu as pltpu
from jax.sharding import PartitionSpec as P

HEADS = 25
HEAD_DIM = 64
GROUP = 7
SPAN = GROUP * HEAD_DIM
EPS = 1e-05
MESH = pl.DeviceIdType.MESH
NEG = -1e30
LOG2E = 1.4426950408889634

def attend_forward(received, inverse, place, block):
    parts, wide, rows = received.shape
    dim = wide // 3
    per = block // rows
    count = parts // per

    def kernel(inverse_ref, place_ref, in_ref, out_ref, q_ref, kt_ref, vt_ref, k_ref, v_ref, att_ref, lse_ref):
        def arrange(index, carry):
            for sub in range(per):
                piece = in_ref[inverse_ref[index * per + sub]]
                lanes = pl.ds(sub * rows, rows)
                q_ref[index, :, lanes] = piece[:dim]
                kt_ref[index, :, lanes] = piece[dim : 2 * dim]
                vt_ref[index, :, lanes] = piece[2 * dim :]
                k_ref[index, lanes, :] = piece[dim : 2 * dim].T
                v_ref[index, lanes, :] = piece[2 * dim :].T
            return carry

        lax.fori_loop(0, count, arrange, 0)
        row = lax.broadcasted_iota(jnp.int32, (block, block), 0)
        col = lax.broadcasted_iota(jnp.int32, (block, block), 1)
        factor = LOG2E * dim**-0.5

        def step(qi, kj, carry, diagonal):
            peak, mass, total = carry
            scores = jnp.dot(k_ref[kj], q_ref[qi], preferred_element_type=jnp.float32) * factor
            if diagonal:
                scores = jnp.where(row <= col, scores, NEG)
            new_peak = jnp.maximum(peak, jnp.max(scores, axis=0, keepdims=True))
            weights = jnp.exp2(scores - new_peak)
            shrink = jnp.exp2(peak - new_peak)
            mass = mass * shrink + jnp.sum(weights, axis=0, keepdims=True)
            total = total * shrink + jnp.dot(
                vt_ref[kj], weights.astype(jnp.bfloat16), preferred_element_type=jnp.float32
            )
            return (new_peak, mass, total)

        def query_block(qi, carry):
            start = (
                jnp.full((1, block), NEG, jnp.float32),
                jnp.zeros((1, block), jnp.float32),
                jnp.zeros((dim, block), jnp.float32),
            )
            state = lax.fori_loop(0, qi, lambda kj, cur: step(qi, kj, cur, False), start)
            peak, mass, total = step(qi, qi, state, True)
            att_ref[qi] = total / mass
            lse_ref[qi] = peak + jnp.log2(mass)
            return carry

        lax.fori_loop(0, count, query_block, 0)

        def give_back(index, carry):
            where = place_ref[index]
            whole = att_ref[where // per]
            picked = whole[:, :rows]
            for sub in range(1, per):
                picked = jnp.where(where % per == sub, whole[:, sub * rows : (sub + 1) * rows], picked)
            out_ref[index] = picked.astype(jnp.bfloat16)
            return carry

        lax.fori_loop(0, parts, give_back, 0)

    smem = pl.BlockSpec(memory_space=pltpu.SMEM)
    vmem = pl.BlockSpec(memory_space=pltpu.VMEM)
    lane_first = jax.ShapeDtypeStruct((count, dim, block), jnp.bfloat16)
    row_first = jax.ShapeDtypeStruct((count, block, dim), jnp.bfloat16)
    return pl.pallas_call(
        kernel,
        out_shape=(
            jax.ShapeDtypeStruct((parts, dim, rows), jnp.bfloat16),
            lane_first, lane_first, lane_first, row_first, row_first,
            jax.ShapeDtypeStruct((count, dim, block), jnp.float32),
            jax.ShapeDtypeStruct((count, 1, block), jnp.float32),
        ),
        in_specs=[smem, smem, vmem],
        out_specs=(vmem,) * 8,
        compiler_params=pltpu.CompilerParams(vmem_limit_bytes=40 * 2**20),
        name="attend_forward",
    )(inverse, place, received)


def attend_backward(upstream, inverse, place, saved, block):
    parts, dim, rows = upstream.shape
    per = block // rows
    count = parts // per
    q, kt, vt, k, v, attended, lse = saved

    def kernel(inverse_ref, place_ref, up_ref, q_ref, kt_ref, k_ref, v_ref, att_ref, lse_ref, out_ref, up_sorted, up_rows, q_rows, delta_ref, gq_ref, gk_ref, gv_ref):
        def arrange(index, carry):
            for sub in range(per):
                piece = up_ref[inverse_ref[index * per + sub]]
                lanes = pl.ds(sub * rows, rows)
                up_sorted[index, :, lanes] = piece
                up_rows[index, lanes, :] = piece.T
            q_rows[index] = q_ref[index].T
            delta_ref[index] = jnp.sum(up_sorted[index].astype(jnp.float32) * att_ref[index], axis=0, keepdims=True)
            gk_ref[index] = jnp.zeros((block, dim), jnp.float32)
            gv_ref[index] = jnp.zeros((block, dim), jnp.float32)
            return carry

        lax.fori_loop(0, count, arrange, 0)
        row = lax.broadcasted_iota(jnp.int32, (block, block), 0)
        col = lax.broadcasted_iota(jnp.int32, (block, block), 1)
        factor = LOG2E * dim**-0.5

        def step(qi, kj, total, diagonal):
            scores = jnp.dot(k_ref[kj], q_ref[qi], preferred_element_type=jnp.float32) * factor
            weights = jnp.exp2(scores - lse_ref[qi])
            if diagonal:
                weights = jnp.where(row <= col, weights, 0.0)
            prob_grad = jnp.dot(v_ref[kj], up_sorted[qi], preferred_element_type=jnp.float32)
            score_grad = (weights * (prob_grad - delta_ref[qi])).astype(jnp.bfloat16)
            gv_ref[kj] += jnp.dot(weights.astype(jnp.bfloat16), up_rows[qi], preferred_element_type=jnp.float32)
            gk_ref[kj] += jnp.dot(score_grad, q_rows[qi], preferred_element_type=jnp.float32)
            return total + jnp.dot(kt_ref[kj], score_grad, preferred_element_type=jnp.float32)

        def query_block(qi, carry):
            total = lax.fori_loop(
                0, qi, lambda kj, cur: step(qi, kj, cur, False), jnp.zeros((dim, block), jnp.float32)
            )
            gq_ref[qi] = step(qi, qi, total, True) * dim**-0.5
            return carry

        lax.fori_loop(0, count, query_block, 0)

        def give_back(index, carry):
            where = place_ref[index]
            hold = where // per
            off = where % per
            whole = gq_ref[hold]
            picked = whole[:, :rows]
            for sub in range(1, per):
                picked = jnp.where(off == sub, whole[:, sub * rows : (sub + 1) * rows], picked)
            out_ref[index, :dim] = picked.astype(jnp.bfloat16)
            line = pl.ds(pl.multiple_of(off * rows, rows), rows)
            out_ref[index, dim : 2 * dim] = (gk_ref[hold, line, :] * dim**-0.5).T.astype(jnp.bfloat16)
            out_ref[index, 2 * dim :] = gv_ref[hold, line, :].T.astype(jnp.bfloat16)
            return carry

        lax.fori_loop(0, parts, give_back, 0)

    smem = pl.BlockSpec(memory_space=pltpu.SMEM)
    vmem = pl.BlockSpec(memory_space=pltpu.VMEM)
    return pl.pallas_call(
        kernel,
        out_shape=jax.ShapeDtypeStruct((parts, 3 * dim, rows), jnp.bfloat16),
        in_specs=[smem, smem] + [vmem] * 7,
        out_specs=vmem,
        scratch_shapes=[
            pltpu.VMEM((count, dim, block), jnp.bfloat16),
            pltpu.VMEM((count, block, dim), jnp.bfloat16),
            pltpu.VMEM((count, block, dim), jnp.bfloat16),
            pltpu.VMEM((count, 1, block), jnp.float32),
            pltpu.VMEM((count, dim, block), jnp.float32),
            pltpu.VMEM((count, block, dim), jnp.float32),
            pltpu.VMEM((count, block, dim), jnp.float32),
        ],
        compiler_params=pltpu.CompilerParams(vmem_limit_bytes=40 * 2**20),
        name="attend_backward",
    )(inverse, place, upstream, q, kt, k, v, attended, lse)


def layer_norm(values, gain_row, shift_row):
    centered = values - jnp.mean(values, axis=-1, keepdims=True)
    variance = jnp.mean(centered * centered, axis=-1, keepdims=True)
    return centered * lax.rsqrt(variance + EPS) * gain_row + shift_row


def gelu_tanh(values):
    return jax.nn.gelu(values, approximate=True)


def dot(left, right, left_dim=1, right_dim=0):
    return lax.dot_general(
        left, right, (((left_dim,), (right_dim,)), ((), ())), preferred_element_type=jnp.float32
    )


def greet(peers):
    barrier = pltpu.get_barrier_semaphore()
    for peer in peers:
        pl.semaphore_signal(barrier, inc=1, device_id=peer, device_id_type=MESH)
    pl.semaphore_wait(barrier, len(peers))


def gather_wt(arrays, collective):
    count = len(arrays)

    def kernel(*refs):
        sources, targets = refs[:count], refs[count : 2 * count]
        send, receive, local = refs[2 * count :]
        ctx, wt = lax.axis_index("ctx"), lax.axis_index("wt")
        near, far = (ctx, wt ^ 1), (ctx, wt ^ 2)
        greet((near, far))

        def move(item, step, source, slot, peer):
            return pltpu.make_async_remote_copy(
                source, targets[item].at[slot], send.at[item, step], receive.at[item, step],
                device_id=peer, device_id_type=MESH,
            )

        firsts = [move(item, 0, sources[item], wt, far) for item in range(count)]
        for copy in firsts:
            copy.start()
        seconds = [move(item, 1, sources[item], wt, near) for item in range(count)]
        own = [
            pltpu.make_async_copy(sources[item], targets[item].at[wt], local.at[item])
            for item in range(count)
        ]
        for copy in seconds + own:
            copy.start()
        thirds = []
        for item in range(count):
            firsts[item].wait_recv()
            copy = move(item, 2, targets[item].at[wt ^ 2], wt ^ 2, near)
            copy.start()
            thirds.append(copy)
        for copy in firsts:
            copy.wait_send()
        for copy in seconds + thirds + own:
            copy.wait()

    hbm = pl.BlockSpec(memory_space=pl.ANY)
    return pl.pallas_call(
        kernel,
        out_shape=tuple(jax.ShapeDtypeStruct((4,) + member.shape, member.dtype) for member in arrays),
        in_specs=[hbm] * count,
        out_specs=(hbm,) * count,
        scratch_shapes=[
            pltpu.SemaphoreType.DMA((count, 3)),
            pltpu.SemaphoreType.DMA((count, 3)),
            pltpu.SemaphoreType.DMA((count,)),
        ],
        compiler_params=pltpu.CompilerParams(collective_id=collective, has_side_effects=True),
        name="gather_wt",
    )(*arrays)


def scatter_wt(parts, collective):
    count = len(parts)
    extents = [member.shape[1:] for member in parts]

    def kernel(*refs):
        terms, sums = refs[:count], refs[count : 2 * count]
        bufs = refs[2 * count : 3 * count]
        send, receive = refs[3 * count :]
        ctx, wt = lax.axis_index("ctx"), lax.axis_index("wt")
        near, far = (ctx, wt ^ 1), (ctx, wt ^ 2)
        greet((near, far))

        def move(item, step, source, target, peer):
            return pltpu.make_async_remote_copy(
                bufs[item].at[source], bufs[item].at[target], send.at[item, step], receive.at[item, step],
                device_id=peer, device_id_type=MESH,
            )

        waits = []
        for item in range(count):
            bufs[item][0] = terms[item][wt ^ 3].astype(jnp.bfloat16)
            copy = move(item, 0, 0, 3, near)
            copy.start()
            waits.append(copy)
        rests = []
        for item in range(count):
            bufs[item][1] = terms[item][wt ^ 1].astype(jnp.bfloat16)
            copy = move(item, 1, 1, 4, near)
            copy.start()
            rests.append(copy)
        lasts = []
        for item in range(count):
            waits[item].wait_recv()
            bufs[item][2] = (terms[item][wt ^ 2] + bufs[item][3].astype(jnp.float32)).astype(jnp.bfloat16)
            copy = move(item, 2, 2, 5, far)
            copy.start()
            lasts.append(copy)
        for item in range(count):
            rests[item].wait_recv()
            sums[item][...] = terms[item][wt] + bufs[item][4].astype(jnp.float32)
        for item in range(count):
            lasts[item].wait_recv()
            sums[item][...] += bufs[item][5].astype(jnp.float32)
        for copy in waits + rests + lasts:
            copy.wait_send()

    vmem = pl.BlockSpec(memory_space=pltpu.VMEM)
    return pl.pallas_call(
        kernel,
        out_shape=tuple(jax.ShapeDtypeStruct(extent, jnp.float32) for extent in extents),
        in_specs=[vmem] * count,
        out_specs=(vmem,) * count,
        scratch_shapes=[pltpu.VMEM((6,) + extent, jnp.bfloat16) for extent in extents]
        + [pltpu.SemaphoreType.DMA((count, 3)), pltpu.SemaphoreType.DMA((count, 3))],
        compiler_params=pltpu.CompilerParams(
            collective_id=collective, has_side_effects=True, vmem_limit_bytes=40 * 2**20
        ),
        name="scatter_wt",
    )(*parts)


def exchange(blocks, axis, collective):
    count = blocks.shape[0]

    def kernel(source, target, send, receive, local):
        ctx, wt = lax.axis_index("ctx"), lax.axis_index("wt")
        own = ctx if axis == "ctx" else wt

        def peer(step):
            other = lax.rem(own + step, count)
            return other, ((other, wt) if axis == "ctx" else (ctx, other))

        barrier = pltpu.get_barrier_semaphore()

        def signal(step, carry):
            pl.semaphore_signal(barrier, inc=1, device_id=peer(step)[1], device_id_type=MESH)
            return carry

        lax.fori_loop(1, count, signal, 0)
        pl.semaphore_wait(barrier, count - 1)

        def move(step):
            other, device = peer(step)
            return pltpu.make_async_remote_copy(
                source.at[other], target.at[own], send.at[step], receive.at[step],
                device_id=device, device_id_type=MESH,
            )

        def begin(step, carry):
            move(step).start()
            return carry

        def finish(step, carry):
            move(step).wait()
            return carry

        lax.fori_loop(1, count, begin, 0)
        keep = pltpu.make_async_copy(source.at[own], target.at[own], local)
        keep.start()
        keep.wait()
        lax.fori_loop(1, count, finish, 0)

    hbm = pl.BlockSpec(memory_space=pl.ANY)
    return pl.pallas_call(
        kernel,
        out_shape=jax.ShapeDtypeStruct(blocks.shape, blocks.dtype),
        in_specs=[hbm],
        out_specs=hbm,
        scratch_shapes=[
            pltpu.SemaphoreType.DMA((count,)),
            pltpu.SemaphoreType.DMA((count,)),
            pltpu.SemaphoreType.DMA,
        ],
        compiler_params=pltpu.CompilerParams(collective_id=collective, has_side_effects=True),
        name="exchange_" + axis,
    )(blocks)


def swap_wt(blocks):
    wt = lax.axis_index("wt")
    kept = lax.dynamic_index_in_dim(blocks, wt, 0, keepdims=False)
    result = jnp.zeros_like(blocks)
    result = lax.dynamic_update_index_in_dim(result, kept, wt, 0)
    for step in (1, 2, 3):
        piece = lax.dynamic_index_in_dim(blocks, wt ^ step, 0, keepdims=False)
        piece = lax.ppermute(piece, "wt", [(source, source ^ step) for source in range(4)])
        result = lax.dynamic_update_index_in_dim(result, piece, wt ^ step, 0)
    return result


def to_heads(rows_by_token):
    parts = rows_by_token.shape[0] // SPAN
    rows = rows_by_token.shape[1] // 4
    blocks = rows_by_token.reshape(parts, GROUP, HEAD_DIM, 4, rows).transpose(3, 1, 0, 2, 4)
    blocks = blocks.reshape(4 * GROUP, parts * HEAD_DIM, rows)
    spare = lax.axis_size("ctx") - 4 * GROUP
    return jnp.concatenate([blocks, jnp.zeros((spare,) + blocks.shape[1:], blocks.dtype)])


def from_heads(blocks):
    parts, rows = blocks.shape[1] // HEAD_DIM, blocks.shape[2]
    used = blocks[: 4 * GROUP].reshape(4, GROUP, parts, HEAD_DIM, rows)
    return used.transpose(2, 1, 3, 0, 4).reshape(parts * SPAN, 4 * rows)


def local(
    inputs,
    block_order,
    cotangent,
    ln1_gain,
    ln1_bias,
    w_qkv,
    bias_q,
    bias_v,
    w_out,
    bias_out,
    ln2_gain,
    ln2_bias,
    w_fc,
    bias_fc,
    w_proj,
    bias_proj,
):
    ctx, wt = lax.axis_index("ctx"), lax.axis_index("wt")
    ctx_count = lax.axis_size("ctx")
    rows, features = inputs.shape[1:]
    share = features // 4
    shift = 16 * wt

    small = jnp.stack([ln1_gain, ln1_bias, bias_q, bias_v, bias_out, ln2_gain, ln2_bias, bias_proj])
    small = jnp.pad(small, ((0, 8), (0, 0)))
    order = jnp.pad(block_order, ((0, 7), (0, 128 - ctx_count)))
    all_inputs, all_small, all_order, all_cot = gather_wt((inputs[0], small, order, cotangent[0]), 1)
    vectors = all_small[:, :8].transpose(1, 0, 2).reshape(8, features).astype(jnp.float32)
    gain_one, shift_one, full_bq, full_bv, full_bout, gain_two, shift_two, full_bproj = vectors
    orders = all_order[:, 0, :ctx_count]
    place = lax.dynamic_index_in_dim(orders, jnp.minimum(ctx // GROUP, 3), 0, keepdims=False)
    slots = jnp.arange(ctx_count, dtype=jnp.int32)
    inverse = jnp.sum(jnp.where(place[None, :] == slots[:, None], slots[None, :], 0), axis=1)

    starts = [384 * member for member in range(4)]
    columns = jnp.stack(
        [
            jnp.concatenate(
                [w_qkv[:, part * features + start : part * features + start + SPAN] for part in range(3)],
                axis=1,
            )
            for start in starts
        ]
    )
    own_qkv = exchange(columns, "wt", 2).reshape(features, 3 * SPAN)
    own_fc = swap_wt(w_fc.reshape(share, 4, -1).transpose(1, 0, 2)).reshape(features, -1)
    edge = SPAN - share
    below = lax.ppermute(w_out[share - edge :], "wt", [(source, (source + 1) % 4) for source in range(4)])
    above = lax.ppermute(w_out[:edge], "wt", [(source, (source - 1) % 4) for source in range(4)])
    wide_out = lax.dynamic_slice_in_dim(jnp.concatenate([below, w_out, above]), edge - shift, SPAN, 0)
    span_ids = jnp.arange(SPAN, dtype=jnp.int32)
    mine = (span_ids >= shift) & (span_ids < shift + share)
    masked_out = jnp.where(mine[:, None], wide_out, 0)

    group_tokens = all_inputs.reshape(4 * rows, features).astype(jnp.float32)
    normed_one = layer_norm(group_tokens, gain_one, shift_one).astype(jnp.bfloat16)
    bias_cols = jnp.concatenate(
        [
            lax.dynamic_slice_in_dim(full_bq, 384 * wt, SPAN),
            jnp.zeros((SPAN,), jnp.float32),
            lax.dynamic_slice_in_dim(full_bv, 384 * wt, SPAN),
        ]
    )
    projected = (dot(own_qkv, normed_one, 0, 1) + bias_cols[:, None]).astype(jnp.bfloat16)
    received = exchange(to_heads(projected), "ctx", 3)
    block = math.gcd(512, ctx_count * rows)
    attended_blocks, *saved = attend_forward(received, inverse, place, block)
    attended = from_heads(exchange(attended_blocks, "ctx", 4))

    tokens = inputs[0].astype(jnp.float32)
    (branch,) = scatter_wt((dot(attended, masked_out, 0, 0).reshape(4, rows, features),), 5)
    middle = tokens + branch + full_bout
    normed_two = layer_norm(middle, gain_two, shift_two).astype(jnp.bfloat16)
    (all_two,) = gather_wt((normed_two,), 6)
    all_two = all_two.reshape(4 * rows, features)
    hidden_pre = dot(all_two, own_fc) + bias_fc.astype(jnp.float32)
    hidden_low = gelu_tanh(hidden_pre).astype(jnp.bfloat16)
    group_cot = all_cot.reshape(4 * rows, features)
    hidden_grad = dot(group_cot, w_proj, 1, 1)
    unused_gelu, gelu_back = jax.vjp(gelu_tanh, hidden_pre)
    pre_grad = gelu_back(hidden_grad)[0].astype(jnp.bfloat16)
    projected_out, normed_two_grad = scatter_wt(
        (
            dot(hidden_low, w_proj).reshape(4, rows, features),
            dot(pre_grad, own_fc, 1, 1).reshape(4, rows, features),
        ),
        7,
    )
    outputs = middle + projected_out + full_bproj
    unused_norm, norm_back = jax.vjp(layer_norm, middle, gain_two, shift_two)
    middle_part, grad_gain_two, grad_shift_two = norm_back(normed_two_grad)
    middle_grad = cotangent[0].astype(jnp.float32) + middle_part
    branch_grad = middle_grad.astype(jnp.bfloat16)
    (all_branch,) = gather_wt((branch_grad,), 8)
    all_branch = all_branch.reshape(4 * rows, features)

    attended_grad = dot(wide_out, all_branch, 1, 1).astype(jnp.bfloat16)
    upstream = exchange(to_heads(attended_grad), "ctx", 9)
    grad_blocks = attend_backward(upstream, inverse, place, saved, block)
    stacked = from_heads(exchange(grad_blocks, "ctx", 10))
    masked = jnp.where(jnp.tile(mine, 3)[:, None], stacked, 0)
    (normed_one_grad,) = scatter_wt((dot(masked, own_qkv, 0, 1).reshape(4, rows, features),), 11)
    unused_first, first_back = jax.vjp(layer_norm, tokens, gain_one, shift_one)
    input_part, grad_gain_one, grad_shift_one = first_back(normed_one_grad)
    input_grad = middle_grad + input_part

    low = jnp.bfloat16
    own_stacked = lax.dynamic_slice_in_dim(stacked.reshape(3, SPAN, -1), shift, share, 1)
    own_attended = lax.dynamic_slice_in_dim(attended, shift, share, 0)
    grad_proj = dot(hidden_low, group_cot, 0, 0).astype(low)
    grad_fc = dot(pre_grad, all_two, 0, 0).astype(low)
    grad_qkv = dot(own_stacked.reshape(3 * share, -1), normed_one).astype(low)
    grad_out = dot(own_attended, all_branch).astype(low)
    column = lambda value: lax.dynamic_slice_in_dim(value, share * wt, share, 0)
    sums = jnp.sum(own_stacked.astype(jnp.float32), axis=2)
    grad_bout = column(jnp.sum(all_branch.astype(jnp.float32), axis=0))
    grad_bproj = column(jnp.sum(group_cot.astype(jnp.float32), axis=0))
    grad_bfc = jnp.sum(pre_grad.astype(jnp.float32), axis=0)
    crossed_vectors = jnp.stack([grad_gain_one, grad_shift_one, grad_gain_two, grad_shift_two]).astype(low)
    kept_vectors = jnp.stack([jnp.concatenate([sums[0], sums[2], grad_bout, grad_bproj]), grad_bfc]).astype(low)
    pad = lambda value, extent: jnp.pad(value, ((0, extent - value.shape[0]), (0, 0)))
    crossed = pad(jnp.concatenate([grad_fc, grad_qkv, crossed_vectors]), 96 * ctx_count)
    kept = pad(jnp.concatenate([grad_proj, grad_out, kept_vectors]), 64 * ctx_count)
    crossed_chunk = lax.psum_scatter(crossed, "ctx", scatter_dimension=0, tiled=True)
    kept_chunk = lax.psum_scatter(kept, "ctx", scatter_dimension=0, tiled=True)
    crossed_chunk = exchange(crossed_chunk.reshape(96, 4, share).transpose(1, 0, 2), "wt", 12)
    crossed_all = lax.all_gather(crossed_chunk, "ctx", axis=1, tiled=True).astype(jnp.float32)
    kept_all = lax.all_gather(kept_chunk, "ctx", axis=0, tiled=True).astype(jnp.float32)
    ff = grad_fc.shape[0]
    sum_fc = crossed_all[:, :ff].transpose(2, 0, 1).reshape(share, 4 * ff)
    sum_qkv = crossed_all[:, ff : ff + 3 * share].reshape(4, 3, share, share)
    sum_qkv = sum_qkv.transpose(3, 1, 0, 2).reshape(share, 3 * features)
    norms = jnp.sum(crossed_all[:, ff + 3 * share : ff + 3 * share + 4], axis=0)
    sum_proj, sum_out = kept_all[:ff], kept_all[ff : ff + share]
    kept_sums = kept_all[ff + share : ff + share + 2]
    sum_bq, sum_bv, sum_bout, sum_bproj = kept_sums[0].reshape(4, share)
    return (
        outputs.astype(jnp.bfloat16)[None],
        input_grad[None],
        norms[0],
        norms[1],
        sum_qkv,
        sum_bq,
        sum_bv,
        sum_out,
        sum_bout,
        norms[2],
        norms[3],
        sum_fc,
        kept_sums[1],
        sum_proj,
        sum_bproj,
    )


def solution(mesh):
    placed = (
        P("wt", "ctx", None),
        P("wt", None),
        P("wt", "ctx", None),
        P("wt"),
        P("wt"),
        P("wt", None),
        P("wt"),
        P("wt"),
        P("wt", None),
        P("wt"),
        P("wt"),
        P("wt"),
        P("wt", None),
        P("wt"),
        P("wt", None),
        P("wt"),
    )
    return jax.shard_map(
        local,
        mesh=mesh,
        in_specs=placed,
        out_specs=(
            P("wt", "ctx", None),
            P("wt", "ctx", None),
            P("wt"),
            P("wt"),
            P("wt", None),
            P("wt"),
            P("wt"),
            P("wt", None),
            P("wt"),
            P("wt"),
            P("wt"),
            P("wt", None),
            P("wt"),
            P("wt", None),
            P("wt"),
        ),
        check_vma=False,
    )
```

time: 3490 us -> 1490 us (0.43)
  waiting for transfers between devices: 2750 us -> 748 us
  Pallas kernels: 0 us -> 371 us
  matrix products: 330 us -> 58.8 us
  blocking collectives: 176 us -> 0 us
  local copies, waits for them, and re-layouts: 92.1 us -> 240 us
  other arithmetic: 114 us -> 43.8 us
    ppermute x64 -> x5, waiting for transfers between devices: 969 us -> 0.01 us  [the longest x3 0.01 us: swap_wt(): lax.ppermute(piece, 'wt', [(source, source ^ step) for source in range(4)])]
    psum x1 -> x0, waiting for transfers between devices: 505 us -> none  [reduce_grads(): lax.psum(owned_part[0].astype(jnp.bfloat16), 'ctx').astype(jnp.float32)]
    all_gather x6 -> x2, waiting for transfers between devices: 819 us -> 418 us  [the longest x1 274 us: local(): lax.all_gather(crossed_chunk, 'ctx', axis=1, tiled=True).astype(jnp.float32)]
    reduce_scatter x4 -> x1, waiting for transfers between devices: 455 us -> 82.6 us  [local(): kept_chunk = lax.psum_scatter(kept, 'ctx', scatter_dimension=0, tiled=True)]
    pallas_call x0 -> x14, Pallas kernels: none -> 371 us  [the longest x6 144 us: exchange(): pl.pallas_call(kernel, out_shape=jax.ShapeDtypeStruct(blocks.shape, block...]
    dot_general x188 -> x12, matrix products: 330 us -> 58.8 us  [dot(): lax.dot_general(left, right, (((left_dim,), (right_dim,)), ((), ())), pre...]
    unnamed x11 -> x5, waiting for transfers between devices: 2.36 us -> 247 us
    psum x1 -> x0, blocking collectives: 147 us -> none  [reduce_grads(): lax.psum(owned_part[2].astype(jnp.bfloat16), 'ctx').astype(jnp.float32)]
  transfers between devices with their start and end apart: 75 -> 9, of which waited for: 73 -> 4; matrix products, arithmetic and copies ran while one was open for 13% -> 12% of each run, Pallas kernels for 0% -> 18%
where the time goes in v1:
time: 1490 us; the launch traced here: 1480 us
  waiting for transfers between devices  748 us (50%)
  Pallas kernels  371 us (25%)
  local copies, waits for them, and re-layouts  240 us (16%)
  matrix products  58.8 us (4%)
  other arithmetic  43.8 us (3%)
    all_gather x1, waiting for transfers between devices, local(): lax.all_gather(crossed_chunk, 'ctx', axis=1, tiled=True).astype(jnp.float32)  274 us
    unnamed x5, waiting for transfers between devices  247 us
    all_gather x1, waiting for transfers between devices, local(): lax.all_gather(kept_chunk, 'ctx', axis=0, tiled=True).astype(jnp.float32)  144 us
    pallas_call x6, Pallas kernels, exchange(): pl.pallas_call(kernel, out_shape=jax.ShapeDtypeStruct(blocks.shape, block...  144 us
    pallas_call x3, Pallas kernels, gather_wt(): pl.pallas_call(kernel, out_shape=tuple((jax.ShapeDtypeStruct((4,) + membe...  106 us
    reduce_scatter x1, waiting for transfers between devices, local(): kept_chunk = lax.psum_scatter(kept, 'ctx', scatter_dimension=0, tiled=True)  82.6 us
    pallas_call x3, Pallas kernels, scatter_wt(): pl.pallas_call(kernel, out_shape=tuple((jax.ShapeDtypeStruct(extent, jnp....  64.4 us
    unnamed x134, local copies, waits for them, and re-layouts  59.5 us
  transfers between devices with their start and end apart: 9, of which 4 were waited for; matrix products, arithmetic and copies ran while one was open for 12% of the time, Pallas kernels for 18%

profile of v1, /device:TPU:1, one launch (start us, length us, event | category | flops | bytes accessed | tf_op | source)
XLA Modules:
  0.0 1483.8 jit_solution(11108500152966305693)
XLA Ops:
  13.1 11.7 reshape.289
  24.8 17.8 %constant_dynamic-slice_fusion.1 = (bf16[400,1,1600]{2,1,0:T(2,128)(2,1)S(1)}, bf16[400,1,1600]{2,1,0:T(2,128)(2,1)S(1)}, bf16[400,1,1600]{2,1,0:T(2,128)(2,1)S(1)}, bf16[400,1,1600]{2,1,0:T(2,128)(2,1)}) fusion(bf16[400,4,1600]{2,1,0:T(4,128)(2,1)} %reshape.289, s32[]{:T(128)S(6)} %select_n.63, s32[]{:T(128)S(6)} %select_n.62, s32[]{:T(128)S(6)} %select_n.61, ...), kind=kLoop, calls=%fused_computation.93 | loop fusion | bytes 10240016 | tf_op jit(solution)/shard_map/dynamic-slice.6
  53.6 74.8 %gather_wt.3 = (bf16[4,128,1600]{2,1,0:T(8,128)(2,1)}, bf16[4,16,400]{2,1,0:T(8,128)(2,1)}, s32[4,8,128]{2,1,0:T(8,128)}, bf16[4,128,1600]{2,1,0:T(8,128)(2,1)}) custom-call(bf16[128,1600]{1,0:T(8,128)(2,1)} %bitcast.143, bf16[16,400]{1,0:T(8,128)(2,1)} %pad.18.refs_1_, s32[8,128]{1,0:T(8,128)} %pad.19.refs_2_, bf16[128,1600]{1,0:T(8,128)(2,1)} %bitcast.146), custom_call_target="tpu_custom_call" | custom-call | tf_op jit(solution)/shard_map/gather_wt/pallas_call | solution.py:242
  148.6 52.7 %exchange_wt.2 = bf16[4,400,1344]{2,1,0:T(8,128)(2,1)} custom-call(bf16[4,400,1344]{2,1,0:T(8,128)(2,1)} %pad_maximum_fusion.source), custom_call_target="tpu_custom_call" | custom-call | tf_op jit(solution)/shard_map/exchange_wt/pallas_call | solution.py:360
  226.1 29.2 %exchange_ctx.4.in_ref = bf16[32,192,128]{2,1,0:T(8,128)(2,1)} custom-call(bf16[32,192,128]{2,1,0:T(8,128)(2,1)} %concatenate.41.source), custom_call_target="tpu_custom_call" | custom-call | tf_op jit(solution)/shard_map/exchange_ctx/pallas_call | solution.py:360
  256.7 24.8 %attend_forward.1 = (bf16[32,64,128]{2,1,0:T(8,128)(2,1)S(1)}, bf16[8,64,512]{2,1,0:T(8,128)(2,1)S(1)}, bf16[8,64,512]{2,1,0:T(8,128)(2,1)S(1)}, bf16[8,64,512]{...) custom-call(s32[32]{0:T(128)S(1)} %select_reduce_fusion.inverse_ref,, ...), custom_call_target="tpu_custom_call" | custom-call | tf_op jit(solution)/shard_map/attend_forward/pallas_call | solution.py:85
  283.8 14.6 exchange_ctx.5
  306.3 15.3 %scatter_wt.3 = f32[128,1600]{1,0:T(8,128)S(1)} custom-call(f32[4,128,1600]{2,1,0:T(8,128)S(1)} %fusion.19.refs_0_), custom_call_target="tpu_custom_call" | custom-call | tf_op jit(solution)/shard_map/scatter_wt/pallas_call | solution.py:304
  324.2 15.7 %gather_wt.4 = bf16[4,128,1600]{2,1,0:T(8,128)(2,1)} custom-call(bf16[128,1600]{1,0:T(8,128)(2,1)} %add_convert_fusion.1.refs_0_), custom_call_target="tpu_custom_call" | custom-call | tf_op jit(solution)/shard_map/gather_wt/pallas_call | solution.py:242
  347.8 9.2 fusion.49
  369.9 24.3 %scatter_wt.4 = (f32[128,1600]{1,0:T(8,128)S(1)}, f32[128,1600]{1,0:T(8,128)S(1)}) custom-call(f32[4,128,1600]{2,1,0:T(8,128)S(1)} %bitcast.138, f32[4,128,1600]{2,1,0:T(8,128)S(1)} %fusion.14.refs_1_), custom_call_target="tpu_custom_call" | custom-call | tf_op jit(solution)/shard_map/scatter_wt/pallas_call | solution.py:304
  397.5 15.8 %gather_wt.5 = bf16[4,128,1600]{2,1,0:T(8,128)(2,1)} custom-call(bf16[128,1600]{1,0:T(8,128)(2,1)} %fusion.34.refs_0_), custom_call_target="tpu_custom_call" | custom-call | tf_op jit(solution)/shard_map/gather_wt/pallas_call | solution.py:242
  423.5 12.8 exchange_ctx.6.up_ref
  439.4 31.8 %attend_backward.1.source = bf16[32,192,128]{2,1,0:T(8,128)(2,1)S(1)} custom-call(s32[32]{0:T(128)S(1)} %select_reduce_fusion.inverse_ref, s32[32]{0:T(128)S(1)} %fusion.41.place_ref, bf16[32,64,128]{2,1,0:T(8,128)(2,1)S(1)} %copy-done.2, bf16[8,64,512]{2,1,0:T(8,128)(2,1)S(1)} %copy-done.5, bf16[8,64,512]{2,1,0:T(8,128)(2,1)S(1)} %copy-done.7, ...), custom_call_target="tpu_custom_call" | custom-call | tf_op jit(solution)/shard_map/attend_backward/pallas_call | solution.py:162
  472.4 24.0 %exchange_ctx.7 = bf16[32,192,128]{2,1,0:T(8,128)(2,1)} custom-call(bf16[32,192,128]{2,1,0:T(8,128)(2,1)} %copy-done.1), custom_call_target="tpu_custom_call" | custom-call | tf_op jit(solution)/shard_map/exchange_ctx/pallas_call | solution.py:360
  508.6 11.1 concatenate.46
  519.8 9.5 copy.219
  544.3 24.8 %scatter_wt.5 = f32[128,1600]{1,0:T(8,128)S(1)} custom-call(f32[4,128,1600]{2,1,0:T(8,128)S(1)} %fusion.60.refs_0_), custom_call_target="tpu_custom_call" | custom-call | tf_op jit(solution)/shard_map/scatter_wt/pallas_call | solution.py:304
  588.0 15.5 %concatenate.44 = bf16[2804,1600]{0,1:T(8,128)(2,1)} concatenate(bf16[1600,1600]{0,1:T(8,128)(2,1)} %convolution_convert_fusion.2, bf16[1200,1600]{0,1:T(8,128)(2,1)} %copy.186, bf16[1,1600]{0,1:T(8,128)(2,1)S(1)} %reshape.310, bf16[1,1600]{0,1:T(8,128)(2,1)S(1)} %reshape.311, bf16[1,1600]{0,1:T(8,128)(2,1)S(1)} %reshape.312, bf16[1,1600]{0,1:T(8,128)(2,1)S(1)} %reshape.313), dimensions={0} | concatenate | bytes 17945600 | tf_op jit(solution)/shard_map/concatenate | solution.py:524
  603.5 12.8 copy.218
  616.4 8.4 pad.20.clone
  624.9 82.6 %reduce-scatter.9.cloned.1.call-done = bf16[64,1600]{1,0:T(8,128)(2,1)} async-done(((bf16[2048,1600]{1,0:T(8,128)(2,1)}), bf16[64,1600]{1,0:T(8,128)(2,1)}) %reduce-scatter.9.cloned.1.call-update) | async-done | bytes 204816 | tf_op jit(solution)/shard_map/reduce_scatter | solution.py:527
  707.6 246.7 %reduce-scatter.7.cloned.1.call-done = bf16[96,1600]{1,0:T(8,128)(2,1)} async-done(((bf16[3072,1600]{1,0:T(8,128)(2,1)}), bf16[96,1600]{1,0:T(8,128)(2,1)}) %reduce-scatter.7.cloned.1.call-update) | async-done | bytes 307216
  956.5 10.4 exchange_wt.3
  969.5 144.1 %all-gather.5.cloned.1.call-done = bf16[2048,1600]{1,0:T(8,128)(2,1)} async-done(((bf16[64,1600]{1,0:T(8,128)(2,1)}), bf16[2048,1600]{1,0:T(8,128)(2,1)}) %all-gather.5.cloned.1.call-update) | async-done | bytes 6553616 | tf_op jit(solution)/shard_map/all_gather | solution.py:530
  1116.8 8.8 convert_element_type.119
  1132.5 274.2 %all-gather.3.cloned.1.call-done = bf16[4,3072,400]{2,1,0:T(8,128)(2,1)} async-done(((bf16[4,96,400]{2,1,0:T(8,128)(2,1)}), bf16[4,3072,400]{2,1,0:T(8,128)(2,1)}) %all-gather.3.cloned.1.call-update) | async-done | bytes 9830416 | tf_op jit(solution)/shard_map/all_gather | solution.py:529
  1406.7 15.2 %convert_element_type.112 = f32[4,3072,400]{2,1,0:T(8,128)} convert(bf16[4,3072,400]{2,1,0:T(8,128)(2,1)} %all-gather.3.cloned.1.call-done) | non-fusion elementwise | flops 4915200 | bytes 29491200 | tf_op jit(solution)/shard_map/convert_element_type | solution.py:529
  1429.4 13.8 copy.193
  1443.2 11.7 reshape.305
  1454.9 9.4 slice.151
  1464.3 12.7 copy.200
  (265 shorter events, 182.5 us)
Async XLA Ops:
  7.2 700.3 %reduce-scatter.9.cloned.1.call-start = ((), (), s32[]{:S(2)}) async-start(), calls=%async_computation.5 | async-start | bytes 7028736 | tf_op jit(solution)/shard_map/reduce_scatter | solution.py:527
  9.0 292.7 %collective-permute-start = (bf16[48,1600]{1,0:T(8,128)(2,1)}, bf16[48,1600]{1,0:T(8,128)(2,1)}, u32[]{:S(2)}, u32[]{:S(2)}) collective-permute-start(bf16[48,1600]{1,0:T(8,128)(2,1)} %get-tuple-element.180), channel_id=1, source_target_pairs={{0,1},{1,2},{2,3},{3,0},{4,5},{5,6},{6,7},{7,4},{8,9},{9,10},{10,1... | collective-permute-start | bytes 460808 | tf_op jit(solution)/shard_map/ppermute | solution.py:450
  13.1 288.5 %collective-permute-start.1 = (bf16[48,1600]{1,0:T(8,128)(2,1)}, bf16[48,1600]{1,0:T(8,128)(2,1)}, u32[]{:S(2)}, u32[]{:S(2)}) collective-permute-start(bf16[48,1600]{1,0:T(8,128)(2,1)} %get-tuple-element.179), channel_id=1, source_target_pairs={{0,3},{1,0},{2,1},{3,2},{4,7},{5,4},{6,5},{7,6},{8,11},{9,8},{10,9... | collective-permute-start | bytes 460808 | tf_op jit(solution)/shard_map/ppermute | solution.py:451
  43.8 296.2 %collective-permute-start.2 = (bf16[400,1600]{1,0:T(8,128)(2,1)}, bf16[400,1600]{1,0:T(8,128)(2,1)}, u32[]{:S(2)}, u32[]{:S(2)}) collective-permute-start(bf16[400,1600]{1,0:T(8,128)(2,1)} %bitcast.135), channel_id=1, source_target_pairs={{0,1},{1,0},{2,3},{3,2},{4,5},{5,4},{6,7},{7,6},{8,9},{9,8},{10,11... | collective-permute-start | bytes 3840008 | tf_op jit(solution)/shard_map/ppermute | solution.py:382
  45.7 6.2 copy-start.34
  45.7 296.8 %collective-permute-start.3 = (bf16[400,1600]{1,0:T(8,128)(2,1)}, bf16[400,1600]{1,0:T(8,128)(2,1)}, u32[]{:S(2)}, u32[]{:S(2)}) collective-permute-start(bf16[400,1600]{1,0:T(8,128)(2,1)} %bitcast.134), channel_id=1, source_target_pairs={{0,2},{1,3},{2,0},{3,1},{4,6},{5,7},{6,4},{7,5},{8,10},{9,11},{10,... | collective-permute-start | bytes 3840008 | tf_op jit(solution)/shard_map/ppermute | solution.py:382
  49.9 295.2 %collective-permute-start.4 = (bf16[400,1600]{1,0:T(8,128)(2,1)}, bf16[400,1600]{1,0:T(8,128)(2,1)}, u32[]{:S(2)}, u32[]{:S(2)}) collective-permute-start(bf16[400,1600]{1,0:T(8,128)(2,1)} %bitcast.133), channel_id=1, source_target_pairs={{0,3},{1,2},{2,1},{3,0},{4,7},{5,6},{6,5},{7,4},{8,11},{9,10},{10,... | collective-permute-start | bytes 3840008 | tf_op jit(solution)/shard_map/ppermute | solution.py:382
  148.6 52.8 %copy-start.13 = (bf16[4,128,1600]{2,1,0:T(8,128)(2,1)S(1)}, bf16[4,128,1600]{2,1,0:T(8,128)(2,1)}, u32[]{:S(2)}) copy-start(bf16[4,128,1600]{2,1,0:T(8,128)(2,1)} %get-tuple-element.29) | copy-start | bytes 4915204
  148.6 52.8 %copy-start.26 = (bf16[4,128,1600]{2,1,0:T(8,128)(2,1)S(1)}, bf16[4,128,1600]{2,1,0:T(8,128)(2,1)}, u32[]{:S(2)}) copy-start(bf16[4,128,1600]{2,1,0:T(8,128)(2,1)} %get-tuple-element.32) | copy-start | bytes 4915204
  214.6 6.9 copy-start.30
  214.7 6.8 copy-start.36
  306.3 15.4 %copy-start.11 = (bf16[1,128,1600]{2,1,0:T(8,128)(2,1)S(1)}, bf16[1,128,1600]{2,1,0:T(8,128)(2,1)}, u32[]{:S(2)}) copy-start(bf16[1,128,1600]{2,1,0:T(8,128)(2,1)} %copy.171) | copy-start | bytes 1228804
  345.1 11.9 slice-start.5
  347.8 9.2 slice-start.6
  347.8 18.6 %slice-start.3 = ((s8[5324800]{0:T(1024)(128)(4,1)}), s8[4194304]{0:T(1024)(128)(4,1)S(1)}, s32[]{:S(2)}) async-start(s8[5324800]{0:T(1024)(128)(4,1)} %bitcast.152), calls=%async_computation.9 | async-start | bytes 8388608
  357.0 9.3 copy-start.53
  357.0 9.3 slice-start.4
  369.9 24.4 %copy-start.10 = (f32[128,1600]{1,0:T(8,128)S(1)}, f32[128,1600]{1,0:T(8,128)}, u32[]{:S(2)}) copy-start(f32[128,1600]{1,0:T(8,128)} %copy-done.9) | copy-start | bytes 2457604
  395.7 23.9 %copy-start.38 = (f32[128]{0:T(128)}, f32[128]{0:T(128)S(1)}, u32[]{:S(2)}) copy-start(f32[128]{0:T(128)S(1)} %negate_multiply_fusion.1) | copy-start | bytes 1540
  535.6 418.8 %reduce-scatter.7.cloned.1.call-start = ((), (), s32[]{:S(2)}) async-start(), calls=%async_computation.4 | async-start | bytes 10543104
  544.3 24.8 %copy-start.31 = (bf16[4,128,1600]{2,1,0:T(8,128)(2,1)S(1)}, bf16[4,128,1600]{2,1,0:T(8,128)(2,1)}, u32[]{:S(2)}) copy-start(bf16[4,128,1600]{2,1,0:T(8,128)(2,1)} %copy-done.30) | copy-start | bytes 4915204
  544.3 24.8 %copy-start.32 = (bf16[3,400,512]{2,1,0:T(8,128)(2,1)S(1)}, bf16[3,400,512]{2,1,0:T(8,128)(2,1)}, u32[]{:S(2)}) copy-start(bf16[3,400,512]{2,1,0:T(8,128)(2,1)} %get-tuple-element.152) | copy-start | bytes 3686404
  573.4 7.0 copy-start.12
  624.8 342.2 %copy-start.25 = (bf16[1,128,1600]{2,1,0:T(8,128)(2,1)S(1)}, bf16[1,128,1600]{2,1,0:T(8,128)(2,1)}, u32[]{:S(2)}) copy-start(bf16[1,128,1600]{2,1,0:T(8,128)(2,1)} %get-tuple-element.181) | copy-start | bytes 1228804
  624.8 343.1 %copy-start.16 = (f32[128,1600]{1,0:T(8,128)S(1)}, f32[128,1600]{1,0:T(8,128)}, u32[]{:S(2)}) copy-start(f32[128,1600]{1,0:T(8,128)} %copy-done.15) | copy-start | bytes 2457604
  624.8 343.1 %copy-start.18 = (bf16[1,128,1600]{2,1,0:T(8,128)(2,1)S(1)}, bf16[1,128,1600]{2,1,0:T(8,128)(2,1)}, u32[]{:S(2)}) copy-start(bf16[1,128,1600]{2,1,0:T(8,128)(2,1)} %copy.172) | copy-start | bytes 1228804
  624.8 343.1 %copy-start.39 = (f32[128]{0:T(128)S(1)}, f32[128]{0:T(128)}, u32[]{:S(2)}) copy-start(f32[128]{0:T(128)} %copy-done.38) | copy-start | bytes 1540
  624.9 488.8 %all-gather.5.cloned.1.call-start = ((), (), s32[]{:S(2)}) async-start(), calls=%async_computation.3 | async-start | bytes 7028736 | tf_op jit(solution)/shard_map/all_gather | solution.py:530
  707.5 699.2 %all-gather.3.cloned.1.call-start = ((), (), s32[]{:S(2)}) async-start(), calls=%async_computation.2 | async-start | bytes 12976128 | tf_op jit(solution)/shard_map/all_gather | solution.py:529
  1113.6 12.0 slice-start
  1116.8 8.9 slice-start.1
  1406.7 17.4 %copy-start.8 = (bf16[4,3072,400]{2,1,0:T(8,128)(2,1)S(1)}, bf16[4,3072,400]{2,1,0:T(8,128)(2,1)}, u32[]{:S(2)}) copy-start(bf16[4,3072,400]{2,1,0:T(8,128)(2,1)} %all-gather.3.cloned.1.call-done) | copy-start | bytes 29491204
  (39 other events, 123.2 us)
Sparse Core Ops, SparseCore 0:
  535.7 171.7 reduce-scatter.8
  710.7 243.6 reduce-scatter.6
  956.0 157.6 all-gather.4
  1115.1 291.5 all-gather.2

commit v2 on v1

--- a/solution.py
+++ b/solution.py
@@ -13,6 +13,10 @@
 SPAN = GROUP * HEAD_DIM
 EPS = 1e-05
 MESH = pl.DeviceIdType.MESH
+
+
+def cost(micros):
+    return pl.CostEstimate(flops=int(micros * 1e9), bytes_accessed=int(micros * 1e6), transcendentals=0)
 NEG = -1e30
 LOG2E = 1.4426950408889634
 
@@ -254,6 +258,103 @@
     )(*arrays)
 
 
+def prologue(arrays, columns, collective):
+    count = len(arrays)
+    pieces = 5
+    extent = columns.shape[1] // pieces
+
+    def kernel(*refs):
+        sources, (blocks,) = refs[:count], refs[count : count + 1]
+        targets, (filled,) = refs[count + 1 : 2 * count + 1], refs[2 * count + 1 : 2 * count + 2]
+        send, receive, local, cross_send, cross_receive, near_send, near_receive = refs[2 * count + 2 :]
+        ctx, wt = lax.axis_index("ctx"), lax.axis_index("wt")
+        low = lax.rem(ctx, 2)
+        near, far, beside = (ctx, wt ^ 1), (ctx, wt ^ 2), (ctx ^ 1, wt)
+        goes, comes = wt ^ (2 + low), wt ^ (3 - low)
+        greet((near, far, beside, (ctx ^ 1, goes), (ctx ^ 1, comes)))
+
+        def move(item, step, source, slot, peer):
+            return pltpu.make_async_remote_copy(
+                source, targets[item].at[slot], send.at[item, step], receive.at[item, step],
+                device_id=peer, device_id_type=MESH,
+            )
+
+        def cross(index):
+            span = pl.ds(index * extent, extent)
+            return pltpu.make_async_remote_copy(
+                blocks.at[goes, span], filled.at[wt, span], cross_send.at[0, index], cross_receive.at[0, index],
+                device_id=(ctx ^ 1, goes), device_id_type=MESH,
+            )
+
+        def crossed(index):
+            span = pl.ds(index * extent, extent)
+            return pltpu.make_async_remote_copy(
+                filled.at[comes, span], filled.at[comes, span], cross_send.at[0, index], cross_receive.at[0, index],
+                device_id=(ctx ^ 1, goes), device_id_type=MESH,
+            )
+
+        def onward(index):
+            span = pl.ds(index * extent, extent)
+            return pltpu.make_async_remote_copy(
+                filled.at[comes, span], filled.at[comes, span], cross_send.at[1, index], cross_receive.at[1, index],
+                device_id=beside, device_id_type=MESH,
+            )
+
+        firsts = [move(item, 0, sources[item], wt, far) for item in range(count)]
+        for copy in firsts:
+            copy.start()
+        crossings = [cross(index) for index in range(pieces)]
+        for copy in crossings:
+            copy.start()
+        seconds = [move(item, 1, sources[item], wt, near) for item in range(count)]
+        own = [
+            pltpu.make_async_copy(sources[item], targets[item].at[wt], local.at[item])
+            for item in range(count)
+        ]
+        own.append(pltpu.make_async_copy(blocks.at[wt], filled.at[wt], local.at[count]))
+        pair = pltpu.make_async_remote_copy(
+            blocks.at[wt ^ 1], filled.at[wt], near_send, near_receive, device_id=near, device_id_type=MESH
+        )
+        for copy in seconds + own + [pair]:
+            copy.start()
+        thirds = []
+        for item in range(count):
+            firsts[item].wait_recv()
+            copy = move(item, 2, targets[item].at[wt ^ 2], wt ^ 2, near)
+            copy.start()
+            thirds.append(copy)
+        onwards = []
+        for index in range(pieces):
+            crossed(index).wait_recv()
+            copy = onward(index)
+            copy.start()
+            onwards.append(copy)
+        for copy in firsts + crossings:
+            copy.wait_send()
+        for copy in seconds + thirds + own + [pair] + onwards:
+            copy.wait()
+
+    hbm = pl.BlockSpec(memory_space=pl.ANY)
+    return pl.pallas_call(
+        kernel,
+        out_shape=tuple(jax.ShapeDtypeStruct((4,) + member.shape, member.dtype) for member in arrays)
+        + (jax.ShapeDtypeStruct(columns.shape, columns.dtype),),
+        in_specs=[hbm] * (count + 1),
+        out_specs=(hbm,) * (count + 1),
+        scratch_shapes=[
+            pltpu.SemaphoreType.DMA((count, 3)),
+            pltpu.SemaphoreType.DMA((count, 3)),
+            pltpu.SemaphoreType.DMA((count + 1,)),
+            pltpu.SemaphoreType.DMA((2, pieces)),
+            pltpu.SemaphoreType.DMA((2, pieces)),
+            pltpu.SemaphoreType.DMA,
+            pltpu.SemaphoreType.DMA,
+        ],
+        compiler_params=pltpu.CompilerParams(collective_id=collective, has_side_effects=True),
+        name="prologue",
+    )(*arrays, columns)
+
+
 def scatter_wt(parts, collective):
     count = len(parts)
     extents = [member.shape[1:] for member in parts]
@@ -372,16 +473,319 @@
     )(blocks)
 
 
-def swap_wt(blocks):
+def swap_wt(pieces):
     wt = lax.axis_index("wt")
-    kept = lax.dynamic_index_in_dim(blocks, wt, 0, keepdims=False)
-    result = jnp.zeros_like(blocks)
-    result = lax.dynamic_update_index_in_dim(result, kept, wt, 0)
-    for step in (1, 2, 3):
-        piece = lax.dynamic_index_in_dim(blocks, wt ^ step, 0, keepdims=False)
-        piece = lax.ppermute(piece, "wt", [(source, source ^ step) for source in range(4)])
+    stacked = jnp.stack(pieces)
+    result = jnp.zeros_like(stacked)
+    for step in range(4):
+        piece = lax.dynamic_index_in_dim(stacked, wt ^ step, 0, keepdims=False)
+        if step:
+            piece = lax.ppermute(piece, "wt", [(source, source ^ step) for source in range(4)])
         result = lax.dynamic_update_index_in_dim(result, piece, wt ^ step, 0)
     return result
+
+
+def ring_shift(value, axis, step):
+    pairs = []
+    for source in range(32):
+        place = [source // 8, source // 2 % 4, source % 2]
+        place[axis] = (place[axis] + step) % (4, 4, 2)[axis]
+        pairs.append((source, place[0] * 8 + place[1] * 2 + place[2]))
+    return lax.ppermute(value, "ctx", pairs)
+
+
+def spot(axis):
+    ctx = lax.axis_index("ctx")
+    return (ctx // 8, ctx // 2 % 4, ctx % 2)[axis]
+
+
+def pieces_along(value, axis):
+    own = spot(axis)
+    rows = value.shape[0] // 4
+    cut = lambda step: lax.dynamic_slice_in_dim(value, (own + step) % 4 * rows, rows, 0)
+    return [cut(0)] + [ring_shift(cut(step), axis, step) for step in (1, 3, 2)]
+
+
+def added(pieces):
+    total = pieces[0].astype(jnp.float32)
+    for piece in pieces[1:]:
+        total = total + piece.astype(jnp.float32)
+    return total.astype(pieces[0].dtype)
+
+
+def passed_along(value, axis):
+    return [value] + [ring_shift(value, axis, step) for step in (1, 3, 2)]
+
+
+def outer_start(place):
+    return pl.multiple_of(16 * (13 * place - 1 + (4 - place) // 4), 16)
+
+
+def reduce_spread(first, second, outer, collective, micros):
+    features = first.shape[1]
+    share = features // 4
+    size, inner, stride = (208, 64, 48) if outer else (400, 112, 96)
+    low = jnp.bfloat16
+
+    def kernel(first_ref, second_ref, first_out, second_out, *scratch):
+        window, outer_in, inner_in, mid, pair_in, lanes_out, lanes_in, inner_all, outer_send, outer_receive, inner_send, inner_receive, pair_send, pair_receive, lane_send, lane_receive, all_send, all_receive, spread_send, spread_receive = scratch
+        ctx, wt = lax.axis_index("ctx"), lax.axis_index("wt")
+        y, z, low_x = ctx // 8, ctx // 2 % 4, ctx % 2
+        at_y = lambda place: (place * 8 + z * 2 + low_x, wt)
+        at_z = lambda place: (y * 8 + place * 2 + low_x, wt)
+        beside = (ctx ^ 1, wt)
+        halves = [(y, at_y, z, at_z, first_ref, first_out), (z, at_z, y, at_y, second_ref, second_out)]
+        peers = [at_y((y + step) % 4) for step in (1, 2, 3)] + [at_z((z + step) % 4) for step in (1, 2, 3)]
+        peers += [beside] + [(ctx, wt ^ step) for step in (1, 2, 3)]
+        greet(peers)
+        inner_at = lambda place: pl.ds(pl.multiple_of(stride * place, 16), inner)
+
+        def remote(source, target, sends, receives, device):
+            return pltpu.make_async_remote_copy(
+                source, target, sends, receives, device_id=device, device_id_type=MESH
+            )
+
+        started = []
+        if outer:
+            copies = [[], []]
+            for step in (1, 3, 2):
+                for half, (place, at, _, _, source, _) in enumerate(halves):
+                    other = (place + step) % 4
+                    copy = remote(
+                        source.at[pl.ds(outer_start(other), size)], outer_in.at[half, step - 1],
+                        outer_send.at[half, step - 1], outer_receive.at[half, step - 1], at(other),
+                    )
+                    copy.start()
+                    copies[half].append(copy)
+            for half, (place, _, _, _, source, _) in enumerate(halves):
+                for copy in copies[half]:
+                    copy.wait_recv()
+                total = source[pl.ds(outer_start(place), size)].astype(jnp.float32)
+                for step in range(3):
+                    total += outer_in[half, step].astype(jnp.float32)
+                window[half] = total.astype(low)
+            started += copies[0] + copies[1]
+        else:
+            for half in range(2):
+                window[half] = halves[half][4][...]
+        copies = [[], []]
+        for half, (_, _, place, at, _, _) in enumerate(halves):
+            for step in (1, 3, 2):
+                other = (place + step) % 4
+                copy = remote(
+                    window.at[half, inner_at(other)], inner_in.at[half, step - 1],
+                    inner_send.at[half, step - 1], inner_receive.at[half, step - 1], at(other),
+                )
+                copy.start()
+                copies[half].append(copy)
+        pairs = []
+        for half, (_, _, place, _, _, _) in enumerate(halves):
+            for copy in copies[half]:
+                copy.wait_recv()
+            total = window[half, inner_at(place)].astype(jnp.float32)
+            for step in range(3):
+                total += inner_in[half, step].astype(jnp.float32)
+            mid[half] = total.astype(low)
+            copy = remote(mid.at[half], pair_in.at[half], pair_send.at[half], pair_receive.at[half], beside)
+            copy.start()
+            pairs.append(copy)
+        started += copies[0] + copies[1] + pairs
+
+        def to_owners(half):
+            total = (mid[half].astype(jnp.float32) + pair_in[half].astype(jnp.float32)).astype(low)
+            pair_in[half] = total
+            moves = []
+            for owner in range(4):
+                lanes_out[half, owner] = total[:, owner * share : (owner + 1) * share]
+            for step in (2, 3, 1):
+                copy = remote(
+                    lanes_out.at[half, wt ^ step], lanes_in.at[half, wt],
+                    lane_send.at[half, step - 1], lane_receive.at[half, step - 1], (ctx, wt ^ step),
+                )
+                copy.start()
+                moves.append(copy)
+            lanes_in[half, wt] = lanes_out[half, wt]
+            return moves
+
+        def from_owners(half, moves, keep):
+            for copy in moves:
+                copy.wait_recv()
+            for sender in range(4):
+                part = lanes_in[half, sender]
+                if keep is not None:
+                    part = jnp.where(keep, pair_in[half, :, sender * share : (sender + 1) * share], part)
+                pair_in[half, :, sender * share : (sender + 1) * share] = part
+
+        def spread_inner(half):
+            _, _, place, at, _, _ = halves[half]
+            moves = []
+            for step in (1, 3, 2):
+                copy = remote(
+                    pair_in.at[half], inner_all.at[half, place],
+                    all_send.at[half, step - 1], all_receive.at[half, step - 1], at((place + step) % 4),
+                )
+                copy.start()
+                moves.append(copy)
+            inner_all[half, place] = pair_in[half]
+            return moves
+
+        def fill(half, moves):
+            for copy in moves:
+                copy.wait_recv()
+            for place in range(4):
+                window[half, stride * place : stride * place + inner] = inner_all[half, place]
+
+        pairs[0].wait_recv()
+        lane_moves = to_owners(0)
+        pairs[1].wait_recv()
+        if outer:
+            second_lanes = to_owners(1)
+        else:
+            pair_in[1] = (mid[1].astype(jnp.float32) + pair_in[1].astype(jnp.float32)).astype(low)
+            second_lanes = []
+            second_moves = spread_inner(1)
+        from_owners(0, lane_moves, None)
+        first_moves = spread_inner(0)
+        if outer:
+            from_owners(1, second_lanes, z >= 2)
+            second_moves = spread_inner(1)
+        for copy in started:
+            copy.wait_send()
+        spreads = []
+        for half, moves in ((0, first_moves), (1, second_moves)):
+            fill(half, moves)
+            place, at, _, _, _, target = halves[half]
+            if outer:
+                for step in (1, 3, 2):
+                    copy = remote(
+                        window.at[half], target.at[place],
+                        spread_send.at[half, step - 1], spread_receive.at[half, step - 1], at((place + step) % 4),
+                    )
+                    copy.start()
+                    spreads.append(copy)
+                target[place] = window[half]
+            else:
+                target[...] = window[half]
+        for copy in lane_moves + second_lanes + first_moves + second_moves:
+            copy.wait_send()
+        for copy in spreads:
+            copy.wait()
+
+    vmem = pl.BlockSpec(memory_space=pltpu.VMEM)
+    result = jax.ShapeDtypeStruct((4, size, features) if outer else (size, features), low)
+    pairs_of = lambda: [pltpu.SemaphoreType.DMA((2, 3)), pltpu.SemaphoreType.DMA((2, 3))]
+    return pl.pallas_call(
+        kernel,
+        out_shape=(result, result),
+        in_specs=[vmem] * 2,
+        out_specs=(vmem,) * 2,
+        scratch_shapes=[
+            pltpu.VMEM((2, size, features), low),
+            pltpu.VMEM((2, 3, size if outer else 16, features), low),
+            pltpu.VMEM((2, 3, inner, features), low),
+            pltpu.VMEM((2, inner, features), low),
+            pltpu.VMEM((2, inner, features), low),
+            pltpu.VMEM((2, 4, inner, share), low),
+            pltpu.VMEM((2, 4, inner, share), low),
+            pltpu.VMEM((2, 4, inner, features), low),
+        ]
+        + pairs_of()
+        + pairs_of()
+        + [pltpu.SemaphoreType.DMA((2,)), pltpu.SemaphoreType.DMA((2,))]
+        + pairs_of()
+        + pairs_of()
+        + pairs_of(),
+        compiler_params=pltpu.CompilerParams(
+            collective_id=collective, has_side_effects=True, vmem_limit_bytes=48 * 2**20
+        ),
+        cost_estimate=cost(micros),
+        name="reduce_spread",
+    )(first, second)
+
+
+def turn_rows(pieces, place, width):
+    rows, features = pieces[0].shape
+    share = features // 4
+
+    def kernel(place_ref, *refs):
+        out, held = refs[4:]
+        for step, piece in zip((0, 1, 3, 2), refs[:4]):
+            held[lax.rem(place_ref[0] + 4 - step, 4)] = piece[...]
+        for block in range(4):
+            for sender in range(4):
+                part = held[block, :, sender * share : (sender + 1) * share].astype(jnp.float32).T
+                start = sender * width + block * rows
+                out[:, start : start + rows] = part
+
+    vmem = pl.BlockSpec(memory_space=pltpu.VMEM)
+    return pl.pallas_call(
+        kernel,
+        out_shape=jax.ShapeDtypeStruct((share, 4 * width), jnp.float32),
+        in_specs=[pl.BlockSpec(memory_space=pltpu.SMEM)] + [vmem] * 4,
+        out_specs=vmem,
+        scratch_shapes=[pltpu.VMEM((4, rows, features), pieces[0].dtype)],
+        compiler_params=pltpu.CompilerParams(vmem_limit_bytes=48 * 2**20),
+        cost_estimate=cost(9),
+        name="turn_rows",
+    )(place.reshape(1), *pieces)
+
+
+def place_rows(pieces, place):
+    rows, features = pieces[0].shape
+
+    def kernel(place_ref, *refs):
+        out = refs[4]
+        for step, piece in zip((0, 1, 3, 2), refs[:4]):
+            start = pl.multiple_of(lax.rem(place_ref[0] + 4 - step, 4) * rows, 16)
+            out[pl.ds(start, rows), :] = piece[...].astype(jnp.float32)
+
+    vmem = pl.BlockSpec(memory_space=pltpu.VMEM)
+    return pl.pallas_call(
+        kernel,
+        out_shape=jax.ShapeDtypeStruct((4 * rows, features), jnp.float32),
+        in_specs=[pl.BlockSpec(memory_space=pltpu.SMEM)] + [vmem] * 4,
+        out_specs=vmem,
+        compiler_params=pltpu.CompilerParams(vmem_limit_bytes=48 * 2**20),
+        cost_estimate=cost(6),
+        name="place_rows",
+    )(place.reshape(1), *pieces)
+
+
+def turn_windows(first, second):
+    size, features = first.shape[1:]
+    share = features // 4
+    cut = 2 * size - share
+
+    def kernel(first_ref, second_ref, qkv_ref, out_ref):
+        def lay(source, block, skip, start):
+            rows = size - skip
+            for sender in range(4):
+                part = source[block, skip:, sender * share : (sender + 1) * share].astype(jnp.float32).T
+                at = start + sender * share
+                qkv_ref[:, at : at + rows] = part
+
+        lay(first_ref, 0, 0, 0)
+        lay(first_ref, 1, cut, size)
+        lay(first_ref, 2, cut, features)
+        lay(first_ref, 3, 0, features + size - cut)
+        lay(second_ref, 0, 0, 2 * features)
+        lay(second_ref, 1, cut, 2 * features + size)
+        out_ref[: size - cut] = second_ref[2, cut:].astype(jnp.float32)
+        out_ref[size - cut :] = second_ref[3].astype(jnp.float32)
+
+    vmem = pl.BlockSpec(memory_space=pltpu.VMEM)
+    return pl.pallas_call(
+        kernel,
+        out_shape=(
+            jax.ShapeDtypeStruct((share, 3 * features), jnp.float32),
+            jax.ShapeDtypeStruct((share, features), jnp.float32),
+        ),
+        in_specs=[vmem] * 2,
+        out_specs=(vmem,) * 2,
+        compiler_params=pltpu.CompilerParams(vmem_limit_bytes=48 * 2**20),
+        cost_estimate=cost(9),
+        name="turn_windows",
+    )(first, second)
 
 
 def to_heads(rows_by_token):
@@ -421,35 +825,37 @@
     ctx_count = lax.axis_size("ctx")
     rows, features = inputs.shape[1:]
     share = features // 4
+    ff = w_fc.shape[1] // 4
     shift = 16 * wt
 
     small = jnp.stack([ln1_gain, ln1_bias, bias_q, bias_v, bias_out, ln2_gain, ln2_bias, bias_proj])
     small = jnp.pad(small, ((0, 8), (0, 0)))
     order = jnp.pad(block_order, ((0, 7), (0, 128 - ctx_count)))
-    all_inputs, all_small, all_order, all_cot = gather_wt((inputs[0], small, order, cotangent[0]), 1)
+    starts = [384 * member for member in range(4)]
+    columns = jnp.stack(
+        [
+            jnp.concatenate(
+                [w_qkv[:, part * features + start : part * features + start + SPAN] for part in range(3)],
+                axis=1,
+            )
+            for start in starts
+        ]
+    )
+    all_inputs, all_small, all_order, own_qkv = prologue((inputs[0], small, order), columns, 1)
+    own_qkv = own_qkv.reshape(features, 3 * SPAN)
     vectors = all_small[:, :8].transpose(1, 0, 2).reshape(8, features).astype(jnp.float32)
     gain_one, shift_one, full_bq, full_bv, full_bout, gain_two, shift_two, full_bproj = vectors
     orders = all_order[:, 0, :ctx_count]
     place = lax.dynamic_index_in_dim(orders, jnp.minimum(ctx // GROUP, 3), 0, keepdims=False)
     slots = jnp.arange(ctx_count, dtype=jnp.int32)
     inverse = jnp.sum(jnp.where(place[None, :] == slots[:, None], slots[None, :], 0), axis=1)
-
-    starts = [384 * member for member in range(4)]
-    columns = jnp.stack(
-        [
-            jnp.concatenate(
-                [w_qkv[:, part * features + start : part * features + start + SPAN] for part in range(3)],
-                axis=1,
-            )
-            for start in starts
-        ]
-    )
-    own_qkv = exchange(columns, "wt", 2).reshape(features, 3 * SPAN)
-    own_fc = swap_wt(w_fc.reshape(share, 4, -1).transpose(1, 0, 2)).reshape(features, -1)
+    later_fc, later_out, later_cot, own_qkv = lax.optimization_barrier((w_fc, w_out, cotangent[0], own_qkv))
+    own_fc = swap_wt([later_fc[:, rows_ff * ff : (rows_ff + 1) * ff] for rows_ff in range(4)]).reshape(features, ff)
+    group_cot = swap_wt([later_cot] * 4).reshape(4 * rows, features)
     edge = SPAN - share
-    below = lax.ppermute(w_out[share - edge :], "wt", [(source, (source + 1) % 4) for source in range(4)])
-    above = lax.ppermute(w_out[:edge], "wt", [(source, (source - 1) % 4) for source in range(4)])
-    wide_out = lax.dynamic_slice_in_dim(jnp.concatenate([below, w_out, above]), edge - shift, SPAN, 0)
+    below = lax.ppermute(later_out[share - edge :], "wt", [(source, (source + 1) % 4) for source in range(4)])
+    above = lax.ppermute(later_out[:edge], "wt", [(source, (source - 1) % 4) for source in range(4)])
+    wide_out = lax.dynamic_slice_in_dim(jnp.concatenate([below, later_out, above]), edge - shift, SPAN, 0)
     span_ids = jnp.arange(SPAN, dtype=jnp.int32)
     mine = (span_ids >= shift) & (span_ids < shift + share)
     masked_out = jnp.where(mine[:, None], wide_out, 0)
@@ -477,17 +883,20 @@
     all_two = all_two.reshape(4 * rows, features)
     hidden_pre = dot(all_two, own_fc) + bias_fc.astype(jnp.float32)
     hidden_low = gelu_tanh(hidden_pre).astype(jnp.bfloat16)
-    group_cot = all_cot.reshape(4 * rows, features)
     hidden_grad = dot(group_cot, w_proj, 1, 1)
     unused_gelu, gelu_back = jax.vjp(gelu_tanh, hidden_pre)
     pre_grad = gelu_back(hidden_grad)[0].astype(jnp.bfloat16)
-    projected_out, normed_two_grad = scatter_wt(
-        (
-            dot(hidden_low, w_proj).reshape(4, rows, features),
-            dot(pre_grad, own_fc, 1, 1).reshape(4, rows, features),
-        ),
-        7,
+    low = jnp.bfloat16
+    grad_fc = dot(pre_grad, all_two, 0, 0).astype(low)
+    grad_proj = dot(hidden_low, group_cot, 0, 0).astype(low)
+    terms_two = (
+        dot(hidden_low, w_proj).reshape(4, rows, features),
+        dot(pre_grad, own_fc, 1, 1).reshape(4, rows, features),
     )
+    terms_two, grad_fc, grad_proj = lax.optimization_barrier((terms_two, grad_fc, grad_proj))
+    window_fc = added(pieces_along(grad_fc, 0))
+    window_proj = added(pieces_along(grad_proj, 1))
+    projected_out, normed_two_grad = scatter_wt(terms_two, 7)
     outputs = middle + projected_out + full_bproj
     unused_norm, norm_back = jax.vjp(layer_norm, middle, gain_two, shift_two)
     middle_part, grad_gain_two, grad_shift_two = norm_back(normed_two_grad)
@@ -498,6 +907,10 @@
 
     attended_grad = dot(wide_out, all_branch, 1, 1).astype(jnp.bfloat16)
     upstream = exchange(to_heads(attended_grad), "ctx", 9)
+    upstream, window_fc, window_proj = lax.optimization_barrier((upstream, window_fc, window_proj))
+    window_fc, window_proj = reduce_spread(window_fc, window_proj, False, 12, 30)
+    upstream, window_fc, window_proj = lax.optimization_barrier((upstream, window_fc, window_proj))
+    all_fc, all_proj = passed_along(window_fc, 0), passed_along(window_proj, 1)
     grad_blocks = attend_backward(upstream, inverse, place, saved, block)
     stacked = from_heads(exchange(grad_blocks, "ctx", 10))
     masked = jnp.where(jnp.tile(mine, 3)[:, None], stacked, 0)
@@ -506,11 +919,8 @@
     input_part, grad_gain_one, grad_shift_one = first_back(normed_one_grad)
     input_grad = middle_grad + input_part
 
-    low = jnp.bfloat16
     own_stacked = lax.dynamic_slice_in_dim(stacked.reshape(3, SPAN, -1), shift, share, 1)
     own_attended = lax.dynamic_slice_in_dim(attended, shift, share, 0)
-    grad_proj = dot(hidden_low, group_cot, 0, 0).astype(low)
-    grad_fc = dot(pre_grad, all_two, 0, 0).astype(low)
     grad_qkv = dot(own_stacked.reshape(3 * share, -1), normed_one).astype(low)
     grad_out = dot(own_attended, all_branch).astype(low)
     column = lambda value: lax.dynamic_slice_in_dim(value, share * wt, share, 0)
@@ -520,21 +930,15 @@
     grad_bfc = jnp.sum(pre_grad.astype(jnp.float32), axis=0)
     crossed_vectors = jnp.stack([grad_gain_one, grad_shift_one, grad_gain_two, grad_shift_two]).astype(low)
     kept_vectors = jnp.stack([jnp.concatenate([sums[0], sums[2], grad_bout, grad_bproj]), grad_bfc]).astype(low)
-    pad = lambda value, extent: jnp.pad(value, ((0, extent - value.shape[0]), (0, 0)))
-    crossed = pad(jnp.concatenate([grad_fc, grad_qkv, crossed_vectors]), 96 * ctx_count)
-    kept = pad(jnp.concatenate([grad_proj, grad_out, kept_vectors]), 64 * ctx_count)
-    crossed_chunk = lax.psum_scatter(crossed, "ctx", scatter_dimension=0, tiled=True)
-    kept_chunk = lax.psum_scatter(kept, "ctx", scatter_dimension=0, tiled=True)
-    crossed_chunk = exchange(crossed_chunk.reshape(96, 4, share).transpose(1, 0, 2), "wt", 12)
-    crossed_all = lax.all_gather(crossed_chunk, "ctx", axis=1, tiled=True).astype(jnp.float32)
-    kept_all = lax.all_gather(kept_chunk, "ctx", axis=0, tiled=True).astype(jnp.float32)
-    ff = grad_fc.shape[0]
-    sum_fc = crossed_all[:, :ff].transpose(2, 0, 1).reshape(share, 4 * ff)
-    sum_qkv = crossed_all[:, ff : ff + 3 * share].reshape(4, 3, share, share)
-    sum_qkv = sum_qkv.transpose(3, 1, 0, 2).reshape(share, 3 * features)
-    norms = jnp.sum(crossed_all[:, ff + 3 * share : ff + 3 * share + 4], axis=0)
-    sum_proj, sum_out = kept_all[:ff], kept_all[ff : ff + share]
-    kept_sums = kept_all[ff + share : ff + share + 2]
+    tail = lambda value: jnp.pad(value, ((0, 16 - value.shape[0]), (0, 0)))
+    first = jnp.concatenate([grad_qkv[:share], tail(crossed_vectors), grad_qkv[share : 2 * share]])
+    second = jnp.concatenate([grad_qkv[2 * share :], tail(kept_vectors), grad_out])
+    first, second = reduce_spread(first, second, True, 13, 110)
+    sum_fc = turn_rows(all_fc, spot(0), ff)
+    sum_proj = place_rows(all_proj, spot(1))
+    sum_qkv, sum_out = turn_windows(first, second)
+    norms = jnp.sum(first[2, :4].reshape(4, 4, share).astype(jnp.float32), axis=1)
+    kept_sums = second[2, :2].astype(jnp.float32)
     sum_bq, sum_bv, sum_bout, sum_bproj = kept_sums[0].reshape(4, share)
     return (
         outputs.astype(jnp.bfloat16)[None],

time: 1490 us -> 846 us (0.57)
  waiting for transfers between devices: 748 us -> 17.1 us
  Pallas kernels: 371 us -> 590 us
  local copies, waits for them, and re-layouts: 240 us -> 107 us
  starting transfers between devices: 8.05 us -> 32.1 us
    all_gather x2 -> x0, waiting for transfers between devices: 418 us -> none  [the longest x1 274 us: local(): lax.all_gather(crossed_chunk, 'ctx', axis=1, tiled=True).astype(jnp.float32)]
    pallas_call x0 -> x6, Pallas kernels: none -> 258 us  [the longest x2 177 us: reduce_spread(): pl.pallas_call(kernel, out_shape=(result, result), in_specs=[vmem] * 2, o...]
    unnamed x5 -> x0, waiting for transfers between devices: 247 us -> none
    reduce_scatter x1 -> x0, waiting for transfers between devices: 82.6 us -> none  [local(): kept_chunk = lax.psum_scatter(kept, 'ctx', scatter_dimension=0, tiled=True)]
    pallas_call x3 -> x2, Pallas kernels: 106 us -> 33.5 us  [gather_wt(): pl.pallas_call(kernel, out_shape=tuple((jax.ShapeDtypeStruct((4,) + membe...]
    pallas_call x3, Pallas kernels: 64.4 us -> 104 us  [scatter_wt(): pl.pallas_call(kernel, out_shape=tuple((jax.ShapeDtypeStruct(extent, jnp....]
    unnamed x134 -> x131, local copies, waits for them, and re-layouts: 59.5 us -> 26.6 us
    concatenate x2 -> x0, local copies, waits for them, and re-layouts: 26.7 us -> none  [the longest x1 15.5 us: local(): jnp.concatenate([grad_fc, grad_qkv, crossed_vectors])]
  transfers between devices with their start and end apart: 9 -> 20, of which waited for: 4 -> 2; matrix products, arithmetic and copies ran while one was open for 12% -> 12% of each run, Pallas kernels for 18% -> 52%
where the time goes in v2:
time: 846 us; the launch traced here: 840 us
  Pallas kernels  590 us (70%)
  local copies, waits for them, and re-layouts  107 us (13%)
  matrix products  58 us (7%)
  other arithmetic  34.2 us (4%)
  starting transfers between devices  32.1 us (4%)
  waiting for transfers between devices  17.1 us (2%)
    pallas_call x2, Pallas kernels, reduce_spread(): pl.pallas_call(kernel, out_shape=(result, result), in_specs=[vmem] * 2, o...  177 us
    pallas_call x4, Pallas kernels, exchange(): pl.pallas_call(kernel, out_shape=jax.ShapeDtypeStruct(blocks.shape, block...  137 us
    pallas_call x3, Pallas kernels, scatter_wt(): pl.pallas_call(kernel, out_shape=tuple((jax.ShapeDtypeStruct(extent, jnp....  104 us
    dot_general x12, matrix products, dot(): lax.dot_general(left, right, (((left_dim,), (right_dim,)), ((), ())), pre...  58 us
    pallas_call x1, Pallas kernels, prologue(): pl.pallas_call(kernel, out_shape=tuple((jax.ShapeDtypeStruct((4,) + membe...  53 us
    pallas_call x2, Pallas kernels, gather_wt(): pl.pallas_call(kernel, out_shape=tuple((jax.ShapeDtypeStruct((4,) + membe...  33.5 us
    pallas_call x1, Pallas kernels, attend_backward(): pl.pallas_call(kernel, out_shape=jax.ShapeDtypeStruct((parts, 3 * dim, ro...  32.1 us
    unnamed x131, local copies, waits for them, and re-layouts  26.6 us
  transfers between devices with their start and end apart: 20, of which 2 were waited for; matrix products, arithmetic and copies ran while one was open for 12% of the time, Pallas kernels for 52%

profile of v2, /device:TPU:1, one launch (start us, length us, event | category | flops | bytes accessed | tf_op | source)
XLA Modules:
  0.0 839.8 jit_solution(2185700326364097104)
XLA Ops:
  9.4 5.2 fusion.68
  30.0 53.0 %prologue.1 = (bf16[4,128,1600]{2,1,0:T(8,128)(2,1)}, bf16[4,16,400]{2,1,0:T(8,128)(2,1)}, s32[4,8,128]{2,1,0:T(8,128)}, bf16[4,400,1344]{2,1,0:T(8,128)(2,1)}) custom-call(bf16[128,1600]{1,0:T(8,128)(2,1)} %bitcast.158, bf16[16,400]{1,0:T(8,128)(2,1)} %pad.18.refs_1_, s32[8,128]{1,0:T(8,128)} %pad.19.refs_2_, bf16[4,400,1344]{2,1,0:T(8,128)(2,1)} %pad_maximum_fusion.1.refs_3_), custom_call_target="tpu_custom_call" | custom-call | tf_op jit(solution)/shard_map/prologue/pallas_call | solution.py:338
  97.2 5.8 slice_bitcast_fusion.3
  109.2 7.0 fusion.13
  126.5 26.8 %exchange_ctx.4.in_ref = bf16[32,192,128]{2,1,0:T(8,128)(2,1)} custom-call(bf16[32,192,128]{2,1,0:T(8,128)(2,1)} %concatenate.39.source), custom_call_target="tpu_custom_call" | custom-call | tf_op jit(solution)/shard_map/exchange_ctx/pallas_call | solution.py:461
  154.8 24.9 %attend_forward.1 = (bf16[32,64,128]{2,1,0:T(8,128)(2,1)S(1)}, bf16[8,64,512]{2,1,0:T(8,128)(2,1)S(1)}, bf16[8,64,512]{2,1,0:T(8,128)(2,1)S(1)}, bf16[8,64,512]{...) custom-call(s32[32]{0:T(128)S(1)} %select_reduce_fusion.inverse_ref,, ...), custom_call_target="tpu_custom_call" | custom-call | tf_op jit(solution)/shard_map/attend_forward/pallas_call | solution.py:89
  185.2 13.7 %exchange_ctx.5 = bf16[32,64,128]{2,1,0:T(8,128)(2,1)} custom-call(bf16[32,64,128]{2,1,0:T(8,128)(2,1)} %copy-done.10), custom_call_target="tpu_custom_call" | custom-call | tf_op jit(solution)/shard_map/exchange_ctx/pallas_call | solution.py:461
  201.2 4.7 collective-permute-start.4
  208.9 62.9 %scatter_wt.3 = f32[128,1600]{1,0:T(8,128)S(1)} custom-call(f32[4,128,1600]{2,1,0:T(8,128)S(1)} %fusion.19.refs_0_), custom_call_target="tpu_custom_call" | custom-call | tf_op jit(solution)/shard_map/scatter_wt/pallas_call | solution.py:405
  274.0 17.6 %gather_wt.2 = bf16[4,128,1600]{2,1,0:T(8,128)(2,1)} custom-call(bf16[128,1600]{1,0:T(8,128)(2,1)} %add_convert_fusion.4.refs_0_), custom_call_target="tpu_custom_call" | custom-call | tf_op jit(solution)/shard_map/gather_wt/pallas_call | solution.py:246
  306.7 5.9 convolution_add_fusion.1
  312.6 5.4 fusion.60
  318.0 7.7 fusion.62
  325.8 6.9 convolution_convert_fusion.1
  332.7 4.8 convolution_convert_fusion.2
  337.5 4.9 fusion.14
  347.8 24.7 %scatter_wt.4 = (f32[128,1600]{1,0:T(8,128)S(1)}, f32[128,1600]{1,0:T(8,128)S(1)}) custom-call(f32[4,128,1600]{2,1,0:T(8,128)S(1)} %bitcast.157, f32[4,128,1600]{2,1,0:T(8,128)S(1)} %copy.68.refs_1_), custom_call_target="tpu_custom_call" | custom-call | tf_op jit(solution)/shard_map/scatter_wt/pallas_call | solution.py:405
  373.0 4.2 constant_dynamic-slice_fusion.6
  385.1 15.9 %gather_wt.3 = bf16[4,128,1600]{2,1,0:T(8,128)(2,1)} custom-call(bf16[128,1600]{1,0:T(8,128)(2,1)} %fusion.34.refs_0_), custom_call_target="tpu_custom_call" | custom-call | tf_op jit(solution)/shard_map/gather_wt/pallas_call | solution.py:246
  401.1 4.3 constant_dynamic-slice_fusion.3
  414.8 57.0 %exchange_ctx.6.up_ref = bf16[32,64,128]{2,1,0:T(8,128)(2,1)} custom-call(bf16[32,64,128]{2,1,0:T(8,128)(2,1)} %concatenate.41.source), custom_call_target="tpu_custom_call" | custom-call | tf_op jit(solution)/shard_map/exchange_ctx/pallas_call | solution.py:461
  481.3 66.1 %reduce_spread.2 = (bf16[400,1600]{1,0:T(8,128)(2,1)S(1)}, bf16[400,1600]{1,0:T(8,128)(2,1)}) custom-call(bf16[400,1600]{1,0:T(8,128)(2,1)S(1)} %add_convert_fusion.2.first_ref, bf16[400,1600]{1,0:T(8,128)(2,1)S(1)} %add_convert_fusion.1.second_ref), custom_call_target="tpu_custom_call" | custom-call | flops 30000001024 | bytes 30000000 | tf_op jit(solution)/shard_map/reduce_spread/pallas_call | solution.py:677
  556.0 32.1 %attend_backward.1.source = bf16[32,192,128]{2,1,0:T(8,128)(2,1)S(1)} custom-call(s32[32]{0:T(128)S(1)} %select_reduce_fusion.inverse_ref, s32[32]{0:T(128)S(1)} %fusion.51.place_ref, bf16[32,64,128]{2,1,0:T(8,128)(2,1)S(1)} %copy-done.3, bf16[8,64,512]{2,1,0:T(8,128)(2,1)S(1)} %copy-done.12, bf16[8,64,512]{2,1,0:T(8,128)(2,1)S(1)} %copy-done.14, ...), custom_call_target="tpu_custom_call" | custom-call | tf_op jit(solution)/shard_map/attend_backward/pallas_call | solution.py:166
  589.3 39.7 %exchange_ctx.7 = bf16[32,192,128]{2,1,0:T(8,128)(2,1)} custom-call(bf16[32,192,128]{2,1,0:T(8,128)(2,1)} %copy-done.1), custom_call_target="tpu_custom_call" | custom-call | tf_op jit(solution)/shard_map/exchange_ctx/pallas_call | solution.py:461
  636.5 5.8 fusion.refs_0_
  642.3 16.1 %scatter_wt.5 = f32[128,1600]{1,0:T(8,128)S(1)} custom-call(f32[4,128,1600]{2,1,0:T(8,128)S(1)} %fusion.refs_0_), custom_call_target="tpu_custom_call" | custom-call | tf_op jit(solution)/shard_map/scatter_wt/pallas_call | solution.py:405
  669.4 4.2 convolution_convert_fusion
  675.9 111.0 %reduce_spread.3 = (bf16[4,208,1600]{2,1,0:T(8,128)(2,1)}, bf16[4,208,1600]{2,1,0:T(8,128)(2,1)}) custom-call(bf16[816,1600]{1,0:T(8,128)(2,1)S(1)} %pad_maximum_fusion.2.first_ref, bf16[816,1600]{1,0:T(8,128)(2,1)S(1)} %pad_maximum_fusion.3.second_ref), custom_call_target="tpu_custom_call" | custom-call | flops 109999996928 | bytes 110000000 | tf_op jit(solution)/shard_map/reduce_spread/pallas_call | solution.py:677
  792.8 9.0 %turn_windows.1 = (f32[400,4800]{1,0:T(8,128)}, f32[400,1600]{1,0:T(8,128)}) custom-call(bf16[4,208,1600]{2,1,0:T(8,128)(2,1)S(1)} %copy-done.15, bf16[4,208,1600]{2,1,0:T(8,128)(2,1)S(1)} %copy-done.16), custom_call_target="tpu_custom_call" | custom-call | flops 8999999488 | bytes 9000000 | tf_op jit(solution)/shard_map/turn_windows/pallas_call | solution.py:777
  804.0 12.1 %turn_rows.1 = f32[400,6400]{1,0:T(8,128)} custom-call(s32[1]{0:T(128)} %bitcast.59.place_ref, bf16[400,1600]{1,0:T(8,128)(2,1)S(1)} %get-tuple-element.79.refs_0_, bf16[400,1600]{1,0:T(8,128)(2,1)} %collective-permute-done.14.refs_1_, bf16[400,1600]{1,0:T(8,128)(2,1)} %collective-permute-done.15.refs_2_, bf16[400,1600]{1,0:T(8,128)(2,1)S(1)} %collective-permute-done.16.refs_3_), custom_call_target="tpu_custom_call" | custom-call | flops 8999999488 | bytes 9000000 | tf_op jit(solution)/shard_map/turn_rows/pallas_call | solution.py:721
  816.1 16.5 %collective-permute-done.17.refs_1_ = bf16[400,1600]{1,0:T(8,128)(2,1)S(1)} collective-permute-done((bf16[400,1600]{1,0:T(8,128)(2,1)}, bf16[400,1600]{1,0:T(8,128)(2,1)S(1)}, u32[]{:S(2)}, u32[]{:S(2)}) %collective-permute-start.17) | collective-permute-done | bytes 1280032 | tf_op jit(solution)/shard_map/ppermute | solution.py:494
  832.6 7.0 place_rows.1
  (287 shorter events, 155.0 us)
Async XLA Ops:
  9.3 95.0 %copy-start.23 = (bf16[1,128,1600]{2,1,0:T(8,128)(2,1)}, bf16[1,128,1600]{2,1,0:T(8,128)(2,1)S(1)}, u32[]{:S(2)}) copy-start(bf16[1,128,1600]{2,1,0:T(8,128)(2,1)S(1)} %copy.61) | copy-start | bytes 1228804
  83.0 213.1 %collective-permute-start.7 = (bf16[128,1600]{1,0:T(8,128)(2,1)S(1)}, bf16[128,1600]{1,0:T(8,128)(2,1)}, u32[]{:S(2)}, u32[]{:S(2)}) collective-permute-start(bf16[128,1600]{1,0:T(8,128)(2,1)S(1)} %bitcast.161), channel_id=1, source_target_pairs={{0,3},{1,2},{2,1},{3,0},{4,7},{5,6},{6,5},{7,4},{8,11},{9,10},{10,... | collective-permute-start | bytes 1228808 | tf_op jit(solution)/shard_map/ppermute | solution.py:483
  84.6 209.7 %collective-permute-start.6 = (bf16[128,1600]{1,0:T(8,128)(2,1)S(1)}, bf16[128,1600]{1,0:T(8,128)(2,1)}, u32[]{:S(2)}, u32[]{:S(2)}) collective-permute-start(bf16[128,1600]{1,0:T(8,128)(2,1)S(1)} %bitcast.162), channel_id=1, source_target_pairs={{0,2},{1,3},{2,0},{3,1},{4,6},{5,7},{6,4},{7,5},{8,10},{9,11},{10,... | collective-permute-start | bytes 1228808 | tf_op jit(solution)/shard_map/ppermute | solution.py:483
  86.6 205.5 %collective-permute-start.5 = (bf16[128,1600]{1,0:T(8,128)(2,1)S(1)}, bf16[128,1600]{1,0:T(8,128)(2,1)}, u32[]{:S(2)}, u32[]{:S(2)}) collective-permute-start(bf16[128,1600]{1,0:T(8,128)(2,1)S(1)} %bitcast.163), channel_id=1, source_target_pairs={{0,1},{1,0},{2,3},{3,2},{4,5},{5,4},{6,7},{7,6},{8,9},{9,8},{10,11... | collective-permute-start | bytes 1228808 | tf_op jit(solution)/shard_map/ppermute | solution.py:483
  88.5 112.7 %collective-permute-start.1 = (bf16[48,1600]{1,0:T(8,128)(2,1)}, bf16[48,1600]{1,0:T(8,128)(2,1)}, u32[]{:S(2)}, u32[]{:S(2)}) collective-permute-start(bf16[48,1600]{1,0:T(8,128)(2,1)} %get-tuple-element.185), channel_id=1, source_target_pairs={{0,3},{1,0},{2,1},{3,2},{4,7},{5,4},{6,5},{7,6},{8,11},{9,8},{10,9... | collective-permute-start | bytes 460808 | tf_op jit(solution)/shard_map/ppermute | solution.py:857
  88.9 117.0 %collective-permute-start = (bf16[48,1600]{1,0:T(8,128)(2,1)}, bf16[48,1600]{1,0:T(8,128)(2,1)}, u32[]{:S(2)}, u32[]{:S(2)}) collective-permute-start(bf16[48,1600]{1,0:T(8,128)(2,1)} %get-tuple-element.186), channel_id=1, source_target_pairs={{0,1},{1,2},{2,3},{3,0},{4,5},{5,6},{6,7},{7,4},{8,9},{9,10},{10,1... | collective-permute-start | bytes 460808 | tf_op jit(solution)/shard_map/ppermute | solution.py:856
  154.8 51.0 %copy-start.33 = (bf16[400,1600]{1,0:T(8,128)(2,1)S(1)}, bf16[400,1600]{1,0:T(8,128)(2,1)}, u32[]{:S(2)}) copy-start(bf16[400,1600]{1,0:T(8,128)(2,1)} %param.24) | copy-start | bytes 3840004
  201.2 102.9 %collective-permute-start.4 = (bf16[400,1600]{1,0:T(8,128)(2,1)}, bf16[400,1600]{1,0:T(8,128)(2,1)}, u32[]{:S(2)}, u32[]{:S(2)}) collective-permute-start(bf16[400,1600]{1,0:T(8,128)(2,1)} %get-tuple-element.158), channel_id=1, source_target_pairs={{0,3},{1,2},{2,1},{3,0},{4,7},{5,6},{6,5},{7,4},{8,11},{9,10},{10,... | collective-permute-start | bytes 3840008 | tf_op jit(solution)/shard_map/ppermute | solution.py:483
  205.9 95.6 %collective-permute-start.3 = (bf16[400,1600]{1,0:T(8,128)(2,1)}, bf16[400,1600]{1,0:T(8,128)(2,1)}, u32[]{:S(2)}, u32[]{:S(2)}) collective-permute-start(bf16[400,1600]{1,0:T(8,128)(2,1)} %get-tuple-element.159), channel_id=1, source_target_pairs={{0,2},{1,3},{2,0},{3,1},{4,6},{5,7},{6,4},{7,5},{8,10},{9,11},{10,... | collective-permute-start | bytes 3840008 | tf_op jit(solution)/shard_map/ppermute | solution.py:483
  208.9 62.9 %copy-start.20 = (bf16[1,128,1600]{2,1,0:T(8,128)(2,1)S(1)}, bf16[1,128,1600]{2,1,0:T(8,128)(2,1)}, u32[]{:S(2)}) copy-start(bf16[1,128,1600]{2,1,0:T(8,128)(2,1)} %copy.60) | copy-start | bytes 1228804
  272.1 100.4 %copy-start.44 = (f32[128]{0:T(128)}, f32[128]{0:T(128)S(1)}, u32[]{:S(2)}) copy-start(f32[128]{0:T(128)S(1)} %broadcast_multiply_fusion.2) | copy-start | bytes 1540
  273.0 99.5 %copy-start.49 = (f32[128]{0:T(128)}, f32[128]{0:T(128)S(1)}, u32[]{:S(2)}) copy-start(f32[128]{0:T(128)S(1)} %fusion.53) | copy-start | bytes 1540
  292.1 8.2 collective-permute-start.2
  312.6 25.0 %slice-start.1 = ((s8[5324800]{0:T(1024)(128)(4,1)}), s8[4194304]{0:T(1024)(128)(4,1)S(1)}, s32[]{:S(2)}) async-start(s8[5324800]{0:T(1024)(128)(4,1)} %bitcast.170), calls=%async_computation.1 | async-start | bytes 8388608
  377.2 32.3 %collective-permute-start.8 = (bf16[400,1600]{1,0:T(8,128)(2,1)}, bf16[400,1600]{1,0:T(8,128)(2,1)}, u32[]{:S(2)}, u32[]{:S(2)}) collective-permute-start(bf16[400,1600]{1,0:T(8,128)(2,1)} %get-tuple-element.155), channel_id=1, source_target_pairs={{0,32},{4,36},{8,40},{12,44},{16,48},{20,52},{24,56},{28,60},{32,6... | collective-permute-start | bytes 3840008 | tf_op jit(solution)/shard_map/ppermute | solution.py:494
  377.2 97.6 %collective-permute-start.10 = (bf16[400,1600]{1,0:T(8,128)(2,1)}, bf16[400,1600]{1,0:T(8,128)(2,1)}, u32[]{:S(2)}, u32[]{:S(2)}) collective-permute-start(bf16[400,1600]{1,0:T(8,128)(2,1)} %get-tuple-element.156), channel_id=1, source_target_pairs={{0,64},{4,68},{8,72},{12,76},{16,80},{20,84},{24,88},{28,92},{32,9... | collective-permute-start | bytes 3840008 | tf_op jit(solution)/shard_map/ppermute | solution.py:494
  379.5 95.3 %collective-permute-start.9 = (bf16[400,1600]{1,0:T(8,128)(2,1)}, bf16[400,1600]{1,0:T(8,128)(2,1)}, u32[]{:S(2)}, u32[]{:S(2)}) collective-permute-start(bf16[400,1600]{1,0:T(8,128)(2,1)} %get-tuple-element.157), channel_id=1, source_target_pairs={{0,96},{4,100},{8,104},{12,108},{16,112},{20,116},{24,120},{28,124... | collective-permute-start | bytes 3840008 | tf_op jit(solution)/shard_map/ppermute | solution.py:494
  405.4 72.6 %collective-permute-start.11 = (bf16[400,1600]{1,0:T(8,128)(2,1)}, bf16[400,1600]{1,0:T(8,128)(2,1)}, u32[]{:S(2)}, u32[]{:S(2)}) collective-permute-start(bf16[400,1600]{1,0:T(8,128)(2,1)} %get-tuple-element.152), channel_id=1, source_target_pairs={{0,8},{4,12},{8,16},{12,20},{16,24},{20,28},{24,0},{28,4},{32,40},... | collective-permute-start | bytes 3840008 | tf_op jit(solution)/shard_map/ppermute | solution.py:494
  405.7 72.3 %collective-permute-start.13 = (bf16[400,1600]{1,0:T(8,128)(2,1)}, bf16[400,1600]{1,0:T(8,128)(2,1)}, u32[]{:S(2)}, u32[]{:S(2)}) collective-permute-start(bf16[400,1600]{1,0:T(8,128)(2,1)} %get-tuple-element.153), channel_id=1, source_target_pairs={{0,16},{4,20},{8,24},{12,28},{16,0},{20,4},{24,8},{28,12},{32,48},... | collective-permute-start | bytes 3840008 | tf_op jit(solution)/shard_map/ppermute | solution.py:494
  409.4 68.6 %collective-permute-start.12 = (bf16[400,1600]{1,0:T(8,128)(2,1)}, bf16[400,1600]{1,0:T(8,128)(2,1)}, u32[]{:S(2)}, u32[]{:S(2)}) collective-permute-start(bf16[400,1600]{1,0:T(8,128)(2,1)} %get-tuple-element.154), channel_id=1, source_target_pairs={{0,24},{4,28},{8,0},{12,4},{16,8},{20,12},{24,16},{28,20},{32,56},... | collective-permute-start | bytes 3840008 | tf_op jit(solution)/shard_map/ppermute | solution.py:494
  481.2 74.8 %copy-start.3 = (bf16[32,64,128]{2,1,0:T(8,128)(2,1)S(1)}, bf16[32,64,128]{2,1,0:T(8,128)(2,1)}, u32[]{:S(2)}) copy-start(bf16[32,64,128]{2,1,0:T(8,128)(2,1)} %exchange_ctx.6.up_ref) | copy-start | bytes 1572868
  481.2 74.8 %copy-start.5 = (bf16[8,512,64]{2,1,0:T(8,128)(2,1)S(1)}, bf16[8,512,64]{2,1,0:T(8,128)(2,1)}, u32[]{:S(2)}) copy-start(bf16[8,512,64]{2,1,0:T(8,128)(2,1)} %copy-done.4) | copy-start | bytes 1572868
  481.2 74.8 %copy-start.7 = (bf16[8,512,64]{2,1,0:T(8,128)(2,1)S(1)}, bf16[8,512,64]{2,1,0:T(8,128)(2,1)}, u32[]{:S(2)}) copy-start(bf16[8,512,64]{2,1,0:T(8,128)(2,1)} %copy-done.6) | copy-start | bytes 1572868
  481.2 74.8 %copy-start.9 = (f32[8,64,512]{2,1,0:T(8,128)S(1)}, f32[8,64,512]{2,1,0:T(8,128)}, u32[]{:S(2)}) copy-start(f32[8,64,512]{2,1,0:T(8,128)} %copy-done.8) | copy-start | bytes 3145732
  481.3 74.8 %copy-start.12 = (bf16[8,64,512]{2,1,0:T(8,128)(2,1)S(1)}, bf16[8,64,512]{2,1,0:T(8,128)(2,1)}, u32[]{:S(2)}) copy-start(bf16[8,64,512]{2,1,0:T(8,128)(2,1)} %copy-done.11) | copy-start | bytes 1572868
  481.3 74.8 %copy-start.14 = (bf16[8,64,512]{2,1,0:T(8,128)(2,1)S(1)}, bf16[8,64,512]{2,1,0:T(8,128)(2,1)}, u32[]{:S(2)}) copy-start(bf16[8,64,512]{2,1,0:T(8,128)(2,1)} %copy-done.13) | copy-start | bytes 1572868
  547.4 254.4 %collective-permute-start.16 = (bf16[400,1600]{1,0:T(8,128)(2,1)S(1)}, bf16[400,1600]{1,0:T(8,128)(2,1)S(1)}, u32[]{:S(2)}, u32[]{:S(2)}) collective-permute-start(bf16[400,1600]{1,0:T(8,128)(2,1)S(1)} %get-tuple-element.79.refs_0_), channel_id=1, source_target_pairs={{0,64},{4,68},{8,72},{12,76},{16,80},{20,84},{24,88},{28,92},{32,9... | collective-permute-start | bytes 3840008 | tf_op jit(solution)/shard_map/ppermute | solution.py:494
  551.2 252.9 %collective-permute-start.15 = (bf16[400,1600]{1,0:T(8,128)(2,1)S(1)}, bf16[400,1600]{1,0:T(8,128)(2,1)}, u32[]{:S(2)}, u32[]{:S(2)}) collective-permute-start(bf16[400,1600]{1,0:T(8,128)(2,1)S(1)} %get-tuple-element.79.refs_0_), channel_id=1, source_target_pairs={{0,96},{4,100},{8,104},{12,108},{16,112},{20,116},{24,120},{28,124... | collective-permute-start | bytes 3840008 | tf_op jit(solution)/shard_map/ppermute | solution.py:494
  551.2 252.9 %collective-permute-start.14 = (bf16[400,1600]{1,0:T(8,128)(2,1)S(1)}, bf16[400,1600]{1,0:T(8,128)(2,1)}, u32[]{:S(2)}, u32[]{:S(2)}) collective-permute-start(bf16[400,1600]{1,0:T(8,128)(2,1)S(1)} %get-tuple-element.79.refs_0_), channel_id=1, source_target_pairs={{0,32},{4,36},{8,40},{12,44},{16,48},{20,52},{24,56},{28,60},{32,6... | collective-permute-start | bytes 3840008 | tf_op jit(solution)/shard_map/ppermute | solution.py:494
  552.7 263.5 %collective-permute-start.19 = (bf16[400,1600]{1,0:T(8,128)(2,1)}, bf16[400,1600]{1,0:T(8,128)(2,1)}, u32[]{:S(2)}, u32[]{:S(2)}) collective-permute-start(bf16[400,1600]{1,0:T(8,128)(2,1)} %get-tuple-element.80.refs_0_), channel_id=1, source_target_pairs={{0,16},{4,20},{8,24},{12,28},{16,0},{20,4},{24,8},{28,12},{32,48},... | collective-permute-start | bytes 3840008 | tf_op jit(solution)/shard_map/ppermute | solution.py:494
  553.5 262.6 %collective-permute-start.18 = (bf16[400,1600]{1,0:T(8,128)(2,1)}, bf16[400,1600]{1,0:T(8,128)(2,1)}, u32[]{:S(2)}, u32[]{:S(2)}) collective-permute-start(bf16[400,1600]{1,0:T(8,128)(2,1)} %get-tuple-element.80.refs_0_), channel_id=1, source_target_pairs={{0,24},{4,28},{8,0},{12,4},{16,8},{20,12},{24,16},{28,20},{32,56},... | collective-permute-start | bytes 3840008 | tf_op jit(solution)/shard_map/ppermute | solution.py:494
  801.7 30.9 %collective-permute-start.17 = (bf16[400,1600]{1,0:T(8,128)(2,1)}, bf16[400,1600]{1,0:T(8,128)(2,1)S(1)}, u32[]{:S(2)}, u32[]{:S(2)}) collective-permute-start(bf16[400,1600]{1,0:T(8,128)(2,1)} %get-tuple-element.80.refs_0_), channel_id=1, source_target_pairs={{0,8},{4,12},{8,16},{12,20},{16,24},{20,28},{24,0},{28,4},{32,40},... | collective-permute-start | bytes 3840008 | tf_op jit(solution)/shard_map/ppermute | solution.py:494
  (52 other events, 334.7 us)

commit v3 on v1

v3 whole, which is shorter than its diff:
```python
import math

import jax
import jax.numpy as jnp
from jax import lax
from jax.experimental import pallas as pl
from jax.experimental.pallas import tpu as pltpu
from jax.sharding import PartitionSpec as P

HEADS = 25
HEAD_DIM = 64
GROUP = 7
SPAN = GROUP * HEAD_DIM
EPS = 1e-05
MESH = pl.DeviceIdType.MESH


def cost(micros):
    return pl.CostEstimate(flops=int(micros * 1e9), bytes_accessed=int(micros * 1e6), transcendentals=0)
NEG = -1e30
LOG2E = 1.4426950408889634

def layer_norm(values, gain_row, shift_row):
    centered = values - jnp.mean(values, axis=-1, keepdims=True)
    variance = jnp.mean(centered * centered, axis=-1, keepdims=True)
    return centered * lax.rsqrt(variance + EPS) * gain_row + shift_row


def gelu_tanh(values):
    return jax.nn.gelu(values, approximate=True)


def dot(left, right, left_dim=1, right_dim=0):
    return lax.dot_general(
        left, right, (((left_dim,), (right_dim,)), ((), ())), preferred_element_type=jnp.float32
    )


def greet(peers):
    barrier = pltpu.get_barrier_semaphore()
    for peer in peers:
        pl.semaphore_signal(barrier, inc=1, device_id=peer, device_id_type=MESH)
    pl.semaphore_wait(barrier, len(peers))


def prologue(arrays, columns, collective):
    count = len(arrays)
    pieces = 5
    extent = columns.shape[1] // pieces

    def kernel(*refs):
        sources, (blocks,) = refs[:count], refs[count : count + 1]
        targets, (filled,) = refs[count + 1 : 2 * count + 1], refs[2 * count + 1 : 2 * count + 2]
        send, receive, local, cross_send, cross_receive, near_send, near_receive = refs[2 * count + 2 :]
        ctx, wt = lax.axis_index("ctx"), lax.axis_index("wt")
        low = lax.rem(ctx, 2)
        near, far, beside = (ctx, wt ^ 1), (ctx, wt ^ 2), (ctx ^ 1, wt)
        goes, comes = wt ^ (2 + low), wt ^ (3 - low)
        greet((near, far, beside, (ctx ^ 1, goes), (ctx ^ 1, comes)))

        def move(item, step, source, slot, peer):
            return pltpu.make_async_remote_copy(
                source, targets[item].at[slot], send.at[item, step], receive.at[item, step],
                device_id=peer, device_id_type=MESH,
            )

        def cross(index):
            span = pl.ds(index * extent, extent)
            return pltpu.make_async_remote_copy(
                blocks.at[goes, span], filled.at[wt, span], cross_send.at[0, index], cross_receive.at[0, index],
                device_id=(ctx ^ 1, goes), device_id_type=MESH,
            )

        def crossed(index):
            span = pl.ds(index * extent, extent)
            return pltpu.make_async_remote_copy(
                filled.at[comes, span], filled.at[comes, span], cross_send.at[0, index], cross_receive.at[0, index],
                device_id=(ctx ^ 1, goes), device_id_type=MESH,
            )

        def onward(index):
            span = pl.ds(index * extent, extent)
            return pltpu.make_async_remote_copy(
                filled.at[comes, span], filled.at[comes, span], cross_send.at[1, index], cross_receive.at[1, index],
                device_id=beside, device_id_type=MESH,
            )

        firsts = [move(item, 0, sources[item], wt, far) for item in range(count)]
        for copy in firsts:
            copy.start()
        crossings = [cross(index) for index in range(pieces)]
        for copy in crossings:
            copy.start()
        seconds = [move(item, 1, sources[item], wt, near) for item in range(count)]
        own = [
            pltpu.make_async_copy(sources[item], targets[item].at[wt], local.at[item])
            for item in range(count)
        ]
        own.append(pltpu.make_async_copy(blocks.at[wt], filled.at[wt], local.at[count]))
        pair = pltpu.make_async_remote_copy(
            blocks.at[wt ^ 1], filled.at[wt], near_send, near_receive, device_id=near, device_id_type=MESH
        )
        for copy in seconds + own + [pair]:
            copy.start()
        thirds = []
        for item in range(count):
            firsts[item].wait_recv()
            copy = move(item, 2, targets[item].at[wt ^ 2], wt ^ 2, near)
            copy.start()
            thirds.append(copy)
        onwards = []
        for index in range(pieces):
            crossed(index).wait_recv()
            copy = onward(index)
            copy.start()
            onwards.append(copy)
        for copy in firsts + crossings:
            copy.wait_send()
        for copy in seconds + thirds + own + [pair] + onwards:
            copy.wait()

    hbm = pl.BlockSpec(memory_space=pl.ANY)
    return pl.pallas_call(
        kernel,
        out_shape=tuple(jax.ShapeDtypeStruct((4,) + member.shape, member.dtype) for member in arrays)
        + (jax.ShapeDtypeStruct(columns.shape, columns.dtype),),
        in_specs=[hbm] * (count + 1),
        out_specs=(hbm,) * (count + 1),
        scratch_shapes=[
            pltpu.SemaphoreType.DMA((count, 3)),
            pltpu.SemaphoreType.DMA((count, 3)),
            pltpu.SemaphoreType.DMA((count + 1,)),
            pltpu.SemaphoreType.DMA((2, pieces)),
            pltpu.SemaphoreType.DMA((2, pieces)),
            pltpu.SemaphoreType.DMA,
            pltpu.SemaphoreType.DMA,
        ],
        compiler_params=pltpu.CompilerParams(collective_id=collective, has_side_effects=True),
        name="prologue",
    )(*arrays, columns)


def exchange(blocks, axis, collective):
    count = blocks.shape[0]

    def kernel(source, target, send, receive, local):
        ctx, wt = lax.axis_index("ctx"), lax.axis_index("wt")
        own = ctx if axis == "ctx" else wt

        def peer(step):
            other = lax.rem(own + step, count)
            return other, ((other, wt) if axis == "ctx" else (ctx, other))

        barrier = pltpu.get_barrier_semaphore()

        def signal(step, carry):
            pl.semaphore_signal(barrier, inc=1, device_id=peer(step)[1], device_id_type=MESH)
            return carry

        lax.fori_loop(1, count, signal, 0)
        pl.semaphore_wait(barrier, count - 1)

        def move(step):
            other, device = peer(step)
            return pltpu.make_async_remote_copy(
                source.at[other], target.at[own], send.at[step], receive.at[step],
                device_id=device, device_id_type=MESH,
            )

        def begin(step, carry):
            move(step).start()
            return carry

        def finish(step, carry):
            move(step).wait()
            return carry

        lax.fori_loop(1, count, begin, 0)
        keep = pltpu.make_async_copy(source.at[own], target.at[own], local)
        keep.start()
        keep.wait()
        lax.fori_loop(1, count, finish, 0)

    hbm = pl.BlockSpec(memory_space=pl.ANY)
    return pl.pallas_call(
        kernel,
        out_shape=jax.ShapeDtypeStruct(blocks.shape, blocks.dtype),
        in_specs=[hbm],
        out_specs=hbm,
        scratch_shapes=[
            pltpu.SemaphoreType.DMA((count,)),
            pltpu.SemaphoreType.DMA((count,)),
            pltpu.SemaphoreType.DMA,
        ],
        compiler_params=pltpu.CompilerParams(collective_id=collective, has_side_effects=True),
        name="exchange_" + axis,
    )(blocks)


def remote(source, target, send, receive, device):
    return pltpu.make_async_remote_copy(source, target, send, receive, device_id=device, device_id_type=MESH)


def greet_ctx(ctx, wt, others):
    barrier = pltpu.get_barrier_semaphore()

    def signal(step, carry):
        pl.semaphore_signal(barrier, inc=1, device_id=((ctx + step) % 32, wt), device_id_type=MESH)
        return carry

    lax.fori_loop(1, 32, signal, 0)
    for other in others:
        pl.semaphore_signal(barrier, inc=1, device_id=other, device_id_type=MESH)
    pl.semaphore_wait(barrier, 31 + len(others))


class RingSum:
    def __init__(self, source, rows, place, at, relay, arrive, send, receive):
        self.source, self.rows, self.place = source, rows, place
        self.relay, self.arrive, self.send, self.receive = relay, arrive, send, receive
        self.up, self.down = (place + 1) % 4, (place + 3) % 4
        self.to = (at(self.up), at(self.down))
        cut = (rows // 32) * 16 + 16
        self.parts = ((0, cut), (cut, rows - cut))

    def block(self, place, part):
        start, extent = self.parts[part]
        return pl.ds(pl.multiple_of(place * self.rows + start, 16), extent)

    def copy(self, index):
        first, second = self.parts
        opposite = (self.place + 2) % 4
        ends = (
            (self.source.at[self.block(opposite, 0)], self.relay.at[0, pl.ds(0, first[1])], 0),
            (self.source.at[self.block(opposite, 1)], self.relay.at[1, pl.ds(0, second[1])], 1),
            (self.source.at[self.block(self.up, 1)], self.arrive.at[0, pl.ds(*second)], 0),
            (self.source.at[self.block(self.down, 0)], self.arrive.at[1, pl.ds(*first)], 1),
            (self.source.at[self.block(self.up, 0)], self.arrive.at[0, pl.ds(*first)], 0),
            (self.source.at[self.block(self.down, 1)], self.arrive.at[1, pl.ds(*second)], 1),
        )
        source, target, way = ends[index]
        return remote(source, target, self.send.at[index], self.receive.at[index], self.to[way])

    def begin(self):
        for index in range(4):
            self.copy(index).start()

    def pass_on(self):
        for way in range(2):
            self.copy(way).wait_recv()
            extent = self.parts[way][1]
            mine = self.block(self.up if way == 0 else self.down, way)
            total = self.source[mine].astype(jnp.float32) + self.relay[way, :extent].astype(jnp.float32)
            self.source[mine] = total.astype(self.source.dtype)
            self.copy(4 + way).start()

    def finish(self):
        for index in (2, 3, 4, 5):
            self.copy(index).wait_recv()
        mine = pl.ds(pl.multiple_of(self.place * self.rows, 16), self.rows)
        total = self.source[mine].astype(jnp.float32)
        return total + self.arrive[0].astype(jnp.float32) + self.arrive[1].astype(jnp.float32)

    def drain(self):
        for index in range(6):
            self.copy(index).wait_send()


class RingSpread:
    def __init__(self, target, place, at, send, receive):
        self.target, self.place, self.send, self.receive = target, place, send, receive
        self.up, self.down = (place + 1) % 4, (place + 3) % 4
        self.to = (at(self.up), at(self.down))
        rows = target.shape[1]
        cut = (rows // 32) * 16 + 16
        self.parts = (pl.ds(0, cut), pl.ds(cut, rows - cut))

    def whole(self, way, slot):
        return remote(self.target.at[slot], self.target.at[slot], self.send.at[way], self.receive.at[way], self.to[way])

    def half(self, way, slot):
        piece = self.target.at[slot, self.parts[way]]
        return remote(piece, piece, self.send.at[2 + way], self.receive.at[2 + way], self.to[way])

    def begin(self):
        self.whole(0, self.place).start()
        self.whole(1, self.place).start()

    def pass_on(self):
        self.whole(0, self.down).wait_recv()
        self.half(0, self.down).start()
        self.whole(1, self.up).wait_recv()
        self.half(1, self.up).start()

    def finish(self):
        opposite = (self.place + 2) % 4
        self.half(0, opposite).wait_recv()
        self.half(1, opposite).wait_recv()

    def drain(self):
        for way in range(2):
            self.whole(way, self.place).wait_send()
            self.half(way, self.down if way == 0 else self.up).wait_send()


class Inner:
    def __init__(self, window, inner, place, at, ctx, wt, crosses, bufs, sems):
        self.window, self.inner, self.place, self.at, self.ctx, self.wt, self.crosses = window, inner, place, at, ctx, wt, crosses
        self.came, self.mid, self.pair, self.lanes_out, self.lanes_in, self.all = bufs
        self.inner_send, self.inner_receive, self.lane_send, self.lane_receive, self.all_send, self.all_receive, self.pair_sems = sems
        self.stride = (window.shape[0] - inner) // 3
        self.share = window.shape[1] // 4

    def rows(self, place):
        return pl.ds(pl.multiple_of(self.stride * place, 16), self.inner)

    def outward(self, step):
        other = (self.place + step) % 4
        return remote(
            self.window.at[self.rows(other)], self.came.at[step - 1],
            self.inner_send.at[step - 1], self.inner_receive.at[step - 1], self.at(other),
        )

    def beside(self):
        return remote(self.mid, self.pair, self.pair_sems.at[0], self.pair_sems.at[1], (self.ctx ^ 1, self.wt))

    def lane(self, step):
        return remote(
            self.lanes_out.at[self.wt ^ step], self.lanes_in.at[self.wt],
            self.lane_send.at[step - 1], self.lane_receive.at[step - 1], (self.ctx, self.wt ^ step),
        )

    def around(self, step):
        return remote(
            self.pair, self.all.at[self.place],
            self.all_send.at[step - 1], self.all_receive.at[step - 1], self.at((self.place + step) % 4),
        )

    def begin(self):
        for step in (1, 3, 2):
            self.outward(step).start()

    def add_inner(self):
        for step in (1, 3, 2):
            self.outward(step).wait_recv()
        total = self.window[self.rows(self.place)].astype(jnp.float32)
        for step in range(3):
            total += self.came[step].astype(jnp.float32)
        self.mid[...] = total.astype(self.mid.dtype)
        self.beside().start()

    def add_beside(self):
        self.beside().wait_recv()
        total = (self.mid[...].astype(jnp.float32) + self.pair[...].astype(jnp.float32)).astype(self.mid.dtype)
        self.pair[...] = total
        if self.crosses is False:
            self.spread()
            return
        for owner in range(4):
            self.lanes_out[owner] = total[:, owner * self.share : (owner + 1) * self.share]
        for step in (2, 3, 1):
            self.lane(step).start()
        self.lanes_in[self.wt] = self.lanes_out[self.wt]

    def spread(self):
        for step in (1, 3, 2):
            self.around(step).start()
        self.all[self.place] = self.pair[...]

    def collect(self):
        if self.crosses is False:
            return
        for step in (1, 2, 3):
            self.lane(step).wait_recv()
        for sender in range(4):
            span = slice(sender * self.share, (sender + 1) * self.share)
            part = self.lanes_in[sender]
            if self.crosses is not True:
                part = jnp.where(self.crosses, part, self.pair[:, span])
            self.pair[:, span] = part
        self.spread()

    def fill(self):
        for step in (1, 2, 3):
            self.outward(step).wait_send()
            self.around(step).wait_recv()
        for place in range(4):
            start = self.stride * place
            self.window[start : start + self.inner] = self.all[place]

    def drain(self):
        self.beside().wait_send()
        for step in (1, 2, 3):
            self.around(step).wait_send()
            if self.crosses is not False:
                self.lane(step).wait_send()


def inner_scratch(inner, features):
    low = jnp.bfloat16
    share = features // 4
    return [
        pltpu.VMEM((2, 3, inner, features), low),
        pltpu.VMEM((2, inner, features), low),
        pltpu.VMEM((2, inner, features), low),
        pltpu.VMEM((2, 4, inner, share), low),
        pltpu.VMEM((2, 4, inner, share), low),
        pltpu.VMEM((2, 4, inner, features), low),
    ] + [pltpu.SemaphoreType.DMA((2, 3))] * 6 + [pltpu.SemaphoreType.DMA((2, 2))]


def inners(windows, inner, y, z, at_y, at_z, ctx, wt, crosses, scratch):
    pick = lambda half: [ref.at[half] for ref in scratch]
    return [
        Inner(windows[0], inner, z, at_z, ctx, wt, crosses[0], pick(0)[:6], pick(0)[6:]),
        Inner(windows[1], inner, y, at_y, ctx, wt, crosses[1], pick(1)[:6], pick(1)[6:]),
    ]


def attend(received, inverse, place, placed_out, tokens, small, pieces, cotangent, collective):
    parts, wide, rows = received.shape
    dim = wide // 3
    features = tokens.shape[1]
    block = math.gcd(512, parts * rows)
    per = block // rows
    count = parts // per
    chunks = 5
    extent = pieces.shape[1] // chunks
    low = jnp.bfloat16
    hold, off = place // per, place % per

    def kernel(
        inverse_ref, hold_ref, off_ref, in_ref, weight_ref, token_ref, small_ref, pieces_ref, cot_ref,
        q_ref, kt_ref, k_ref, v_ref, att_ref, lse_ref, stacked_ref, middle_ref, all_ref, fc_ref, all_cot_ref,
        vt_ref, blocks_ref, came_ref, turned_ref, terms_ref, bufs,
        head_send, head_receive, term_send, term_receive, all_send, all_receive,
        cross_send, cross_receive, cot_send, cot_receive, near_sems, local_sems,
    ):
        ctx, wt = lax.axis_index("ctx"), lax.axis_index("wt")
        low_x = ctx % 2
        near, far, beside = (ctx, wt ^ 1), (ctx, wt ^ 2), (ctx ^ 1, wt)
        goes, comes = wt ^ (2 + low_x), wt ^ (3 - low_x)
        greet_ctx(ctx, wt, (near, far, (ctx ^ 1, goes), (ctx ^ 1, comes)))

        def cross(index, source, slot):
            span = pl.ds(index * extent, extent)
            return remote(
                source.at[slot, span], fc_ref.at[wt, span], cross_send.at[0, index], cross_receive.at[0, index], (ctx ^ 1, goes)
            )

        def onward(index):
            piece = fc_ref.at[comes, pl.ds(index * extent, extent)]
            return remote(piece, piece, cross_send.at[1, index], cross_receive.at[1, index], beside)

        def upstream(step, source, slot, peer):
            return remote(source, all_cot_ref.at[slot], cot_send.at[step], cot_receive.at[step], peer)

        pair = remote(pieces_ref.at[wt ^ 1], fc_ref.at[wt], near_sems.at[0], near_sems.at[1], near)
        own = (
            pltpu.make_async_copy(pieces_ref.at[wt], fc_ref.at[wt], local_sems.at[0]),
            pltpu.make_async_copy(cot_ref, all_cot_ref.at[wt], local_sems.at[1]),
        )
        for index in range(chunks):
            cross(index, pieces_ref, goes).start()
        upstream(0, cot_ref, wt, far).start()
        upstream(1, cot_ref, wt, near).start()
        pair.start()
        for copy in own:
            copy.start()

        def arrange(index, carry):
            for sub in range(per):
                piece = in_ref[inverse_ref[index * per + sub]]
                lanes = pl.ds(sub * rows, rows)
                q_ref[index, :, lanes] = piece[:dim]
                kt_ref[index, :, lanes] = piece[dim : 2 * dim]
                vt_ref[index, :, lanes] = piece[2 * dim :]
                k_ref[index, lanes, :] = piece[dim : 2 * dim].T
                v_ref[index, lanes, :] = piece[2 * dim :].T
            return carry

        lax.fori_loop(0, count, arrange, 0)
        row = lax.broadcasted_iota(jnp.int32, (block, block), 0)
        col = lax.broadcasted_iota(jnp.int32, (block, block), 1)
        factor = LOG2E * dim**-0.5

        def step(qi, kj, carry, diagonal):
            peak, mass, total = carry
            scores = jnp.dot(k_ref[kj], q_ref[qi], preferred_element_type=jnp.float32) * factor
            if diagonal:
                scores = jnp.where(row <= col, scores, NEG)
            new_peak = jnp.maximum(peak, jnp.max(scores, axis=0, keepdims=True))
            weights = jnp.exp2(scores - new_peak)
            shrink = jnp.exp2(peak - new_peak)
            mass = mass * shrink + jnp.sum(weights, axis=0, keepdims=True)
            total = total * shrink + jnp.dot(vt_ref[kj], weights.astype(low), preferred_element_type=jnp.float32)
            return (new_peak, mass, total)

        def query_block(qi, carry):
            start = (
                jnp.full((1, block), NEG, jnp.float32),
                jnp.zeros((1, block), jnp.float32),
                jnp.zeros((dim, block), jnp.float32),
            )
            state = lax.fori_loop(0, qi, lambda kj, cur: step(qi, kj, cur, False), start)
            peak, mass, total = step(qi, qi, state, True)
            att_ref[qi] = total / mass
            lse_ref[qi] = peak + jnp.log2(mass)
            return carry

        lax.fori_loop(0, count, query_block, 0)

        def to_owner(index):
            return remote(blocks_ref.at[index], came_ref.at[ctx], head_send.at[index], head_receive.at[ctx], (index, wt))

        def give_back(index, carry):
            whole = att_ref[hold_ref[index]]
            picked = whole[:, :rows]
            for sub in range(1, per):
                picked = jnp.where(off_ref[index] == sub, whole[:, sub * rows : (sub + 1) * rows], picked)
            blocks_ref[index] = picked.astype(low)

            @pl.when(index != ctx)
            def _():
                to_owner(index).start()

            @pl.when(index == ctx)
            def _():
                came_ref[index] = blocks_ref[index]

            return carry

        @pl.when(ctx < 4 * GROUP)
        def _():
            lax.fori_loop(0, parts, give_back, 0)

        for index in range(chunks):
            cross(index, pieces_ref, goes).wait_recv()
            onward(index).start()
        upstream(0, cot_ref, wt ^ 2, far).wait_recv()
        upstream(2, all_cot_ref.at[wt ^ 2], wt ^ 2, near).start()

        def owner_here(source, carry):
            @pl.when(source != ctx)
            def _():
                remote(
                    blocks_ref.at[0], came_ref.at[source], head_send.at[0], head_receive.at[source], (source, wt)
                ).wait_recv()

            return carry

        lax.fori_loop(0, 4 * GROUP, owner_here, 0)

        def make_terms(sequence):
            for head in range(GROUP):
                turned_ref[head * dim : (head + 1) * dim] = came_ref[sequence * GROUP + head]
            stacked_ref[sequence] = turned_ref[...].T
            terms_ref[...] = jnp.dot(stacked_ref[sequence], weight_ref[...], preferred_element_type=jnp.float32)

        def term(index, source, target, peer):
            return remote(bufs.at[source], bufs.at[target], term_send.at[index], term_receive.at[index], peer)

        make_terms(wt ^ 3)
        bufs[0] = terms_ref[...].astype(low)
        term(0, 0, 3, near).start()
        make_terms(wt ^ 1)
        bufs[1] = terms_ref[...].astype(low)
        term(1, 1, 4, near).start()
        make_terms(wt ^ 2)
        term(0, 0, 3, near).wait_recv()
        bufs[2] = (terms_ref[...] + bufs[3].astype(jnp.float32)).astype(low)
        term(2, 2, 5, far).start()
        make_terms(wt)
        middle_ref[...] = token_ref[...].astype(jnp.float32) + terms_ref[...] + small_ref[0:1]
        term(1, 1, 4, near).wait_recv()
        middle_ref[...] += bufs[4].astype(jnp.float32)
        term(2, 2, 5, far).wait_recv()
        middle_ref[...] += bufs[5].astype(jnp.float32)
        all_ref[wt] = layer_norm(middle_ref[...], small_ref[1:2], small_ref[2:3]).astype(low)

        def normed(step, slot, peer):
            return remote(all_ref.at[slot], all_ref.at[slot], all_send.at[step], all_receive.at[step], peer)

        normed(0, wt, far).start()
        normed(1, wt, near).start()
        normed(0, wt ^ 2, far).wait_recv()
        normed(2, wt ^ 2, near).start()
        normed(1, wt ^ 1, near).wait_recv()
        normed(2, wt ^ 3, near).wait_recv()
        normed(0, wt, far).wait_send()
        normed(1, wt, near).wait_send()
        normed(2, wt ^ 2, near).wait_send()
        term(0, 0, 3, near).wait_send()
        term(1, 1, 4, near).wait_send()
        term(2, 2, 5, far).wait_send()
        upstream(1, cot_ref, wt ^ 1, near).wait_recv()
        upstream(2, all_cot_ref.at[wt ^ 2], wt ^ 3, near).wait_recv()
        upstream(0, cot_ref, wt, far).wait_send()
        upstream(1, cot_ref, wt, near).wait_send()
        upstream(2, all_cot_ref.at[wt ^ 2], wt ^ 2, near).wait_send()
        pair.wait()
        for copy in own:
            copy.wait()
        for index in range(chunks):
            cross(index, pieces_ref, goes).wait_send()
            onward(index).wait()

        def sent(index, carry):
            @pl.when(index != ctx)
            def _():
                to_owner(index).wait_send()

            return carry

        @pl.when(ctx < 4 * GROUP)
        def _():
            lax.fori_loop(0, parts, sent, 0)

    smem = pl.BlockSpec(memory_space=pltpu.SMEM)
    vmem = pl.BlockSpec(memory_space=pltpu.VMEM)
    hbm = pl.BlockSpec(memory_space=pl.ANY)
    lane_first = jax.ShapeDtypeStruct((count, dim, block), low)
    row_first = jax.ShapeDtypeStruct((count, block, dim), low)
    return pl.pallas_call(
        kernel,
        out_shape=(
            lane_first,
            lane_first,
            row_first,
            row_first,
            jax.ShapeDtypeStruct((count, dim, block), jnp.float32),
            jax.ShapeDtypeStruct((count, 1, block), jnp.float32),
            jax.ShapeDtypeStruct((4, rows, SPAN), low),
            jax.ShapeDtypeStruct((rows, features), jnp.float32),
            jax.ShapeDtypeStruct((4, rows, features), low),
            jax.ShapeDtypeStruct(pieces.shape, low),
            jax.ShapeDtypeStruct((4, rows, features), low),
        ),
        in_specs=[smem] * 3 + [vmem] * 4 + [hbm] * 2,
        out_specs=(vmem,) * 9 + (hbm,) * 2,
        scratch_shapes=[
            pltpu.VMEM((count, dim, block), low),
            pltpu.VMEM((parts, dim, rows), low),
            pltpu.VMEM((parts, dim, rows), low),
            pltpu.VMEM((SPAN, rows), low),
            pltpu.VMEM((rows, features), jnp.float32),
            pltpu.VMEM((6, rows, features), low),
            pltpu.SemaphoreType.DMA((parts,)),
            pltpu.SemaphoreType.DMA((parts,)),
            pltpu.SemaphoreType.DMA((3,)),
            pltpu.SemaphoreType.DMA((3,)),
            pltpu.SemaphoreType.DMA((3,)),
            pltpu.SemaphoreType.DMA((3,)),
            pltpu.SemaphoreType.DMA((2, chunks)),
            pltpu.SemaphoreType.DMA((2, chunks)),
            pltpu.SemaphoreType.DMA((3,)),
            pltpu.SemaphoreType.DMA((3,)),
            pltpu.SemaphoreType.DMA((2,)),
            pltpu.SemaphoreType.DMA((2,)),
        ],
        compiler_params=pltpu.CompilerParams(
            collective_id=collective, has_side_effects=True, vmem_limit_bytes=56 * 2**20
        ),
        name="attend",
    )(inverse, hold, off, received, placed_out, tokens, small, pieces, cotangent)


def feed_back(terms_out, terms_two, grad_fc, grad_proj, middle, gain, cotangent, wide_out, collective):
    rows, features = middle.shape
    block = grad_fc.shape[0] // 4
    low = jnp.bfloat16

    def kernel(
        out_terms, two_terms, fc_ref, proj_ref, middle_ref, gain_ref, cot_ref, wide_ref,
        out_ref, middle_grad_ref, vectors_ref, all_ref, up_ref, fc_out, proj_out,
        fc_work, proj_work, bufs, relay, arrive, blocks_ref,
        ring_send, ring_receive, term_send, term_receive, all_send, all_receive, head_send, head_receive, fetch,
    ):
        ctx, wt = lax.axis_index("ctx"), lax.axis_index("wt")
        y, z, low_x = ctx // 8, ctx // 2 % 4, ctx % 2
        at_y = lambda place: (place * 8 + z * 2 + low_x, wt)
        at_z = lambda place: (y * 8 + place * 2 + low_x, wt)
        near, far = (ctx, wt ^ 1), (ctx, wt ^ 2)
        loads = [
            pltpu.make_async_copy(source, target, fetch.at[index])
            for index, (source, target) in enumerate(((fc_ref, fc_work), (proj_ref, proj_work)))
        ]
        for load in loads:
            load.start()
        greet_ctx(ctx, wt, (near, far))

        def term(item, step, source, target, peer):
            return remote(
                bufs.at[item, source], bufs.at[item, target], term_send.at[item, step], term_receive.at[item, step], peer
            )

        terms = (two_terms, out_terms)

        def begin_terms(item):
            bufs[item, 0] = terms[item][wt ^ 3].astype(low)
            term(item, 0, 0, 3, near).start()
            bufs[item, 1] = terms[item][wt ^ 1].astype(low)
            term(item, 1, 1, 4, near).start()

        def pass_terms(item):
            term(item, 0, 0, 3, near).wait_recv()
            bufs[item, 2] = (terms[item][wt ^ 2] + bufs[item, 3].astype(jnp.float32)).astype(low)
            term(item, 2, 2, 5, far).start()

        def end_terms(item):
            term(item, 1, 1, 4, near).wait_recv()
            total = terms[item][wt] + bufs[item, 4].astype(jnp.float32)
            term(item, 2, 2, 5, far).wait_recv()
            return total + bufs[item, 5].astype(jnp.float32)

        begin_terms(0)
        rings = [
            RingSum(fc_work, block, y, at_y, relay.at[0], arrive.at[0], ring_send.at[0], ring_receive.at[0]),
            RingSum(proj_work, block, z, at_z, relay.at[1], arrive.at[1], ring_send.at[1], ring_receive.at[1]),
        ]
        for load, ring in zip(loads, rings):
            load.wait()
            ring.begin()
        pass_terms(0)
        begin_terms(1)
        pass_terms(1)
        grad = end_terms(0)
        values = middle_ref[...]
        centered = values - jnp.mean(values, axis=-1, keepdims=True)
        scale = lax.rsqrt(jnp.mean(centered * centered, axis=-1, keepdims=True) + EPS)
        normed = centered * scale
        vectors_ref[0:1] = jnp.sum(grad * normed, axis=0, keepdims=True)
        vectors_ref[1:2] = jnp.sum(grad, axis=0, keepdims=True)
        weighted = grad * gain_ref[...]
        part = weighted - jnp.mean(weighted, axis=-1, keepdims=True)
        part = part - normed * jnp.mean(weighted * normed, axis=-1, keepdims=True)
        middle_grad = cot_ref[...].astype(jnp.float32) + scale * part
        middle_grad_ref[...] = middle_grad
        all_ref[wt] = middle_grad.astype(low)

        def branch(step, slot, peer):
            return remote(all_ref.at[slot], all_ref.at[slot], all_send.at[step], all_receive.at[step], peer)

        branch(0, wt, far).start()
        branch(1, wt, near).start()

        def to_head(index, other):
            return remote(
                blocks_ref.at[index], up_ref.at[ctx], head_send.at[index], head_receive.at[ctx], (other, wt)
            )

        def heads(turn, sequence):
            grads = lax.dot_general(
                wide_ref[...], all_ref[sequence], (((1,), (1,)), ((), ())), preferred_element_type=jnp.float32
            ).astype(low)
            for head in range(GROUP):
                index, other = turn * GROUP + head, sequence * GROUP + head
                blocks_ref[index] = grads[head * HEAD_DIM : (head + 1) * HEAD_DIM]

                @pl.when(other != ctx)
                def _():
                    to_head(index, other).start()

                @pl.when(other == ctx)
                def _():
                    up_ref[other] = blocks_ref[index]

        heads(0, wt)
        branch(0, wt ^ 2, far).wait_recv()
        branch(2, wt ^ 2, near).start()
        branch(1, wt ^ 1, near).wait_recv()
        heads(1, wt ^ 1)
        heads(2, wt ^ 2)
        branch(2, wt ^ 3, near).wait_recv()
        heads(3, wt ^ 3)
        for ring in rings:
            ring.pass_on()
        out_ref[...] = end_terms(1)
        fc_out[...] = rings[0].finish().astype(low)
        proj_out[...] = rings[1].finish().astype(low)

        def head_here(step, carry):
            source = (ctx + step) % 32
            remote(blocks_ref.at[0], up_ref.at[source], head_send.at[0], head_receive.at[source], (source, wt)).wait_recv()
            return carry

        @pl.when(ctx < 4 * GROUP)
        def _():
            lax.fori_loop(1, 32, head_here, 0)

        for turn, sequence in enumerate((wt, wt ^ 1, wt ^ 2, wt ^ 3)):
            for head in range(GROUP):
                index, other = turn * GROUP + head, sequence * GROUP + head

                @pl.when(other != ctx)
                def _():
                    to_head(index, other).wait_send()

        for item in range(2):
            term(item, 0, 0, 3, near).wait_send()
            term(item, 1, 1, 4, near).wait_send()
            term(item, 2, 2, 5, far).wait_send()
        branch(0, wt, far).wait_send()
        branch(1, wt, near).wait_send()
        branch(2, wt ^ 2, near).wait_send()
        for ring in rings:
            ring.drain()

    vmem = pl.BlockSpec(memory_space=pltpu.VMEM)
    hbm = pl.BlockSpec(memory_space=pl.ANY)
    cut = (block // 32) * 16 + 16
    return pl.pallas_call(
        kernel,
        out_shape=(
            jax.ShapeDtypeStruct((rows, features), jnp.float32),
            jax.ShapeDtypeStruct((rows, features), jnp.float32),
            jax.ShapeDtypeStruct((8, features), jnp.float32),
            jax.ShapeDtypeStruct((4, rows, features), low),
            jax.ShapeDtypeStruct((32, HEAD_DIM, rows), low),
            jax.ShapeDtypeStruct((block, features), low),
            jax.ShapeDtypeStruct((block, features), low),
        ),
        in_specs=[vmem, vmem, hbm, hbm, vmem, vmem, vmem, vmem],
        out_specs=(vmem,) * 7,
        scratch_shapes=[
            pltpu.VMEM(grad_fc.shape, low),
            pltpu.VMEM(grad_proj.shape, low),
            pltpu.VMEM((2, 6, rows, features), low),
            pltpu.VMEM((2, 2, cut, features), low),
            pltpu.VMEM((2, 2, block, features), low),
            pltpu.VMEM((4 * GROUP, HEAD_DIM, rows), low),
            pltpu.SemaphoreType.DMA((2, 6)),
            pltpu.SemaphoreType.DMA((2, 6)),
            pltpu.SemaphoreType.DMA((2, 3)),
            pltpu.SemaphoreType.DMA((2, 3)),
            pltpu.SemaphoreType.DMA((3,)),
            pltpu.SemaphoreType.DMA((3,)),
            pltpu.SemaphoreType.DMA((4 * GROUP,)),
            pltpu.SemaphoreType.DMA((32,)),
            pltpu.SemaphoreType.DMA((2,)),
        ],
        compiler_params=pltpu.CompilerParams(
            collective_id=collective, has_side_effects=True, vmem_limit_bytes=56 * 2**20
        ),
        name="feed_back",
    )(terms_out, terms_two, grad_fc, grad_proj, middle, gain, cotangent, wide_out)


def attend_back(upstream, inverse, place, saved, window_fc, window_proj, own_qkv, collective):
    parts, dim, rows = upstream.shape
    q, kt, k, v, attended, lse = saved
    count, block = k.shape[:2]
    per = block // rows
    features = window_fc.shape[1]
    inner = 112
    low = jnp.bfloat16
    hold, off = place // per, place % per

    def kernel(
        inverse_ref, hold_ref, off_ref, up_ref, q_ref, kt_ref, k_ref, v_ref, att_ref, lse_ref, fc_ref, proj_ref, qkv_ref,
        stacked_ref, grad_ref, fc_out, proj_out,
        up_sorted, up_rows, q_rows, delta_ref, gq_ref, gk_ref, gv_ref, blocks_ref, came_ref, turned_ref, terms_ref, bufs,
        head_send, head_receive, term_send, term_receive, *scratch,
    ):
        ctx, wt = lax.axis_index("ctx"), lax.axis_index("wt")
        y, z, low_x = ctx // 8, ctx // 2 % 4, ctx % 2
        at_y = lambda where: (where * 8 + z * 2 + low_x, wt)
        at_z = lambda where: (y * 8 + where * 2 + low_x, wt)
        near, far = (ctx, wt ^ 1), (ctx, wt ^ 2)
        fc_out[...] = fc_ref[...]
        proj_out[...] = proj_ref[...]
        greet_ctx(ctx, wt, (near, far, (ctx, wt ^ 3)))
        steps = inners((fc_out, proj_out), inner, y, z, at_y, at_z, ctx, wt, (True, False), scratch)
        for one in steps:
            one.begin()

        def arrange(index, carry):
            for sub in range(per):
                piece = up_ref[inverse_ref[index * per + sub]]
                lanes = pl.ds(sub * rows, rows)
                up_sorted[index, :, lanes] = piece
                up_rows[index, lanes, :] = piece.T
            q_rows[index] = q_ref[index].T
            delta_ref[index] = jnp.sum(up_sorted[index].astype(jnp.float32) * att_ref[index], axis=0, keepdims=True)
            gk_ref[index] = jnp.zeros((block, dim), jnp.float32)
            gv_ref[index] = jnp.zeros((block, dim), jnp.float32)
            return carry

        lax.fori_loop(0, count, arrange, 0)
        row = lax.broadcasted_iota(jnp.int32, (block, block), 0)
        col = lax.broadcasted_iota(jnp.int32, (block, block), 1)
        factor = LOG2E * dim**-0.5

        def step(qi, kj, total, diagonal):
            scores = jnp.dot(k_ref[kj], q_ref[qi], preferred_element_type=jnp.float32) * factor
            weights = jnp.exp2(scores - lse_ref[qi])
            if diagonal:
                weights = jnp.where(row <= col, weights, 0.0)
            prob_grad = jnp.dot(v_ref[kj], up_sorted[qi], preferred_element_type=jnp.float32)
            score_grad = (weights * (prob_grad - delta_ref[qi])).astype(low)
            gv_ref[kj] += jnp.dot(weights.astype(low), up_rows[qi], preferred_element_type=jnp.float32)
            gk_ref[kj] += jnp.dot(score_grad, q_rows[qi], preferred_element_type=jnp.float32)
            return total + jnp.dot(kt_ref[kj], score_grad, preferred_element_type=jnp.float32)

        def query_block(qi, carry):
            total = lax.fori_loop(
                0, qi, lambda kj, cur: step(qi, kj, cur, False), jnp.zeros((dim, block), jnp.float32)
            )
            gq_ref[qi] = step(qi, qi, total, True) * dim**-0.5
            return carry

        lax.fori_loop(0, 6, query_block, 0)
        for one in steps:
            one.add_inner()
        lax.fori_loop(6, count, query_block, 0)
        for one in steps:
            one.add_beside()

        def to_owner(index):
            return remote(blocks_ref.at[index], came_ref.at[ctx], head_send.at[index], head_receive.at[ctx], (index, wt))

        def give_back(index, carry):
            def pick(whole, axis):
                cuts = [lax.slice_in_dim(whole, sub * rows, (sub + 1) * rows, axis=axis) for sub in range(per)]
                picked = cuts[0]
                for sub in range(1, per):
                    picked = jnp.where(off_ref[index] == sub, cuts[sub], picked)
                return picked

            blocks_ref[index, :dim] = pick(gq_ref[hold_ref[index]], 1).astype(low)
            blocks_ref[index, dim : 2 * dim] = (pick(gk_ref[hold_ref[index]], 0) * dim**-0.5).T.astype(low)
            blocks_ref[index, 2 * dim :] = pick(gv_ref[hold_ref[index]], 0).T.astype(low)

            @pl.when(index != ctx)
            def _():
                to_owner(index).start()

            @pl.when(index == ctx)
            def _():
                came_ref[index] = blocks_ref[index]

            return carry

        @pl.when(ctx < 4 * GROUP)
        def _():
            lax.fori_loop(0, parts, give_back, 0)

        for one in steps:
            one.collect()

        def owner_here(source, carry):
            @pl.when(source != ctx)
            def _():
                remote(
                    blocks_ref.at[0], came_ref.at[source], head_send.at[0], head_receive.at[source], (source, wt)
                ).wait_recv()

            return carry

        lax.fori_loop(0, 4 * GROUP, owner_here, 0)
        feature = lax.broadcasted_iota(jnp.int32, (dim, rows), 0)

        def make_terms(sequence):
            for head in range(GROUP):
                piece = came_ref[sequence * GROUP + head]
                place_in = feature + head * dim
                mine = (place_in >= 16 * wt) & (place_in < 16 * wt + features // 4)
                for part in range(3):
                    start = part * SPAN + head * dim
                    turned_ref[start : start + dim] = jnp.where(
                        mine, piece[part * dim : (part + 1) * dim].astype(jnp.float32), 0.0
                    ).astype(low)
            stacked_ref[sequence] = turned_ref[...].T
            terms_ref[...] = lax.dot_general(
                stacked_ref[sequence], qkv_ref[...], (((1,), (1,)), ((), ())), preferred_element_type=jnp.float32
            )

        def term(index, source, target, peer):
            return remote(bufs.at[source], bufs.at[target], term_send.at[index], term_receive.at[index], peer)

        make_terms(wt ^ 3)
        bufs[0] = terms_ref[...].astype(low)
        term(0, 0, 3, near).start()
        make_terms(wt ^ 1)
        bufs[1] = terms_ref[...].astype(low)
        term(1, 1, 4, near).start()
        make_terms(wt ^ 2)
        term(0, 0, 3, near).wait_recv()
        bufs[2] = (terms_ref[...] + bufs[3].astype(jnp.float32)).astype(low)
        term(2, 2, 5, far).start()
        make_terms(wt)
        for one in steps:
            one.fill()
        term(1, 1, 4, near).wait_recv()
        grad_ref[...] = terms_ref[...] + bufs[4].astype(jnp.float32)
        term(2, 2, 5, far).wait_recv()
        grad_ref[...] += bufs[5].astype(jnp.float32)
        term(0, 0, 3, near).wait_send()
        term(1, 1, 4, near).wait_send()
        term(2, 2, 5, far).wait_send()

        def sent(index, carry):
            @pl.when(index != ctx)
            def _():
                to_owner(index).wait_send()

            return carry

        @pl.when(ctx < 4 * GROUP)
        def _():
            lax.fori_loop(0, parts, sent, 0)

        for one in steps:
            one.drain()

    smem = pl.BlockSpec(memory_space=pltpu.SMEM)
    vmem = pl.BlockSpec(memory_space=pltpu.VMEM)
    return pl.pallas_call(
        kernel,
        out_shape=(
            jax.ShapeDtypeStruct((4, rows, 3 * SPAN), low),
            jax.ShapeDtypeStruct((rows, features), jnp.float32),
            jax.ShapeDtypeStruct(window_fc.shape, low),
            jax.ShapeDtypeStruct(window_proj.shape, low),
        ),
        in_specs=[smem] * 3 + [vmem] * 10,
        out_specs=(vmem,) * 4,
        scratch_shapes=[
            pltpu.VMEM((count, dim, block), low),
            pltpu.VMEM((count, block, dim), low),
            pltpu.VMEM((count, block, dim), low),
            pltpu.VMEM((count, 1, block), jnp.float32),
            pltpu.VMEM((count, dim, block), jnp.float32),
            pltpu.VMEM((count, block, dim), jnp.float32),
            pltpu.VMEM((count, block, dim), jnp.float32),
            pltpu.VMEM((parts, 3 * dim, rows), low),
            pltpu.VMEM((parts, 3 * dim, rows), low),
            pltpu.VMEM((3 * SPAN, rows), low),
            pltpu.VMEM((rows, features), jnp.float32),
            pltpu.VMEM((6, rows, features), low),
            pltpu.SemaphoreType.DMA((parts,)),
            pltpu.SemaphoreType.DMA((parts,)),
            pltpu.SemaphoreType.DMA((3,)),
            pltpu.SemaphoreType.DMA((3,)),
        ]
        + inner_scratch(inner, features),
        compiler_params=pltpu.CompilerParams(
            collective_id=collective, has_side_effects=True, vmem_limit_bytes=56 * 2**20
        ),
        name="attend_back",
    )(inverse, hold, off, upstream, q, kt, k, v, attended, lse, window_fc, window_proj, own_qkv)


def finish_gradients(first, second, window_fc, window_proj, collective):
    _, size, features = first.shape
    block = window_fc.shape[0]
    inner = 64
    low = jnp.bfloat16

    def kernel(
        first_ref, second_ref, fc_ref, proj_ref, first_out, second_out, fc_out, proj_out,
        work, relay, arrive, ring_send, ring_receive, mlp_send, mlp_receive, out_send, out_receive, fetch, *scratch,
    ):
        ctx, wt = lax.axis_index("ctx"), lax.axis_index("wt")
        y, z, low_x = ctx // 8, ctx // 2 % 4, ctx % 2
        at_y = lambda place: (place * 8 + z * 2 + low_x, wt)
        at_z = lambda place: (y * 8 + place * 2 + low_x, wt)
        loads = [
            pltpu.make_async_copy(first_ref, work.at[0], fetch.at[0]),
            pltpu.make_async_copy(second_ref, work.at[1], fetch.at[1]),
            pltpu.make_async_copy(fc_ref, fc_out.at[y], fetch.at[2]),
            pltpu.make_async_copy(proj_ref, proj_out.at[z], fetch.at[3]),
        ]
        for load in loads:
            load.start()
        peers = [at_y((y + step) % 4) for step in (1, 2, 3)] + [at_z((z + step) % 4) for step in (1, 2, 3)]
        greet(peers + [(ctx ^ 1, wt)] + [(ctx, wt ^ step) for step in (1, 2, 3)])
        for load in loads:
            load.wait()
        rings = [
            RingSum(work.at[0], size, y, at_y, relay.at[0], arrive.at[0], ring_send.at[0], ring_receive.at[0]),
            RingSum(work.at[1], size, z, at_z, relay.at[1], arrive.at[1], ring_send.at[1], ring_receive.at[1]),
        ]
        mlp = [
            RingSpread(fc_out, y, at_y, mlp_send.at[0], mlp_receive.at[0]),
            RingSpread(proj_out, z, at_z, mlp_send.at[1], mlp_receive.at[1]),
        ]
        for ring in rings:
            ring.begin()
        for ring in rings:
            ring.pass_on()
        for one in mlp:
            one.begin()
        first_out[y] = rings[0].finish().astype(low)
        second_out[z] = rings[1].finish().astype(low)
        steps = inners(
            (first_out.at[y], second_out.at[z]), inner, y, z, at_y, at_z, ctx, wt, (True, z < 2), scratch
        )
        for one in steps:
            one.begin()
        for one in steps:
            one.add_inner()
        for one in steps:
            one.add_beside()
        for one in steps:
            one.collect()
        for one in mlp:
            one.pass_on()
        for one in steps:
            one.fill()
        spreads = [
            RingSpread(first_out, y, at_y, out_send.at[0], out_receive.at[0]),
            RingSpread(second_out, z, at_z, out_send.at[1], out_receive.at[1]),
        ]
        for one in spreads:
            one.begin()
        for one in spreads:
            one.pass_on()
        for one in mlp + spreads:
            one.finish()
        for one in rings + steps + mlp + spreads:
            one.drain()

    vmem = pl.BlockSpec(memory_space=pltpu.VMEM)
    hbm = pl.BlockSpec(memory_space=pl.ANY)
    cut = (size // 32) * 16 + 16
    small = jax.ShapeDtypeStruct((4, size, features), low)
    large = jax.ShapeDtypeStruct((4, block, features), low)
    return pl.pallas_call(
        kernel,
        out_shape=(small, small, large, large),
        in_specs=[hbm] * 4,
        out_specs=(vmem,) * 4,
        scratch_shapes=[
            pltpu.VMEM((2, 4 * size, features), low),
            pltpu.VMEM((2, 2, cut, features), low),
            pltpu.VMEM((2, 2, size, features), low),
            pltpu.SemaphoreType.DMA((2, 6)),
            pltpu.SemaphoreType.DMA((2, 6)),
            pltpu.SemaphoreType.DMA((2, 4)),
            pltpu.SemaphoreType.DMA((2, 4)),
            pltpu.SemaphoreType.DMA((2, 4)),
            pltpu.SemaphoreType.DMA((2, 4)),
            pltpu.SemaphoreType.DMA((4,)),
        ]
        + inner_scratch(inner, features),
        compiler_params=pltpu.CompilerParams(
            collective_id=collective, has_side_effects=True, vmem_limit_bytes=56 * 2**20
        ),
        name="finish_gradients",
    )(first.reshape(4 * size, features), second.reshape(4 * size, features), window_fc, window_proj)


def turn_rows(blocks, width):
    _, rows, features = blocks.shape
    share = features // 4

    def kernel(source, out):
        for block in range(4):
            for sender in range(4):
                part = source[block, :, sender * share : (sender + 1) * share].astype(jnp.float32).T
                start = sender * width + block * rows
                out[:, start : start + rows] = part

    vmem = pl.BlockSpec(memory_space=pltpu.VMEM)
    return pl.pallas_call(
        kernel,
        out_shape=jax.ShapeDtypeStruct((share, 4 * width), jnp.float32),
        in_specs=[vmem],
        out_specs=vmem,
        compiler_params=pltpu.CompilerParams(vmem_limit_bytes=48 * 2**20),
        name="turn_rows",
    )(blocks)


def turn_windows(first, second):
    size, features = first.shape[1:]
    share = features // 4
    rest = share - size

    def kernel(first_ref, second_ref, qkv_ref, out_ref):
        def lay(source, block, rows, start):
            for sender in range(4):
                part = source[block, :rows, sender * share : (sender + 1) * share].astype(jnp.float32).T
                at = start + sender * share
                qkv_ref[:, at : at + rows] = part

        for part, (source, block) in enumerate(((first_ref, 0), (first_ref, 2), (second_ref, 0))):
            lay(source, block, size, part * features)
            lay(source, block + 1, rest, part * features + size)
        out_ref[:size] = second_ref[2].astype(jnp.float32)
        out_ref[size:] = second_ref[3, :rest].astype(jnp.float32)

    vmem = pl.BlockSpec(memory_space=pltpu.VMEM)
    return pl.pallas_call(
        kernel,
        out_shape=(
            jax.ShapeDtypeStruct((share, 3 * features), jnp.float32),
            jax.ShapeDtypeStruct((share, features), jnp.float32),
        ),
        in_specs=[vmem] * 2,
        out_specs=(vmem,) * 2,
        compiler_params=pltpu.CompilerParams(vmem_limit_bytes=48 * 2**20),
        cost_estimate=cost(9),
        name="turn_windows",
    )(first, second)


def to_heads(rows_by_token):
    parts = rows_by_token.shape[0] // SPAN
    rows = rows_by_token.shape[1] // 4
    blocks = rows_by_token.reshape(parts, GROUP, HEAD_DIM, 4, rows).transpose(3, 1, 0, 2, 4)
    blocks = blocks.reshape(4 * GROUP, parts * HEAD_DIM, rows)
    spare = lax.axis_size("ctx") - 4 * GROUP
    return jnp.concatenate([blocks, jnp.zeros((spare,) + blocks.shape[1:], blocks.dtype)])


def from_heads(blocks):
    parts, rows = blocks.shape[1] // HEAD_DIM, blocks.shape[2]
    used = blocks[: 4 * GROUP].reshape(4, GROUP, parts, HEAD_DIM, rows)
    return used.transpose(2, 1, 3, 0, 4).reshape(parts * SPAN, 4 * rows)


def local(
    inputs,
    block_order,
    cotangent,
    ln1_gain,
    ln1_bias,
    w_qkv,
    bias_q,
    bias_v,
    w_out,
    bias_out,
    ln2_gain,
    ln2_bias,
    w_fc,
    bias_fc,
    w_proj,
    bias_proj,
):
    ctx, wt = lax.axis_index("ctx"), lax.axis_index("wt")
    ctx_count = lax.axis_size("ctx")
    rows, features = inputs.shape[1:]
    share = features // 4
    ff = w_fc.shape[1] // 4
    shift = 16 * wt

    small = jnp.stack([ln1_gain, ln1_bias, bias_q, bias_v, bias_out, ln2_gain, ln2_bias, bias_proj])
    small = jnp.pad(small, ((0, 8), (0, 0)))
    order = jnp.pad(block_order, ((0, 7), (0, 128 - ctx_count)))
    starts = [384 * member for member in range(4)]
    columns = jnp.stack(
        [
            jnp.concatenate(
                [w_qkv[:, part * features + start : part * features + start + SPAN] for part in range(3)],
                axis=1,
            )
            for start in starts
        ]
    )
    all_inputs, all_small, all_order, own_qkv = prologue((inputs[0], small, order), columns, 1)
    own_qkv = own_qkv.reshape(features, 3 * SPAN)
    vectors = all_small[:, :8].transpose(1, 0, 2).reshape(8, features).astype(jnp.float32)
    gain_one, shift_one, full_bq, full_bv, full_bout, gain_two, shift_two, full_bproj = vectors
    orders = all_order[:, 0, :ctx_count]
    place = lax.dynamic_index_in_dim(orders, jnp.minimum(ctx // GROUP, 3), 0, keepdims=False)
    slots = jnp.arange(ctx_count, dtype=jnp.int32)
    inverse = jnp.sum(jnp.where(place[None, :] == slots[:, None], slots[None, :], 0), axis=1)
    edge = SPAN - share
    below = lax.ppermute(w_out[share - edge :], "wt", [(source, (source + 1) % 4) for source in range(4)])
    above = lax.ppermute(w_out[:edge], "wt", [(source, (source - 1) % 4) for source in range(4)])
    wide_out = lax.dynamic_slice_in_dim(jnp.concatenate([below, w_out, above]), edge - shift, SPAN, 0)
    placed_out = lax.dynamic_update_slice_in_dim(jnp.zeros((SPAN, features), w_out.dtype), w_out, shift, 0)
    pieces = jnp.stack([w_fc[:, member * ff : (member + 1) * ff] for member in range(4)])

    group_tokens = all_inputs.reshape(4 * rows, features).astype(jnp.float32)
    normed_one = layer_norm(group_tokens, gain_one, shift_one).astype(jnp.bfloat16)
    bias_cols = jnp.concatenate(
        [
            lax.dynamic_slice_in_dim(full_bq, 384 * wt, SPAN),
            jnp.zeros((SPAN,), jnp.float32),
            lax.dynamic_slice_in_dim(full_bv, 384 * wt, SPAN),
        ]
    )
    projected = (dot(own_qkv, normed_one, 0, 1) + bias_cols[:, None]).astype(jnp.bfloat16)
    received = exchange(to_heads(projected), "ctx", 3)
    *saved, attended, middle, all_two, own_fc, group_cot = attend(
        received,
        inverse,
        place,
        placed_out,
        inputs[0],
        jnp.concatenate([full_bout[None], gain_two[None], shift_two[None], jnp.zeros((5, features), jnp.float32)]),
        pieces,
        cotangent[0],
        4,
    )

    tokens = inputs[0].astype(jnp.float32)
    all_two = all_two.reshape(4 * rows, features)
    own_fc = own_fc.reshape(features, ff)
    group_cot = group_cot.reshape(4 * rows, features)
    hidden_pre = dot(all_two, own_fc) + bias_fc.astype(jnp.float32)
    hidden_low = gelu_tanh(hidden_pre).astype(jnp.bfloat16)
    hidden_grad = dot(group_cot, w_proj, 1, 1)
    unused_gelu, gelu_back = jax.vjp(gelu_tanh, hidden_pre)
    pre_grad = gelu_back(hidden_grad)[0].astype(jnp.bfloat16)
    low = jnp.bfloat16
    grad_fc = dot(pre_grad, all_two, 0, 0).astype(low)
    grad_proj = dot(hidden_low, group_cot, 0, 0).astype(low)
    projected_out, middle_grad, norm_sums, all_branch, upstream, window_fc, window_proj = feed_back(
        dot(hidden_low, w_proj).reshape(4, rows, features),
        dot(pre_grad, own_fc, 1, 1).reshape(4, rows, features),
        grad_fc,
        grad_proj,
        middle,
        gain_two[None],
        cotangent[0],
        wide_out,
        7,
    )
    outputs = middle + projected_out + full_bproj
    grad_gain_two, grad_shift_two = norm_sums[0], norm_sums[1]
    all_branch = all_branch.reshape(4 * rows, features)

    stacked, normed_one_grad, window_fc, window_proj = attend_back(
        upstream, inverse, place, saved, window_fc, window_proj, own_qkv, 8
    )
    unused_first, first_back = jax.vjp(layer_norm, tokens, gain_one, shift_one)
    input_part, grad_gain_one, grad_shift_one = first_back(normed_one_grad)
    input_grad = middle_grad + input_part

    stacked = stacked.reshape(4 * rows, 3, SPAN)
    own_stacked = lax.dynamic_slice_in_dim(stacked, shift, share, 2).reshape(4 * rows, 3 * share)
    own_attended = lax.dynamic_slice_in_dim(attended.reshape(4 * rows, SPAN), shift, share, 1)
    grad_qkv = dot(own_stacked, normed_one, 0, 0).astype(low)
    grad_out = dot(own_attended, all_branch, 0, 0).astype(low)
    column = lambda value: lax.dynamic_slice_in_dim(value, share * wt, share, 0)
    sums = jnp.sum(own_stacked.astype(jnp.float32), axis=0).reshape(3, share)
    grad_bout = column(jnp.sum(all_branch.astype(jnp.float32), axis=0))
    grad_bproj = column(jnp.sum(group_cot.astype(jnp.float32), axis=0))
    grad_bfc = jnp.sum(pre_grad.astype(jnp.float32), axis=0)
    crossed_vectors = jnp.stack([grad_gain_one, grad_shift_one, grad_gain_two, grad_shift_two]).astype(low)
    kept_vectors = jnp.stack([jnp.concatenate([sums[0], sums[2], grad_bout, grad_bproj]), grad_bfc]).astype(low)
    tail = lambda value: jnp.pad(value, ((0, 16 - value.shape[0]), (0, 0)))
    spare = jnp.zeros((16, features), low)
    first = jnp.concatenate([grad_qkv[:share], tail(crossed_vectors), grad_qkv[share : 2 * share], spare])
    second = jnp.concatenate([grad_qkv[2 * share :], spare, grad_out, tail(kept_vectors)])
    window = (share + 16) // 2
    first, second, all_fc, all_proj = finish_gradients(
        first.reshape(4, window, features), second.reshape(4, window, features), window_fc, window_proj, 9
    )
    sum_fc = turn_rows(all_fc, ff)
    sum_proj = all_proj.reshape(ff, features).astype(jnp.float32)
    sum_qkv, sum_out = turn_windows(first, second)
    rest = share - window
    norms = jnp.sum(first[1, rest : rest + 4].reshape(4, 4, share).astype(jnp.float32), axis=1)
    kept_sums = second[3, rest : rest + 2].astype(jnp.float32)
    sum_bq, sum_bv, sum_bout, sum_bproj = kept_sums[0].reshape(4, share)
    return (
        outputs.astype(jnp.bfloat16)[None],
        input_grad[None],
        norms[0],
        norms[1],
        sum_qkv,
        sum_bq,
        sum_bv,
        sum_out,
        sum_bout,
        norms[2],
        norms[3],
        sum_fc,
        kept_sums[1],
        sum_proj,
        sum_bproj,
    )


def solution(mesh):
    placed = (
        P("wt", "ctx", None),
        P("wt", None),
        P("wt", "ctx", None),
        P("wt"),
        P("wt"),
        P("wt", None),
        P("wt"),
        P("wt"),
        P("wt", None),
        P("wt"),
        P("wt"),
        P("wt"),
        P("wt", None),
        P("wt"),
        P("wt", None),
        P("wt"),
    )
    return jax.shard_map(
        local,
        mesh=mesh,
        in_specs=placed,
        out_specs=(
            P("wt", "ctx", None),
            P("wt", "ctx", None),
            P("wt"),
            P("wt"),
            P("wt", None),
            P("wt"),
            P("wt"),
            P("wt", None),
            P("wt"),
            P("wt"),
            P("wt"),
            P("wt", None),
            P("wt"),
            P("wt", None),
            P("wt"),
        ),
        check_vma=False,
    )
```

time: 1490 us -> 668 us (0.45)
  the two profiles are of different devices: /device:TPU:1 before, /device:TPU:6 now
where the time goes in v3:
time: 668 us; the launch traced here: 655 us
  Pallas kernels  506 us (76%)
  local copies, waits for them, and re-layouts  57.8 us (9%)
  matrix products  48.7 us (7%)
  other arithmetic  40.4 us (6%)
    pallas_call x1, Pallas kernels, finish_gradients(): pl.pallas_call(kernel, out_shape=(small, small, large, large), in_specs=[...  146 us
    pallas_call x1, Pallas kernels, attend_back(): pl.pallas_call(kernel, out_shape=(jax.ShapeDtypeStruct((4, rows, 3 * SPAN...  96.8 us
    pallas_call x1, Pallas kernels, attend(): pl.pallas_call(kernel, out_shape=(lane_first, lane_first, row_first, row_...  94.1 us
    pallas_call x1, Pallas kernels, feed_back(): pl.pallas_call(kernel, out_shape=(jax.ShapeDtypeStruct((rows, features),...  68.7 us
    pallas_call x1, Pallas kernels, prologue(): pl.pallas_call(kernel, out_shape=tuple((jax.ShapeDtypeStruct((4,) + membe...  51.6 us
    dot_general x9, matrix products, dot(): lax.dot_general(left, right, (((left_dim,), (right_dim,)), ((), ())), pre...  48.7 us
    pallas_call x1, Pallas kernels, exchange(): pl.pallas_call(kernel, out_shape=jax.ShapeDtypeStruct(blocks.shape, block...  30.7 us
    unnamed x62, local copies, waits for them, and re-layouts  15.2 us
  transfers between devices with their start and end apart: 2, of which 0 were waited for; matrix products, arithmetic and copies ran while one was open for 14% of the time, Pallas kernels for 27%

profile of v3, /device:TPU:6, one launch (start us, length us, event | category | flops | bytes accessed | tf_op | source)
XLA Modules:
  0.0 655.1 jit_solution(7747737243139920711)
XLA Ops:
  11.4 4.9 fusion.48
  16.9 2.4 concatenate.34
  20.5 2.6 concatenate.36
  23.1 3.4 concatenate.35
  26.6 3.6 pad_maximum_fusion.1.refs_3_
  30.1 51.6 %prologue.1 = (bf16[4,128,1600]{2,1,0:T(8,128)(2,1)}, bf16[4,16,400]{2,1,0:T(8,128)(2,1)}, s32[4,8,128]{2,1,0:T(8,128)}, bf16[4,400,1344]{2,1,0:T(8,128)(2,1)}) custom-call(bf16[128,1600]{1,0:T(8,128)(2,1)} %bitcast.84, bf16[16,400]{1,0:T(8,128)(2,1)} %pad.18.refs_1_, s32[8,128]{1,0:T(8,128)} %pad.19.refs_2_, bf16[4,400,1344]{2,1,0:T(8,128)(2,1)} %pad_maximum_fusion.1.refs_3_), custom_call_target="tpu_custom_call" | custom-call | tf_op jit(solution)/shard_map/prologue/pallas_call | solution.py:123
  91.7 5.3 fusion.13
  99.0 30.7 %exchange_ctx.1.in_ref = bf16[32,192,128]{2,1,0:T(8,128)(2,1)} custom-call(bf16[32,192,128]{2,1,0:T(8,128)(2,1)} %concatenate.39.source), custom_call_target="tpu_custom_call" | custom-call | tf_op jit(solution)/shard_map/exchange_ctx/pallas_call | solution.py:185
  129.8 5.9 slice_bitcast_fusion.3
  138.3 3.1 pad_maximum_fusion.pieces_ref
  141.4 94.1 %attend.1 = (bf16[8,64,512]{2,1,0:T(8,128)(2,1)}, bf16[8,64,512]{2,1,0:T(8,128)(2,1)}, bf16[8,512,64]{2,1,0:T(8,128)(2,1)}, bf16[8,512,64]{2,1,0:T(8,128)(2,1)},...) custom-call(s32[32]{0:T(128)} %select_reduce_fusion.inverse_ref, ...), custom_call_target="tpu_custom_call" | custom-call | tf_op jit(solution)/shard_map/attend/pallas_call | solution.py:624
  235.6 1.9 convert_reduce_fusion.1
  237.5 5.8 fusion.52
  243.3 6.6 %fusion.44 = (bf16[1600]{0:T(1024)(128)(2,1)S(1)}, bf16[512,1600]{0,1:T(8,128)(2,1)}, f32[512,1600]{0,1:T(8,128)S(1)}) fusion(f32[512,1600]{0,1:T(8,128)S(1)} %fusion.52, f32[1600]{0:T(1024)S(1)} %convert_element_type.102, bf16[512,1600]{1,0:T(8,128)(2,1)S(1)} %bitcast.121, bf16[1600,1600]{1,0:T(8,128)(2,1)S(1)} %bitcast.119), kind=kOutput, calls=%fused_computation.109 | convolution fusion | flops 2639460864 | bytes 14960000 | tf_op jit(solution)/shard_map/dot_general | solution.py:34
  249.9 5.3 fusion.42
  255.3 5.6 convolution_convert_fusion.1.proj_ref
  261.6 7.6 %convolution_convert_fusion.2.fc_ref = bf16[1600,1600]{1,0:T(8,128)(2,1)} fusion(bf16[512,1600]{0,1:T(8,128)(2,1)} %get-tuple-element.140, bf16[512,1600]{1,0:T(8,128)(2,1)} %bitcast.120), kind=kOutput, calls=%fused_computation.2 | convolution fusion | flops 2624000000 | bytes 8396800 | tf_op jit(solution)/shard_map/dot_general | solution.py:34
  269.2 7.8 %fusion.14.two_terms = f32[4,128,1600]{2,1,0:T(8,128)} fusion(bf16[1600,1600,1]{1,0,2:T(8,128)(2,1)} %bitcast.116, bf16[512,1600]{0,1:T(8,128)(2,1)S(1)} %copy-done.22), kind=kOutput, calls=%fused_computation.35 | convolution fusion | flops 2621440000 | bytes 10035200 | tf_op jit(solution)/shard_map/dot_general | solution.py:34
  277.1 2.9 fusion.18.wide_ref
  280.0 68.7 %feed_back.1 = (f32[128,1600]{1,0:T(8,128)}, f32[128,1600]{1,0:T(8,128)}, f32[8,1600]{1,0:T(8,128)}, bf16[4,128,1600]{2,1,0:T(8,128)(2,1)}, bf16[32,64,128]{2,1,...) custom-call(f32[4,128,1600]{2,1,0:T(8,128)} %bitcast.97, f32[4,128,1600]{2,1,0:T(8,128)} %fusion.14.two_terms, ...), custom_call_target="tpu_custom_call" | custom-call | tf_op jit(solution)/shard_map/feed_back/pallas_call | solution.py:812
  348.7 96.8 %attend_back.1 = (bf16[4,128,1344]{2,1,0:T(8,128)(2,1)}, f32[128,1600]{1,0:T(8,128)}, bf16[400,1600]{1,0:T(8,128)(2,1)}, bf16[400,1600]{1,0:T(8,128)(2,1)}) custom-call(s32[32]{0:T(128)} %select_reduce_fusion.inverse_ref, s32[32]{0:T(128)} %and_select_fusion.1.hold_ref, s32[32]{0:T(128)} %get-tuple-element.141.off_ref, ...), custom_call_target="tpu_custom_call" | custom-call | tf_op jit(solution)/shard_map/attend_back/pallas_call | solution.py:1018
  445.5 3.0 copy.57
  449.9 2.6 fusion.43
  456.2 3.7 convolution_convert_fusion
  462.6 9.7 %pad_maximum_fusion.3 = (bf16[832,1600]{1,0:T(8,128)(2,1)}, bf16[832,1600]{1,0:T(8,128)(2,1)}) fusion(bf16[16,1600]{1,0:T(8,128)(2,1)S(1)} %fusion.36, bf16[400,1600]{1,0:T(8,128)(2,1)S(1)} %convolution_convert_fusion.3, bf16[16,1600]{1,0:T(8,128)(2,1)S(1)} %broadcast.137, bf16[400,1600]{1,0:T(8,128)(2,1)S(1)} %get-tuple-element.147, ...), kind=kLoop, calls=%fused_computation.31 | loop fusion | flops 21299200 | bytes 10598400 | tf_op jit(solution)/shard_map/concatenate | solution.py:1349
  472.3 145.5 %finish_gradients.1 = (bf16[4,208,1600]{2,1,0:T(8,128)(2,1)}, bf16[4,208,1600]{2,1,0:T(8,128)(2,1)}, bf16[4,400,1600]{2,1,0:T(8,128)(2,1)}, bf16[4,400,1600]{2,1,0:T(8,128)(2,1)}) custom-call(bf16[832,1600]{1,0:T(8,128)(2,1)} %get-tuple-element.167.first_ref, bf16[832,1600]{1,0:T(8,128)(2,1)} %get-tuple-element.166.second_ref, ...), custom_call_target="tpu_custom_call" | custom-call | tf_op jit(solution)/shard_map/finish_gradients/pallas_call | solution.py:1129
  619.3 1.8 copy-done.1
  621.1 1.8 copy-done.2
  622.9 9.0 %turn_windows.1 = (f32[400,4800]{1,0:T(8,128)}, f32[400,1600]{1,0:T(8,128)}) custom-call(bf16[4,208,1600]{2,1,0:T(8,128)(2,1)S(1)} %copy-done.1, bf16[4,208,1600]{2,1,0:T(8,128)(2,1)S(1)} %copy-done.2), custom_call_target="tpu_custom_call" | custom-call | flops 8999999488 | bytes 9000000 | tf_op jit(solution)/shard_map/turn_windows/pallas_call | solution.py:1195
  637.7 2.5 copy-done
  640.2 9.5 %turn_rows.1 = f32[400,6400]{1,0:T(8,128)} custom-call(bf16[4,400,1600]{2,1,0:T(8,128)(2,1)S(1)} %copy-done), custom_call_target="tpu_custom_call" | custom-call | tf_op jit(solution)/shard_map/turn_rows/pallas_call | solution.py:1166
  649.7 5.2 bitcast_convert_fusion
  (140 shorter events, 43.0 us)
Async XLA Ops:
  2.4 274.7 %collective-permute-start.1 = (bf16[48,1600]{1,0:T(8,128)(2,1)}, bf16[48,1600]{1,0:T(8,128)(2,1)}, u32[]{:S(2)}, u32[]{:S(2)}) collective-permute-start(bf16[48,1600]{1,0:T(8,128)(2,1)} %get-tuple-element.164), channel_id=1, source_target_pairs={{0,3},{1,0},{2,1},{3,2},{4,7},{5,4},{6,5},{7,6},{8,11},{9,8},{10,9... | collective-permute-start | bytes 460808 | tf_op jit(solution)/shard_map/ppermute | solution.py:1272
  3.2 273.9 %collective-permute-start = (bf16[48,1600]{1,0:T(8,128)(2,1)}, bf16[48,1600]{1,0:T(8,128)(2,1)}, u32[]{:S(2)}, u32[]{:S(2)}) collective-permute-start(bf16[48,1600]{1,0:T(8,128)(2,1)} %get-tuple-element.165), channel_id=1, source_target_pairs={{0,1},{1,2},{2,3},{3,0},{4,5},{5,6},{6,7},{7,4},{8,9},{9,10},{10,1... | collective-permute-start | bytes 460808 | tf_op jit(solution)/shard_map/ppermute | solution.py:1271
  11.2 5.0 copy-start.3
  30.1 55.0 %copy-start.19 = (bf16[1600]{0:T(1024)(128)(2,1)S(1)}, bf16[1600]{0:T(1024)(128)(2,1)}, u32[]{:S(2)}) copy-start(bf16[1600]{0:T(1024)(128)(2,1)} %param.29) | copy-start | bytes 9604
  30.1 55.1 %copy-start.18 = (bf16[1,128,1600]{1,2,0:T(8,128)(2,1)S(1)}, bf16[1,128,1600]{1,2,0:T(8,128)(2,1)}, u32[]{:S(2)}) copy-start(bf16[1,128,1600]{1,2,0:T(8,128)(2,1)} %param.18) | copy-start | bytes 1228804
  81.7 6.2 copy-start.5
  90.5 1.2 copy-start.13
  129.8 6.0 copy-start.7
  135.7 1.4 copy-start.9
  135.7 2.3 copy-start.10
  135.7 2.7 copy-start.11
  136.0 5.4 copy-start.8
  235.5 7.7 %slice-start.4 = ((s8[5324800]{0:T(1024)(128)(4,1)}), s8[4194304]{0:T(1024)(128)(4,1)S(1)}, s32[]{:S(2)}) async-start(s8[5324800]{0:T(1024)(128)(4,1)} %bitcast.117), calls=%async_computation.4 | async-start | bytes 8388608
  237.5 5.8 slice-start.5
  237.5 5.8 copy-start.20
  237.5 12.5 %slice-start.2 = ((s8[5324800]{0:T(1024)(128)(4,1)}), s8[4194304]{0:T(1024)(128)(4,1)S(1)}, s32[]{:S(2)}) async-start(s8[5324800]{0:T(1024)(128)(4,1)} %bitcast.114), calls=%async_computation.2 | async-start | bytes 8388608
  243.3 6.6 %slice-start.3 = ((s8[5324800]{0:T(1024)(128)(4,1)}), s8[1130496]{0:T(1024)(128)(4,1)S(1)}, s32[]{:S(2)}) async-start(s8[5324800]{0:T(1024)(128)(4,1)} %bitcast.114), calls=%async_computation.3 | async-start | bytes 2260992
  249.9 5.3 copy-start.16
  261.6 7.6 %copy-start.22 = (bf16[512,1600]{0,1:T(8,128)(2,1)S(1)}, bf16[512,1600]{0,1:T(8,128)(2,1)}, u32[]{:S(2)}) copy-start(bf16[512,1600]{0,1:T(8,128)(2,1)} %get-tuple-element.140) | copy-start | bytes 4915204
  448.5 6.8 %copy-start.4 = (bf16[1,128,1600]{2,1,0:T(8,128)(2,1)S(1)}, bf16[1,128,1600]{2,1,0:T(8,128)(2,1)}, u32[]{:S(2)}) copy-start(bf16[1,128,1600]{2,1,0:T(8,128)(2,1)} %copy-done.3) | copy-start | bytes 1228804
  448.5 6.8 %copy-start.6 = (f32[128,1600]{1,0:T(8,128)S(1)}, f32[128,1600]{1,0:T(8,128)}, u32[]{:S(2)}) copy-start(f32[128,1600]{1,0:T(8,128)} %get-tuple-element.66) | copy-start | bytes 2457604
  449.9 6.3 copy-start.14
  459.9 1.5 copy-start.15
  459.9 1.5 copy-start.21
  619.3 1.8 copy-start.1
  621.1 1.8 copy-start.2
  622.9 9.0 %copy-start.12 = (f32[128,1600]{1,0:T(8,128)S(1)}, f32[128,1600]{1,0:T(8,128)}, u32[]{:S(2)}) copy-start(f32[128,1600]{1,0:T(8,128)} %get-tuple-element.51.middle_ref) | copy-start | bytes 2457604
  622.9 9.0 %copy-start.17 = (f32[128,1600]{1,0:T(8,128)S(1)}, f32[128,1600]{1,0:T(8,128)}, u32[]{:S(2)}) copy-start(f32[128,1600]{1,0:T(8,128)} %get-tuple-element.55) | copy-start | bytes 2457604
  632.9 16.8 %slice-start = ((s8[5324800]{0:T(1024)(128)(4,1)}), s8[1130496]{0:T(1024)(128)(4,1)S(1)}, s32[]{:S(2)}) async-start(s8[5324800]{0:T(1024)(128)(4,1)} %bitcast.87), calls=%async_computation | async-start | bytes 2260992
  637.7 2.5 copy-start
  640.2 9.5 %slice-start.1 = ((s8[5324800]{0:T(1024)(128)(4,1)}), s8[4194304]{0:T(1024)(128)(4,1)S(1)}, s32[]{:S(2)}) async-start(s8[5324800]{0:T(1024)(128)(4,1)} %bitcast.87), calls=%async_computation.1 | async-start | bytes 8388608

commit v4 on v3

--- a/solution.py
+++ b/solution.py
@@ -41,160 +41,6 @@
     for peer in peers:
         pl.semaphore_signal(barrier, inc=1, device_id=peer, device_id_type=MESH)
     pl.semaphore_wait(barrier, len(peers))
-
-
-def prologue(arrays, columns, collective):
-    count = len(arrays)
-    pieces = 5
-    extent = columns.shape[1] // pieces
-
-    def kernel(*refs):
-        sources, (blocks,) = refs[:count], refs[count : count + 1]
-        targets, (filled,) = refs[count + 1 : 2 * count + 1], refs[2 * count + 1 : 2 * count + 2]
-        send, receive, local, cross_send, cross_receive, near_send, near_receive = refs[2 * count + 2 :]
-        ctx, wt = lax.axis_index("ctx"), lax.axis_index("wt")
-        low = lax.rem(ctx, 2)
-        near, far, beside = (ctx, wt ^ 1), (ctx, wt ^ 2), (ctx ^ 1, wt)
-        goes, comes = wt ^ (2 + low), wt ^ (3 - low)
-        greet((near, far, beside, (ctx ^ 1, goes), (ctx ^ 1, comes)))
-
-        def move(item, step, source, slot, peer):
-            return pltpu.make_async_remote_copy(
-                source, targets[item].at[slot], send.at[item, step], receive.at[item, step],
-                device_id=peer, device_id_type=MESH,
-            )
-
-        def cross(index):
-            span = pl.ds(index * extent, extent)
-            return pltpu.make_async_remote_copy(
-                blocks.at[goes, span], filled.at[wt, span], cross_send.at[0, index], cross_receive.at[0, index],
-                device_id=(ctx ^ 1, goes), device_id_type=MESH,
-            )
-
-        def crossed(index):
-            span = pl.ds(index * extent, extent)
-            return pltpu.make_async_remote_copy(
-                filled.at[comes, span], filled.at[comes, span], cross_send.at[0, index], cross_receive.at[0, index],
-                device_id=(ctx ^ 1, goes), device_id_type=MESH,
-            )
-
-        def onward(index):
-            span = pl.ds(index * extent, extent)
-            return pltpu.make_async_remote_copy(
-                filled.at[comes, span], filled.at[comes, span], cross_send.at[1, index], cross_receive.at[1, index],
-                device_id=beside, device_id_type=MESH,
-            )
-
-        firsts = [move(item, 0, sources[item], wt, far) for item in range(count)]
-        for copy in firsts:
-            copy.start()
-        crossings = [cross(index) for index in range(pieces)]
-        for copy in crossings:
-            copy.start()
-        seconds = [move(item, 1, sources[item], wt, near) for item in range(count)]
-        own = [
-            pltpu.make_async_copy(sources[item], targets[item].at[wt], local.at[item])
-            for item in range(count)
-        ]
-        own.append(pltpu.make_async_copy(blocks.at[wt], filled.at[wt], local.at[count]))
-        pair = pltpu.make_async_remote_copy(
-            blocks.at[wt ^ 1], filled.at[wt], near_send, near_receive, device_id=near, device_id_type=MESH
-        )
-        for copy in seconds + own + [pair]:
-            copy.start()
-        thirds = []
-        for item in range(count):
-            firsts[item].wait_recv()
-            copy = move(item, 2, targets[item].at[wt ^ 2], wt ^ 2, near)
-            copy.start()
-            thirds.append(copy)
-        onwards = []
-        for index in range(pieces):
-            crossed(index).wait_recv()
-            copy = onward(index)
-            copy.start()
-            onwards.append(copy)
-        for copy in firsts + crossings:
-            copy.wait_send()
-        for copy in seconds + thirds + own + [pair] + onwards:
-            copy.wait()
-
-    hbm = pl.BlockSpec(memory_space=pl.ANY)
-    return pl.pallas_call(
-        kernel,
-        out_shape=tuple(jax.ShapeDtypeStruct((4,) + member.shape, member.dtype) for member in arrays)
-        + (jax.ShapeDtypeStruct(columns.shape, columns.dtype),),
-        in_specs=[hbm] * (count + 1),
-        out_specs=(hbm,) * (count + 1),
-        scratch_shapes=[
-            pltpu.SemaphoreType.DMA((count, 3)),
-            pltpu.SemaphoreType.DMA((count, 3)),
-            pltpu.SemaphoreType.DMA((count + 1,)),
-            pltpu.SemaphoreType.DMA((2, pieces)),
-            pltpu.SemaphoreType.DMA((2, pieces)),
-            pltpu.SemaphoreType.DMA,
-            pltpu.SemaphoreType.DMA,
-        ],
-        compiler_params=pltpu.CompilerParams(collective_id=collective, has_side_effects=True),
-        name="prologue",
-    )(*arrays, columns)
-
-
-def exchange(blocks, axis, collective):
-    count = blocks.shape[0]
-
-    def kernel(source, target, send, receive, local):
-        ctx, wt = lax.axis_index("ctx"), lax.axis_index("wt")
-        own = ctx if axis == "ctx" else wt
-
-        def peer(step):
-            other = lax.rem(own + step, count)
-            return other, ((other, wt) if axis == "ctx" else (ctx, other))
-
-        barrier = pltpu.get_barrier_semaphore()
-
-        def signal(step, carry):
-            pl.semaphore_signal(barrier, inc=1, device_id=peer(step)[1], device_id_type=MESH)
-            return carry
-
-        lax.fori_loop(1, count, signal, 0)
-        pl.semaphore_wait(barrier, count - 1)
-
-        def move(step):
-            other, device = peer(step)
-            return pltpu.make_async_remote_copy(
-                source.at[other], target.at[own], send.at[step], receive.at[step],
-                device_id=device, device_id_type=MESH,
-            )
-
-        def begin(step, carry):
-            move(step).start()
-            return carry
-
-        def finish(step, carry):
-            move(step).wait()
-            return carry
-
-        lax.fori_loop(1, count, begin, 0)
-        keep = pltpu.make_async_copy(source.at[own], target.at[own], local)
-        keep.start()
-        keep.wait()
-        lax.fori_loop(1, count, finish, 0)
-
-    hbm = pl.BlockSpec(memory_space=pl.ANY)
-    return pl.pallas_call(
-        kernel,
-        out_shape=jax.ShapeDtypeStruct(blocks.shape, blocks.dtype),
-        in_specs=[hbm],
-        out_specs=hbm,
-        scratch_shapes=[
-            pltpu.SemaphoreType.DMA((count,)),
-            pltpu.SemaphoreType.DMA((count,)),
-            pltpu.SemaphoreType.DMA,
-        ],
-        compiler_params=pltpu.CompilerParams(collective_id=collective, has_side_effects=True),
-        name="exchange_" + axis,
-    )(blocks)
 
 
 def remote(source, target, send, receive, device):
@@ -267,40 +113,62 @@
 
 
 class RingSpread:
-    def __init__(self, target, place, at, send, receive):
-        self.target, self.place, self.send, self.receive = target, place, send, receive
-        self.up, self.down = (place + 1) % 4, (place + 3) % 4
+    def __init__(self, target, place, at, beside, low_x, send, receive):
+        self.target, self.place, self.beside, self.send, self.receive = target, place, beside, send, receive
+        self.up, self.down, self.opposite = (place + 1) % 4, (place + 3) % 4, (place + 2) % 4
         self.to = (at(self.up), at(self.down))
         rows = target.shape[1]
-        cut = (rows // 32) * 16 + 16
+        alone = (rows + 40) // 80 * 16
+        ring = rows - alone
+        cut = (rows // 32) * 16
+        row = lambda start, extent: pl.ds(pl.multiple_of(start, 16), extent)
         self.parts = (pl.ds(0, cut), pl.ds(cut, rows - cut))
-
-    def whole(self, way, slot):
-        return remote(self.target.at[slot], self.target.at[slot], self.send.at[way], self.receive.at[way], self.to[way])
+        self.mine, self.other = row(low_x * ring, alone), row((1 - low_x) * ring, alone)
+        self.common = row(alone, ring - alone)
+
+    def move(self, slot, rows, index, device):
+        piece = self.target.at[slot, rows]
+        return remote(piece, piece, self.send.at[index], self.receive.at[index], device)
+
+    def early(self, way, slot):
+        return self.move(slot, self.mine, way, self.to[way])
+
+    def rest(self, way, slot):
+        return self.move(slot, self.common, 2 + way, self.to[way])
 
     def half(self, way, slot):
-        piece = self.target.at[slot, self.parts[way]]
-        return remote(piece, piece, self.send.at[2 + way], self.receive.at[2 + way], self.to[way])
+        return self.move(slot, self.parts[way], 4 + way, self.to[way])
+
+    def aside(self, way, rows):
+        return self.move((self.down, self.up)[way], rows, 6 + way, self.beside)
 
     def begin(self):
-        self.whole(0, self.place).start()
-        self.whole(1, self.place).start()
+        for way in range(2):
+            self.early(way, self.place).start()
+        for way in range(2):
+            self.rest(way, self.place).start()
+
+    def share(self):
+        for way, slot in enumerate((self.down, self.up)):
+            self.early(way, slot).wait_recv()
+            self.aside(way, self.mine).start()
 
     def pass_on(self):
-        self.whole(0, self.down).wait_recv()
-        self.half(0, self.down).start()
-        self.whole(1, self.up).wait_recv()
-        self.half(1, self.up).start()
+        for way, slot in enumerate((self.down, self.up)):
+            self.rest(way, slot).wait_recv()
+            self.aside(way, self.other).wait_recv()
+            self.half(way, slot).start()
 
     def finish(self):
-        opposite = (self.place + 2) % 4
-        self.half(0, opposite).wait_recv()
-        self.half(1, opposite).wait_recv()
+        for way in range(2):
+            self.half(way, self.opposite).wait_recv()
 
     def drain(self):
-        for way in range(2):
-            self.whole(way, self.place).wait_send()
-            self.half(way, self.down if way == 0 else self.up).wait_send()
+        for way, slot in enumerate((self.down, self.up)):
+            self.early(way, self.place).wait_send()
+            self.rest(way, self.place).wait_send()
+            self.aside(way, self.mine).wait_send()
+            self.half(way, slot).wait_send()
 
 
 class Inner:
@@ -417,6 +285,223 @@
     ]
 
 
+def project(inputs, block_order, vectors, w_qkv, w_fc, collective):
+    rows, features = inputs.shape
+    share = w_qkv.shape[0]
+    ff = w_fc.shape[1] // 4
+    count = vectors.shape[0]
+    chunks = 5
+    extent = share // chunks
+    low = jnp.bfloat16
+    wide = 3 * SPAN
+
+    def kernel(token_ref, order_ref, *refs):
+        (
+            vectors_ref, qkv_ref, fc_ref,
+            received_ref, orders_ref, vec_ref, own_ref, normed_ref, fc_out,
+            all_ref, small_ref, columns_ref, pieces_ref, parts_ref, sum_ref, turned_ref, blocks_ref,
+            gather_send, gather_receive, cross_send, cross_receive, fc_send, fc_receive, near_send, near_receive,
+            head_send, head_receive,
+        ) = refs
+        ctx, wt = lax.axis_index("ctx"), lax.axis_index("wt")
+        low_x = ctx % 2
+        near, far, beside = (ctx, wt ^ 1), (ctx, wt ^ 2), (ctx ^ 1, wt)
+        goes, comes = wt ^ (2 + low_x), wt ^ (3 - low_x)
+        across = (ctx ^ 1, goes)
+        small_ref[wt, :count] = vectors_ref[...]
+        orders_ref[wt, :1, :32] = order_ref[...]
+        all_ref[wt] = token_ref[...]
+
+        def columns(slot, owner):
+            start = 384 * owner
+            columns_ref[slot, :, :SPAN] = qkv_ref[:, pl.ds(pl.multiple_of(start, 128), SPAN)]
+            keys = qkv_ref[:, pl.ds(pl.multiple_of(features - 64 + start, 128), SPAN + 64)]
+            columns_ref[slot, :, SPAN : 2 * SPAN] = keys[:, 64:]
+            columns_ref[slot, :, 2 * SPAN :] = qkv_ref[:, pl.ds(pl.multiple_of(2 * features + start, 128), SPAN)]
+
+        def piece(target, slot, owner):
+            start = pl.multiple_of(128 * ((25 * owner) // 2), 128)
+            held = fc_ref[:, pl.ds(start, ff + 64)]
+
+            @pl.when(owner % 2 == 0)
+            def _():
+                target[slot] = held[:, :ff]
+
+            @pl.when(owner % 2 == 1)
+            def _():
+                target[slot] = held[:, 64:]
+
+        gathered = (all_ref, small_ref, orders_ref)
+
+        def gather(item, step, slot, peer):
+            ref = gathered[item].at[slot]
+            return remote(ref, ref, gather_send.at[item, step], gather_receive.at[item, step], peer)
+
+        def cross(index):
+            span = pl.ds(index * extent, extent)
+            return remote(columns_ref.at[0, span], own_ref.at[wt, span], cross_send.at[0, index], cross_receive.at[0, index], across)
+
+        def onward(index):
+            part = own_ref.at[comes, pl.ds(index * extent, extent)]
+            return remote(part, part, cross_send.at[1, index], cross_receive.at[1, index], beside)
+
+        def cross_fc():
+            return remote(pieces_ref.at[0], fc_out.at[wt], fc_send, fc_receive, across)
+
+        pair = lambda: remote(columns_ref.at[1], own_ref.at[wt], near_send.at[0], near_receive.at[0], near)
+        pair_fc = lambda: remote(pieces_ref.at[1], fc_out.at[wt], near_send.at[1], near_receive.at[1], near)
+
+        columns(0, goes)
+        greet_ctx(ctx, wt, (near, far, across, (ctx ^ 1, comes)))
+        for item in range(3):
+            gather(item, 0, wt, far).start()
+        for index in range(chunks):
+            cross(index).start()
+        for item in range(3):
+            gather(item, 1, wt, near).start()
+        columns(1, wt ^ 1)
+        pair().start()
+        columns(2, wt)
+        own_ref[wt] = columns_ref[2]
+        piece(pieces_ref, 0, goes)
+        piece(pieces_ref, 1, wt ^ 1)
+        piece(fc_out, wt, wt)
+        for item in range(3):
+            gather(item, 0, wt ^ 2, far).wait_recv()
+            gather(item, 2, wt ^ 2, near).start()
+        for item in range(3):
+            gather(item, 1, wt ^ 1, near).wait_recv()
+        for item in range(3):
+            gather(item, 2, wt ^ 3, near).wait_recv()
+        for sender in range(4):
+            span = slice(sender * share, (sender + 1) * share)
+            vec_ref[:, span] = small_ref[sender, :8].astype(jnp.float32)
+
+        def norm(sequence, carry):
+            normed = layer_norm(all_ref[sequence].astype(jnp.float32), vec_ref[0:1], vec_ref[1:2]).astype(low)
+            normed_ref[sequence] = normed
+            tokens = pl.ds(pl.multiple_of(sequence * rows, rows), rows)
+            for sender in range(4):
+                parts_ref[sender, tokens] = normed[:, sender * share : (sender + 1) * share]
+            return carry
+
+        lax.fori_loop(0, 4, norm, 0)
+        start = pl.ds(pl.multiple_of(384 * wt, 128), SPAN)
+        bias = (vec_ref[2:3, start], jnp.zeros((1, SPAN), jnp.float32), vec_ref[3:4, start])
+        for part in range(3):
+            sum_ref[:, part * SPAN : (part + 1) * SPAN] = jnp.broadcast_to(bias[part], (4 * rows, SPAN))
+
+        def add(sender):
+            sum_ref[...] += jnp.dot(parts_ref[sender], own_ref[sender], preferred_element_type=jnp.float32)
+
+        add(wt)
+        pair().wait_recv()
+        add(wt ^ 1)
+        for index in range(chunks):
+            cross(index).wait_recv()
+            onward(index).start()
+        cross_fc().start()
+        pair_fc().start()
+        add(comes)
+        for index in range(chunks):
+            onward(index).wait_recv()
+        add(goes)
+
+        def to_head(index):
+            return remote(blocks_ref.at[index], received_ref.at[ctx], head_send.at[index], head_receive.at[ctx], (index, wt))
+
+        def heads(sequence, carry):
+            tokens = pl.ds(pl.multiple_of(sequence * rows, rows), rows)
+            turned_ref[...] = sum_ref[tokens].astype(low).T
+            for head in range(GROUP):
+                index = sequence * GROUP + head
+                for part in range(3):
+                    line = part * SPAN + head * HEAD_DIM
+                    blocks_ref[index, part * HEAD_DIM : (part + 1) * HEAD_DIM] = turned_ref[line : line + HEAD_DIM]
+
+                @pl.when(index != ctx)
+                def _():
+                    to_head(index).start()
+
+                @pl.when(index == ctx)
+                def _():
+                    received_ref[index] = blocks_ref[index]
+
+            return carry
+
+        lax.fori_loop(0, 4, heads, 0)
+
+        def head_here(step, carry):
+            source = (ctx + step) % 32
+            remote(
+                blocks_ref.at[0], received_ref.at[source], head_send.at[0], head_receive.at[source], (source, wt)
+            ).wait_recv()
+            return carry
+
+        @pl.when(ctx < 4 * GROUP)
+        def _():
+            lax.fori_loop(1, 32, head_here, 0)
+
+        def sent(index, carry):
+            @pl.when(index != ctx)
+            def _():
+                to_head(index).wait_send()
+
+            return carry
+
+        lax.fori_loop(0, 4 * GROUP, sent, 0)
+        for item in range(3):
+            gather(item, 0, wt, far).wait_send()
+            gather(item, 1, wt, near).wait_send()
+            gather(item, 2, wt ^ 2, near).wait_send()
+        pair().wait_send()
+        for index in range(chunks):
+            cross(index).wait_send()
+            onward(index).wait_send()
+        cross_fc().wait()
+        pair_fc().wait()
+
+    vmem = pl.BlockSpec(memory_space=pltpu.VMEM)
+    hbm = pl.BlockSpec(memory_space=pl.ANY)
+    return pl.pallas_call(
+        kernel,
+        out_shape=(
+            jax.ShapeDtypeStruct((32, 3 * HEAD_DIM, rows), low),
+            jax.ShapeDtypeStruct((4, 8, 128), jnp.int32),
+            jax.ShapeDtypeStruct((8, features), jnp.float32),
+            jax.ShapeDtypeStruct((4, share, wide), low),
+            jax.ShapeDtypeStruct((4, rows, features), low),
+            jax.ShapeDtypeStruct((4, share, ff), low),
+        ),
+        in_specs=[vmem] * 5,
+        out_specs=(vmem,) * 6,
+        scratch_shapes=[
+            pltpu.VMEM((4, rows, features), low),
+            pltpu.VMEM((4, 16, share), low),
+            pltpu.VMEM((3, share, wide), low),
+            pltpu.VMEM((2, share, ff), low),
+            pltpu.VMEM((4, 4 * rows, share), low),
+            pltpu.VMEM((4 * rows, wide), jnp.float32),
+            pltpu.VMEM((wide, rows), low),
+            pltpu.VMEM((4 * GROUP, 3 * HEAD_DIM, rows), low),
+            pltpu.SemaphoreType.DMA((3, 3)),
+            pltpu.SemaphoreType.DMA((3, 3)),
+            pltpu.SemaphoreType.DMA((2, chunks)),
+            pltpu.SemaphoreType.DMA((2, chunks)),
+            pltpu.SemaphoreType.DMA,
+            pltpu.SemaphoreType.DMA,
+            pltpu.SemaphoreType.DMA((2,)),
+            pltpu.SemaphoreType.DMA((2,)),
+            pltpu.SemaphoreType.DMA((4 * GROUP,)),
+            pltpu.SemaphoreType.DMA((32,)),
+        ],
+        compiler_params=pltpu.CompilerParams(
+            collective_id=collective, has_side_effects=True, vmem_limit_bytes=56 * 2**20
+        ),
+        name="project",
+    )(inputs, block_order, vectors, w_qkv, w_fc)
+
+
 def attend(received, inverse, place, placed_out, tokens, small, pieces, cotangent, collective):
     parts, wide, rows = received.shape
     dim = wide // 3
@@ -434,39 +519,30 @@
         q_ref, kt_ref, k_ref, v_ref, att_ref, lse_ref, stacked_ref, middle_ref, all_ref, fc_ref, all_cot_ref,
         vt_ref, blocks_ref, came_ref, turned_ref, terms_ref, bufs,
         head_send, head_receive, term_send, term_receive, all_send, all_receive,
-        cross_send, cross_receive, cot_send, cot_receive, near_sems, local_sems,
+        cross_send, cross_receive, cot_send, cot_receive,
     ):
         ctx, wt = lax.axis_index("ctx"), lax.axis_index("wt")
         low_x = ctx % 2
         near, far, beside = (ctx, wt ^ 1), (ctx, wt ^ 2), (ctx ^ 1, wt)
-        goes, comes = wt ^ (2 + low_x), wt ^ (3 - low_x)
-        greet_ctx(ctx, wt, (near, far, (ctx ^ 1, goes), (ctx ^ 1, comes)))
-
-        def cross(index, source, slot):
+        comes = wt ^ (3 - low_x)
+        greet_ctx(ctx, wt, (near, far))
+
+        def onward(index):
             span = pl.ds(index * extent, extent)
             return remote(
-                source.at[slot, span], fc_ref.at[wt, span], cross_send.at[0, index], cross_receive.at[0, index], (ctx ^ 1, goes)
+                pieces_ref.at[comes, span], fc_ref.at[comes, span], cross_send.at[index], cross_receive.at[index], beside
             )
-
-        def onward(index):
-            piece = fc_ref.at[comes, pl.ds(index * extent, extent)]
-            return remote(piece, piece, cross_send.at[1, index], cross_receive.at[1, index], beside)
 
         def upstream(step, source, slot, peer):
             return remote(source, all_cot_ref.at[slot], cot_send.at[step], cot_receive.at[step], peer)
 
-        pair = remote(pieces_ref.at[wt ^ 1], fc_ref.at[wt], near_sems.at[0], near_sems.at[1], near)
-        own = (
-            pltpu.make_async_copy(pieces_ref.at[wt], fc_ref.at[wt], local_sems.at[0]),
-            pltpu.make_async_copy(cot_ref, all_cot_ref.at[wt], local_sems.at[1]),
-        )
         for index in range(chunks):
-            cross(index, pieces_ref, goes).start()
+            onward(index).start()
         upstream(0, cot_ref, wt, far).start()
         upstream(1, cot_ref, wt, near).start()
-        pair.start()
-        for copy in own:
-            copy.start()
+        all_cot_ref[wt] = cot_ref[...]
+        for slot in (wt, wt ^ 1, comes):
+            fc_ref[slot] = pieces_ref[slot]
 
         def arrange(index, carry):
             for sub in range(per):
@@ -534,9 +610,6 @@
         def _():
             lax.fori_loop(0, parts, give_back, 0)
 
-        for index in range(chunks):
-            cross(index, pieces_ref, goes).wait_recv()
-            onward(index).start()
         upstream(0, cot_ref, wt ^ 2, far).wait_recv()
         upstream(2, all_cot_ref.at[wt ^ 2], wt ^ 2, near).start()
 
@@ -598,11 +671,7 @@
         upstream(0, cot_ref, wt, far).wait_send()
         upstream(1, cot_ref, wt, near).wait_send()
         upstream(2, all_cot_ref.at[wt ^ 2], wt ^ 2, near).wait_send()
-        pair.wait()
-        for copy in own:
-            copy.wait()
         for index in range(chunks):
-            cross(index, pieces_ref, goes).wait_send()
             onward(index).wait()
 
         def sent(index, carry):
@@ -636,8 +705,8 @@
             jax.ShapeDtypeStruct(pieces.shape, low),
             jax.ShapeDtypeStruct((4, rows, features), low),
         ),
-        in_specs=[smem] * 3 + [vmem] * 4 + [hbm] * 2,
-        out_specs=(vmem,) * 9 + (hbm,) * 2,
+        in_specs=[smem] * 3 + [vmem] * 6,
+        out_specs=(vmem,) * 11,
         scratch_shapes=[
             pltpu.VMEM((count, dim, block), low),
             pltpu.VMEM((parts, dim, rows), low),
@@ -651,12 +720,10 @@
             pltpu.SemaphoreType.DMA((3,)),
             pltpu.SemaphoreType.DMA((3,)),
             pltpu.SemaphoreType.DMA((3,)),
-            pltpu.SemaphoreType.DMA((2, chunks)),
-            pltpu.SemaphoreType.DMA((2, chunks)),
+            pltpu.SemaphoreType.DMA((chunks,)),
+            pltpu.SemaphoreType.DMA((chunks,)),
             pltpu.SemaphoreType.DMA((3,)),
             pltpu.SemaphoreType.DMA((3,)),
-            pltpu.SemaphoreType.DMA((2,)),
-            pltpu.SemaphoreType.DMA((2,)),
         ],
         compiler_params=pltpu.CompilerParams(
             collective_id=collective, has_side_effects=True, vmem_limit_bytes=56 * 2**20
@@ -665,15 +732,15 @@
     )(inverse, hold, off, received, placed_out, tokens, small, pieces, cotangent)
 
 
-def feed_back(terms_out, terms_two, grad_fc, grad_proj, middle, gain, cotangent, wide_out, collective):
+def feed_back(hidden, pre_grad, w_proj, own_fc, grad_fc, grad_proj, middle, gain, cotangent, wide_out, collective):
     rows, features = middle.shape
     block = grad_fc.shape[0] // 4
     low = jnp.bfloat16
 
     def kernel(
-        out_terms, two_terms, fc_ref, proj_ref, middle_ref, gain_ref, cot_ref, wide_ref,
+        hidden_ref, pre_ref, w_proj_ref, w_fc_ref, fc_ref, proj_ref, middle_ref, gain_ref, cot_ref, wide_ref,
         out_ref, middle_grad_ref, vectors_ref, all_ref, up_ref, fc_out, proj_out,
-        fc_work, proj_work, bufs, relay, arrive, blocks_ref,
+        fc_work, proj_work, terms_ref, bufs, relay, arrive, blocks_ref,
         ring_send, ring_receive, term_send, term_receive, all_send, all_receive, head_send, head_receive, fetch,
     ):
         ctx, wt = lax.axis_index("ctx"), lax.axis_index("wt")
@@ -694,26 +761,26 @@
                 bufs.at[item, source], bufs.at[item, target], term_send.at[item, step], term_receive.at[item, step], peer
             )
 
-        terms = (two_terms, out_terms)
+        def tokens(sequence):
+            return terms_ref[pl.ds(pl.multiple_of(sequence * rows, rows), rows)]
 
         def begin_terms(item):
-            bufs[item, 0] = terms[item][wt ^ 3].astype(low)
+            bufs[item, 0] = tokens(wt ^ 3).astype(low)
             term(item, 0, 0, 3, near).start()
-            bufs[item, 1] = terms[item][wt ^ 1].astype(low)
+            bufs[item, 1] = tokens(wt ^ 1).astype(low)
             term(item, 1, 1, 4, near).start()
 
         def pass_terms(item):
             term(item, 0, 0, 3, near).wait_recv()
-            bufs[item, 2] = (terms[item][wt ^ 2] + bufs[item, 3].astype(jnp.float32)).astype(low)
+            bufs[item, 2] = (tokens(wt ^ 2) + bufs[item, 3].astype(jnp.float32)).astype(low)
             term(item, 2, 2, 5, far).start()
 
         def end_terms(item):
             term(item, 1, 1, 4, near).wait_recv()
-            total = terms[item][wt] + bufs[item, 4].astype(jnp.float32)
+            total = tokens(wt) + bufs[item, 4].astype(jnp.float32)
             term(item, 2, 2, 5, far).wait_recv()
             return total + bufs[item, 5].astype(jnp.float32)
 
-        begin_terms(0)
         rings = [
             RingSum(fc_work, block, y, at_y, relay.at[0], arrive.at[0], ring_send.at[0], ring_receive.at[0]),
             RingSum(proj_work, block, z, at_z, relay.at[1], arrive.at[1], ring_send.at[1], ring_receive.at[1]),
@@ -721,9 +788,11 @@
         for load, ring in zip(loads, rings):
             load.wait()
             ring.begin()
+        terms_ref[...] = lax.dot_general(
+            pre_ref[...], w_fc_ref[...], (((1,), (1,)), ((), ())), preferred_element_type=jnp.float32
+        )
+        begin_terms(0)
         pass_terms(0)
-        begin_terms(1)
-        pass_terms(1)
         grad = end_terms(0)
         values = middle_ref[...]
         centered = values - jnp.mean(values, axis=-1, keepdims=True)
@@ -766,11 +835,14 @@
                     up_ref[other] = blocks_ref[index]
 
         heads(0, wt)
+        terms_ref[...] = jnp.dot(hidden_ref[...], w_proj_ref[...], preferred_element_type=jnp.float32)
+        begin_terms(1)
         branch(0, wt ^ 2, far).wait_recv()
         branch(2, wt ^ 2, near).start()
         branch(1, wt ^ 1, near).wait_recv()
         heads(1, wt ^ 1)
         heads(2, wt ^ 2)
+        pass_terms(1)
         branch(2, wt ^ 3, near).wait_recv()
         heads(3, wt ^ 3)
         for ring in rings:
@@ -820,11 +892,12 @@
             jax.ShapeDtypeStruct((block, features), low),
             jax.ShapeDtypeStruct((block, features), low),
         ),
-        in_specs=[vmem, vmem, hbm, hbm, vmem, vmem, vmem, vmem],
+        in_specs=[vmem] * 4 + [hbm] * 2 + [vmem] * 4,
         out_specs=(vmem,) * 7,
         scratch_shapes=[
             pltpu.VMEM(grad_fc.shape, low),
             pltpu.VMEM(grad_proj.shape, low),
+            pltpu.VMEM((4 * rows, features), jnp.float32),
             pltpu.VMEM((2, 6, rows, features), low),
             pltpu.VMEM((2, 2, cut, features), low),
             pltpu.VMEM((2, 2, block, features), low),
@@ -843,7 +916,7 @@
             collective_id=collective, has_side_effects=True, vmem_limit_bytes=56 * 2**20
         ),
         name="feed_back",
-    )(terms_out, terms_two, grad_fc, grad_proj, middle, gain, cotangent, wide_out)
+    )(hidden, pre_grad, w_proj, own_fc, grad_fc, grad_proj, middle, gain, cotangent, wide_out)
 
 
 def attend_back(upstream, inverse, place, saved, window_fc, window_proj, own_qkv, collective):
@@ -945,9 +1018,6 @@
         def _():
             lax.fori_loop(0, parts, give_back, 0)
 
-        for one in steps:
-            one.collect()
-
         def owner_here(source, carry):
             @pl.when(source != ctx)
             def _():
@@ -958,6 +1028,8 @@
             return carry
 
         lax.fori_loop(0, 4 * GROUP, owner_here, 0)
+        for one in steps:
+            one.collect()
         feature = lax.broadcasted_iota(jnp.int32, (dim, rows), 0)
 
         def make_terms(sequence):
@@ -989,8 +1061,6 @@
         bufs[2] = (terms_ref[...] + bufs[3].astype(jnp.float32)).astype(low)
         term(2, 2, 5, far).start()
         make_terms(wt)
-        for one in steps:
-            one.fill()
         term(1, 1, 4, near).wait_recv()
         grad_ref[...] = terms_ref[...] + bufs[4].astype(jnp.float32)
         term(2, 2, 5, far).wait_recv()
@@ -1010,6 +1080,8 @@
         def _():
             lax.fori_loop(0, parts, sent, 0)
 
+        for one in steps:
+            one.fill()
         for one in steps:
             one.drain()
 
@@ -1051,42 +1123,54 @@
     )(inverse, hold, off, upstream, q, kt, k, v, attended, lse, window_fc, window_proj, own_qkv)
 
 
-def finish_gradients(first, second, window_fc, window_proj, collective):
-    _, size, features = first.shape
+def finish_gradients(grad_qkv, grad_out, crossed, kept, window_fc, window_proj, collective):
+    share, features = grad_out.shape
+    extra = crossed.shape[0]
+    size = (share + extra) // 2
     block = window_fc.shape[0]
     inner = 64
     low = jnp.bfloat16
 
     def kernel(
-        first_ref, second_ref, fc_ref, proj_ref, first_out, second_out, fc_out, proj_out,
-        work, relay, arrive, ring_send, ring_receive, mlp_send, mlp_receive, out_send, out_receive, fetch, *scratch,
+        qkv_ref, out_ref, crossed_ref, kept_ref, fc_ref, proj_ref,
+        qkv_turned, out_rows, crossed_rows, kept_rows, fc_turned, proj_out,
+        first_out, second_out, fc_out, work, relay, arrive, ring_send, ring_receive, mlp_send, mlp_receive, out_send, out_receive, fetch, *scratch,
     ):
         ctx, wt = lax.axis_index("ctx"), lax.axis_index("wt")
         y, z, low_x = ctx // 8, ctx // 2 % 4, ctx % 2
         at_y = lambda place: (place * 8 + z * 2 + low_x, wt)
         at_z = lambda place: (y * 8 + place * 2 + low_x, wt)
-        loads = [
-            pltpu.make_async_copy(first_ref, work.at[0], fetch.at[0]),
-            pltpu.make_async_copy(second_ref, work.at[1], fetch.at[1]),
-            pltpu.make_async_copy(fc_ref, fc_out.at[y], fetch.at[2]),
-            pltpu.make_async_copy(proj_ref, proj_out.at[z], fetch.at[3]),
+        moves = [
+            (qkv_ref.at[pl.ds(0, share)], work.at[0, pl.ds(0, share)]),
+            (crossed_ref, work.at[0, pl.ds(share, extra)]),
+            (qkv_ref.at[pl.ds(share, share)], work.at[0, pl.ds(share + extra, share)]),
+            (qkv_ref.at[pl.ds(2 * share, share)], work.at[1, pl.ds(0, share)]),
+            (out_ref, work.at[1, pl.ds(share + extra, share)]),
+            (kept_ref, work.at[1, pl.ds(2 * share + extra, extra)]),
         ]
+        moves += [(fc_ref, fc_out.at[y]), (proj_ref, proj_out.at[z])]
+        loads = [pltpu.make_async_copy(source, target, fetch.at[index]) for index, (source, target) in enumerate(moves)]
+        work[0, 2 * share + extra :] = jnp.zeros((extra, features), low)
+        work[1, share : share + extra] = jnp.zeros((extra, features), low)
         for load in loads:
             load.start()
         peers = [at_y((y + step) % 4) for step in (1, 2, 3)] + [at_z((z + step) % 4) for step in (1, 2, 3)]
         greet(peers + [(ctx ^ 1, wt)] + [(ctx, wt ^ step) for step in (1, 2, 3)])
-        for load in loads:
+        for load in loads[:6]:
             load.wait()
         rings = [
             RingSum(work.at[0], size, y, at_y, relay.at[0], arrive.at[0], ring_send.at[0], ring_receive.at[0]),
             RingSum(work.at[1], size, z, at_z, relay.at[1], arrive.at[1], ring_send.at[1], ring_receive.at[1]),
         ]
+        beside = (ctx ^ 1, wt)
         mlp = [
-            RingSpread(fc_out, y, at_y, mlp_send.at[0], mlp_receive.at[0]),
-            RingSpread(proj_out, z, at_z, mlp_send.at[1], mlp_receive.at[1]),
+            RingSpread(fc_out, y, at_y, beside, low_x, mlp_send.at[0], mlp_receive.at[0]),
+            RingSpread(proj_out, z, at_z, beside, low_x, mlp_send.at[1], mlp_receive.at[1]),
         ]
         for ring in rings:
             ring.begin()
+        for load in loads[6:]:
+            load.wait()
         for ring in rings:
             ring.pass_on()
         for one in mlp:
@@ -1098,6 +1182,8 @@
         )
         for one in steps:
             one.begin()
+        for one in mlp:
+            one.share()
         for one in steps:
             one.add_inner()
         for one in steps:
@@ -1109,116 +1195,76 @@
         for one in steps:
             one.fill()
         spreads = [
-            RingSpread(first_out, y, at_y, out_send.at[0], out_receive.at[0]),
-            RingSpread(second_out, z, at_z, out_send.at[1], out_receive.at[1]),
+            RingSpread(first_out, y, at_y, beside, low_x, out_send.at[0], out_receive.at[0]),
+            RingSpread(second_out, z, at_z, beside, low_x, out_send.at[1], out_receive.at[1]),
         ]
         for one in spreads:
             one.begin()
+        for one in mlp:
+            one.finish()
+        for one in spreads:
+            one.share()
+
+        def turn(source, place, extent, target, start, width):
+            for sender in range(4):
+                part = source[place, :extent, sender * share : (sender + 1) * share].astype(jnp.float32).T.astype(low)
+                at = start + sender * width
+                target[:, at : at + extent] = part
+
+        turn(fc_out, 0, block, fc_turned, 0, 4 * block)
         for one in spreads:
             one.pass_on()
-        for one in mlp + spreads:
+        for place in range(1, 4):
+            turn(fc_out, place, block, fc_turned, place * block, 4 * block)
+        for one in spreads:
             one.finish()
+        left = share - size
+        for part, (source, place) in enumerate(((first_out, 0), (first_out, 2), (second_out, 0))):
+            turn(source, place, size, qkv_turned, part * features, share)
+            turn(source, place + 1, left, qkv_turned, part * features + size, share)
+        out_rows[:size] = second_out[2]
+        out_rows[size:] = second_out[3, :left]
+        crossed_rows[...] = first_out[1, left:]
+        kept_rows[...] = second_out[3, left:]
         for one in rings + steps + mlp + spreads:
             one.drain()
 
     vmem = pl.BlockSpec(memory_space=pltpu.VMEM)
     hbm = pl.BlockSpec(memory_space=pl.ANY)
     cut = (size // 32) * 16 + 16
-    small = jax.ShapeDtypeStruct((4, size, features), low)
-    large = jax.ShapeDtypeStruct((4, block, features), low)
     return pl.pallas_call(
         kernel,
-        out_shape=(small, small, large, large),
-        in_specs=[hbm] * 4,
-        out_specs=(vmem,) * 4,
+        out_shape=(
+            jax.ShapeDtypeStruct((share, 3 * features), low),
+            jax.ShapeDtypeStruct((share, features), low),
+            jax.ShapeDtypeStruct((extra, features), low),
+            jax.ShapeDtypeStruct((extra, features), low),
+            jax.ShapeDtypeStruct((share, 16 * block), low),
+            jax.ShapeDtypeStruct((4, block, features), low),
+        ),
+        in_specs=[hbm] * 6,
+        out_specs=(vmem,) * 6,
         scratch_shapes=[
+            pltpu.VMEM((4, size, features), low),
+            pltpu.VMEM((4, size, features), low),
+            pltpu.VMEM((4, block, features), low),
             pltpu.VMEM((2, 4 * size, features), low),
             pltpu.VMEM((2, 2, cut, features), low),
             pltpu.VMEM((2, 2, size, features), low),
             pltpu.SemaphoreType.DMA((2, 6)),
             pltpu.SemaphoreType.DMA((2, 6)),
-            pltpu.SemaphoreType.DMA((2, 4)),
-            pltpu.SemaphoreType.DMA((2, 4)),
-            pltpu.SemaphoreType.DMA((2, 4)),
-            pltpu.SemaphoreType.DMA((2, 4)),
-            pltpu.SemaphoreType.DMA((4,)),
+            pltpu.SemaphoreType.DMA((2, 8)),
+            pltpu.SemaphoreType.DMA((2, 8)),
+            pltpu.SemaphoreType.DMA((2, 8)),
+            pltpu.SemaphoreType.DMA((2, 8)),
+            pltpu.SemaphoreType.DMA((8,)),
         ]
         + inner_scratch(inner, features),
         compiler_params=pltpu.CompilerParams(
             collective_id=collective, has_side_effects=True, vmem_limit_bytes=56 * 2**20
         ),
         name="finish_gradients",
-    )(first.reshape(4 * size, features), second.reshape(4 * size, features), window_fc, window_proj)
-
-
-def turn_rows(blocks, width):
-    _, rows, features = blocks.shape
-    share = features // 4
-
-    def kernel(source, out):
-        for block in range(4):
-            for sender in range(4):
-                part = source[block, :, sender * share : (sender + 1) * share].astype(jnp.float32).T
-                start = sender * width + block * rows
-                out[:, start : start + rows] = part
-
-    vmem = pl.BlockSpec(memory_space=pltpu.VMEM)
-    return pl.pallas_call(
-        kernel,
-        out_shape=jax.ShapeDtypeStruct((share, 4 * width), jnp.float32),
-        in_specs=[vmem],
-        out_specs=vmem,
-        compiler_params=pltpu.CompilerParams(vmem_limit_bytes=48 * 2**20),
-        name="turn_rows",
-    )(blocks)
-
-
-def turn_windows(first, second):
-    size, features = first.shape[1:]
-    share = features // 4
-    rest = share - size
-
-    def kernel(first_ref, second_ref, qkv_ref, out_ref):
-        def lay(source, block, rows, start):
-            for sender in range(4):
-                part = source[block, :rows, sender * share : (sender + 1) * share].astype(jnp.float32).T
-                at = start + sender * share
-                qkv_ref[:, at : at + rows] = part
-
-        for part, (source, block) in enumerate(((first_ref, 0), (first_ref, 2), (second_ref, 0))):
-            lay(source, block, size, part * features)
-            lay(source, block + 1, rest, part * features + size)
-        out_ref[:size] = second_ref[2].astype(jnp.float32)
-        out_ref[size:] = second_ref[3, :rest].astype(jnp.float32)
-
-    vmem = pl.BlockSpec(memory_space=pltpu.VMEM)
-    return pl.pallas_call(
-        kernel,
-        out_shape=(
-            jax.ShapeDtypeStruct((share, 3 * features), jnp.float32),
-            jax.ShapeDtypeStruct((share, features), jnp.float32),
-        ),
-        in_specs=[vmem] * 2,
-        out_specs=(vmem,) * 2,
-        compiler_params=pltpu.CompilerParams(vmem_limit_bytes=48 * 2**20),
-        cost_estimate=cost(9),
-        name="turn_windows",
-    )(first, second)
-
-
-def to_heads(rows_by_token):
-    parts = rows_by_token.shape[0] // SPAN
-    rows = rows_by_token.shape[1] // 4
-    blocks = rows_by_token.reshape(parts, GROUP, HEAD_DIM, 4, rows).transpose(3, 1, 0, 2, 4)
-    blocks = blocks.reshape(4 * GROUP, parts * HEAD_DIM, rows)
-    spare = lax.axis_size("ctx") - 4 * GROUP
-    return jnp.concatenate([blocks, jnp.zeros((spare,) + blocks.shape[1:], blocks.dtype)])
-
-
-def from_heads(blocks):
-    parts, rows = blocks.shape[1] // HEAD_DIM, blocks.shape[2]
-    used = blocks[: 4 * GROUP].reshape(4, GROUP, parts, HEAD_DIM, rows)
-    return used.transpose(2, 1, 3, 0, 4).reshape(parts * SPAN, 4 * rows)
+    )(grad_qkv, grad_out, crossed, kept, window_fc, window_proj)
 
 
 def local(
@@ -1247,22 +1293,12 @@
     shift = 16 * wt
 
     small = jnp.stack([ln1_gain, ln1_bias, bias_q, bias_v, bias_out, ln2_gain, ln2_bias, bias_proj])
-    small = jnp.pad(small, ((0, 8), (0, 0)))
-    order = jnp.pad(block_order, ((0, 7), (0, 128 - ctx_count)))
-    starts = [384 * member for member in range(4)]
-    columns = jnp.stack(
-        [
-            jnp.concatenate(
-                [w_qkv[:, part * features + start : part * features + start + SPAN] for part in range(3)],
-                axis=1,
-            )
-            for start in starts
-        ]
+    received, all_order, vectors, own_qkv, normed_one, pieces = project(
+        inputs[0], block_order, small, w_qkv, w_fc, 1
     )
-    all_inputs, all_small, all_order, own_qkv = prologue((inputs[0], small, order), columns, 1)
     own_qkv = own_qkv.reshape(features, 3 * SPAN)
-    vectors = all_small[:, :8].transpose(1, 0, 2).reshape(8, features).astype(jnp.float32)
-    gain_one, shift_one, full_bq, full_bv, full_bout, gain_two, shift_two, full_bproj = vectors
+    normed_one = normed_one.reshape(4 * rows, features)
+    gain_one, shift_one, _, _, full_bout, gain_two, shift_two, full_bproj = vectors
     orders = all_order[:, 0, :ctx_count]
     place = lax.dynamic_index_in_dim(orders, jnp.minimum(ctx // GROUP, 3), 0, keepdims=False)
     slots = jnp.arange(ctx_count, dtype=jnp.int32)
@@ -1272,19 +1308,7 @@
     above = lax.ppermute(w_out[:edge], "wt", [(source, (source - 1) % 4) for source in range(4)])
     wide_out = lax.dynamic_slice_in_dim(jnp.concatenate([below, w_out, above]), edge - shift, SPAN, 0)
     placed_out = lax.dynamic_update_slice_in_dim(jnp.zeros((SPAN, features), w_out.dtype), w_out, shift, 0)
-    pieces = jnp.stack([w_fc[:, member * ff : (member + 1) * ff] for member in range(4)])
-
-    group_tokens = all_inputs.reshape(4 * rows, features).astype(jnp.float32)
-    normed_one = layer_norm(group_tokens, gain_one, shift_one).astype(jnp.bfloat16)
-    bias_cols = jnp.concatenate(
-        [
-            lax.dynamic_slice_in_dim(full_bq, 384 * wt, SPAN),
-            jnp.zeros((SPAN,), jnp.float32),
-            lax.dynamic_slice_in_dim(full_bv, 384 * wt, SPAN),
-        ]
-    )
-    projected = (dot(own_qkv, normed_one, 0, 1) + bias_cols[:, None]).astype(jnp.bfloat16)
-    received = exchange(to_heads(projected), "ctx", 3)
+
     *saved, attended, middle, all_two, own_fc, group_cot = attend(
         received,
         inverse,
@@ -1310,8 +1334,10 @@
     grad_fc = dot(pre_grad, all_two, 0, 0).astype(low)
     grad_proj = dot(hidden_low, group_cot, 0, 0).astype(low)
     projected_out, middle_grad, norm_sums, all_branch, upstream, window_fc, window_proj = feed_back(
-        dot(hidden_low, w_proj).reshape(4, rows, features),
-        dot(pre_grad, own_fc, 1, 1).reshape(4, rows, features),
+        hidden_low,
+        pre_grad,
+        w_proj,
+        own_fc,
         grad_fc,
         grad_proj,
         middle,
@@ -1344,19 +1370,13 @@
     crossed_vectors = jnp.stack([grad_gain_one, grad_shift_one, grad_gain_two, grad_shift_two]).astype(low)
     kept_vectors = jnp.stack([jnp.concatenate([sums[0], sums[2], grad_bout, grad_bproj]), grad_bfc]).astype(low)
     tail = lambda value: jnp.pad(value, ((0, 16 - value.shape[0]), (0, 0)))
-    spare = jnp.zeros((16, features), low)
-    first = jnp.concatenate([grad_qkv[:share], tail(crossed_vectors), grad_qkv[share : 2 * share], spare])
-    second = jnp.concatenate([grad_qkv[2 * share :], spare, grad_out, tail(kept_vectors)])
-    window = (share + 16) // 2
-    first, second, all_fc, all_proj = finish_gradients(
-        first.reshape(4, window, features), second.reshape(4, window, features), window_fc, window_proj, 9
+    sum_qkv, sum_out, crossed, kept, sum_fc, sum_proj = finish_gradients(
+        grad_qkv, grad_out, tail(crossed_vectors), tail(kept_vectors), window_fc, window_proj, 9
     )
-    sum_fc = turn_rows(all_fc, ff)
-    sum_proj = all_proj.reshape(ff, features).astype(jnp.float32)
-    sum_qkv, sum_out = turn_windows(first, second)
-    rest = share - window
-    norms = jnp.sum(first[1, rest : rest + 4].reshape(4, 4, share).astype(jnp.float32), axis=1)
-    kept_sums = second[3, rest : rest + 2].astype(jnp.float32)
+    sum_qkv, sum_out, sum_fc = (member.astype(jnp.float32) for member in (sum_qkv, sum_out, sum_fc))
+    sum_proj = sum_proj.reshape(ff, features).astype(jnp.float32)
+    norms = jnp.sum(crossed[:4].reshape(4, 4, share).astype(jnp.float32), axis=1)
+    kept_sums = kept[:2].astype(jnp.float32)
     sum_bq, sum_bv, sum_bout, sum_bproj = kept_sums[0].reshape(4, share)
     return (
         outputs.astype(jnp.bfloat16)[None],

time: 668 us -> 590 us (0.88)
  the two profiles are of different devices: /device:TPU:6 before, /device:TPU:1 now
where the time goes in v4:
time: 590 us; the launch traced here: 580 us
  Pallas kernels  491 us (83%)
  matrix products  29.8 us (5%)
  other arithmetic  29.5 us (5%)
  local copies, waits for them, and re-layouts  23.7 us (4%)
    pallas_call x1, Pallas kernels, finish_gradients(): pl.pallas_call(kernel, out_shape=(jax.ShapeDtypeStruct((share, 3 * featur...  146 us
    pallas_call x1, Pallas kernels, attend_back(): pl.pallas_call(kernel, out_shape=(jax.ShapeDtypeStruct((4, rows, 3 * SPAN...  101 us
    pallas_call x1, Pallas kernels, attend(): pl.pallas_call(kernel, out_shape=(lane_first, lane_first, row_first, row_...  91.3 us
    pallas_call x1, Pallas kernels, project(): pl.pallas_call(kernel, out_shape=(jax.ShapeDtypeStruct((32, 3 * HEAD_DIM,...  83.3 us
    pallas_call x1, Pallas kernels, feed_back(): pl.pallas_call(kernel, out_shape=(jax.ShapeDtypeStruct((rows, features),...  69.8 us
    dot_general x6, matrix products, dot(): lax.dot_general(left, right, (((left_dim,), (right_dim,)), ((), ())), pre...  29.8 us
    convert_element_type x3, other arithmetic, local(): member.astype(jnp.float32)  11.9 us
  transfers between devices with their start and end apart: 2, of which 0 were waited for; matrix products, arithmetic and copies ran while one was open for 7% of the time, Pallas kernels for 30%

profile of v4, /device:TPU:1, one launch (start us, length us, event | category | flops | bytes accessed | tf_op | source)
XLA Modules:
  0.0 579.6 jit_solution(15305513917327002278)
XLA Ops:
  0.6 1.0 fusion.35
  1.7 1.5 collective-permute-start.1
  3.2 2.8 collective-permute-start
  11.4 1.2 copy.46
  13.5 83.3 %project.1 = (bf16[32,192,128]{2,1,0:T(8,128)(2,1)}, s32[4,8,128]{2,1,0:T(8,128)}, f32[8,1600]{1,0:T(8,128)}, bf16[4,400,1344]{2,1,0:T(8,128)(2,1)}, bf16[4,128,...) custom-call(bf16[128,1600]{1,0:T(8,128)(2,1)} %bitcast.50, s32[1,32]{1,0:T(1,128)} %order_ref.1, ...), custom_call_target="tpu_custom_call" | custom-call | tf_op jit(solution)/shard_map/project/pallas_call | solution.py:466
  99.1 1.5 slice_reduce_fusion.1
  100.7 0.8 unstack.37
  101.5 1.0 copy.47
  104.0 91.3 %attend.1 = (bf16[8,64,512]{2,1,0:T(8,128)(2,1)}, bf16[8,64,512]{2,1,0:T(8,128)(2,1)}, bf16[8,512,64]{2,1,0:T(8,128)(2,1)}, bf16[8,512,64]{2,1,0:T(8,128)(2,1)},...) custom-call(s32[32]{0:T(128)} %select_reduce_fusion.inverse_ref, ...), custom_call_target="tpu_custom_call" | custom-call | tf_op jit(solution)/shard_map/attend/pallas_call | solution.py:693
  195.3 1.9 convert_reduce_fusion
  197.2 6.7 %multiply_convert_fusion = (bf16[512,1600]{1,0:T(8,128)(2,1)S(1)}, f32[512,1600]{1,0:T(8,128)S(1)}) fusion(f32[1600]{0:T(1024)S(1)} %convert_element_type.72, bf16[512,1600]{1,0:T(8,128)(2,1)} %bitcast.76, bf16[1600,1600]{1,0:T(8,128)(2,1)} %bitcast.54), kind=kOutput, calls=%fused_computation.15 | convolution fusion | flops 2629632000 | bytes 11680000 | tf_op jit(solution)/shard_map/dot_general | solution.py:34
  204.0 4.1 fusion.32
  208.2 5.6 convolution_convert_fusion.2.fc_ref
  213.8 5.6 convolution_convert_fusion.1.proj_ref
  219.4 2.3 fusion.8.wide_ref
  221.7 69.8 %feed_back.1 = (f32[128,1600]{1,0:T(8,128)}, f32[128,1600]{1,0:T(8,128)}, f32[8,1600]{1,0:T(8,128)}, bf16[4,128,1600]{2,1,0:T(8,128)(2,1)}, bf16[32,64,128]{2,1,...) custom-call(bf16[512,1600]{1,0:T(8,128)(2,1)} %copy-done.7, bf16[512,1600]{1,0:T(8,128)(2,1)} %copy-done.8, ...), custom_call_target="tpu_custom_call" | custom-call | tf_op jit(solution)/shard_map/feed_back/pallas_call | solution.py:884
  291.5 100.5 %attend_back.1 = (bf16[4,128,1344]{2,1,0:T(8,128)(2,1)}, f32[128,1600]{1,0:T(8,128)}, bf16[400,1600]{1,0:T(8,128)(2,1)}, bf16[400,1600]{1,0:T(8,128)(2,1)}) custom-call(s32[32]{0:T(128)} %select_reduce_fusion.inverse_ref, s32[32]{0:T(128)} %and_select_fusion.1.hold_ref, s32[32]{0:T(128)} %get-tuple-element.141.off_ref, ...), custom_call_target="tpu_custom_call" | custom-call | tf_op jit(solution)/shard_map/attend_back/pallas_call | solution.py:1090
  392.1 3.0 copy.51
  395.1 1.6 reshape.121
  396.7 2.6 fusion.31
  399.9 0.8 slice.91
  401.6 3.5 convolution_convert_fusion.3.out_ref
  405.0 4.4 convolution_convert_fusion.qkv_ref
  410.1 145.8 %finish_gradients.1 = (bf16[400,4800]{1,0:T(8,128)(2,1)}, bf16[400,1600]{1,0:T(8,128)(2,1)}, bf16[16,1600]{1,0:T(8,128)(2,1)}, bf16[16,1600]{1,0:T(8,128)(2,1)},...) custom-call(bf16[1200,1600]{1,0:T(8,128)(2,1)} %convolution_convert_fusion.qkv_ref, ...), custom_call_target="tpu_custom_call" | custom-call | tf_op jit(solution)/shard_map/finish_gradients/pallas_call | solution.py:1235
  556.0 0.7 slice_convert_fusion.2
  558.4 1.2 copy.53
  559.6 1.0 copy.52
  560.6 0.7 slice_convert_fusion.1
  562.1 3.3 convert_element_type.89
  565.4 3.9 convert_element_type.87
  569.3 4.7 convert_element_type.90
  574.0 5.2 bitcast_convert_fusion
  (92 shorter events, 14.7 us)
Async XLA Ops:
  1.7 217.7 %collective-permute-start.1 = (bf16[48,1600]{1,0:T(8,128)(2,1)S(1)}, bf16[48,1600]{1,0:T(8,128)(2,1)S(1)}, u32[]{:S(2)}, u32[]{:S(2)}) collective-permute-start(bf16[48,1600]{1,0:T(8,128)(2,1)S(1)} %get-tuple-element.143), channel_id=1, source_target_pairs={{0,3},{1,0},{2,1},{3,2},{4,7},{5,4},{6,5},{7,6},{8,11},{9,8},{10,9... | collective-permute-start | bytes 460808 | tf_op jit(solution)/shard_map/ppermute | solution.py:1308
  3.2 216.3 %collective-permute-start = (bf16[48,1600]{1,0:T(8,128)(2,1)S(1)}, bf16[48,1600]{1,0:T(8,128)(2,1)S(1)}, u32[]{:S(2)}, u32[]{:S(2)}) collective-permute-start(bf16[48,1600]{1,0:T(8,128)(2,1)S(1)} %get-tuple-element.144), channel_id=1, source_target_pairs={{0,1},{1,2},{2,3},{3,0},{4,5},{5,6},{6,7},{7,4},{8,9},{9,10},{10,1... | collective-permute-start | bytes 460808 | tf_op jit(solution)/shard_map/ppermute | solution.py:1307
  12.7 0.8 copy-start
  13.5 88.0 %copy-start.15 = (bf16[1600]{0:T(1024)(128)(2,1)S(1)}, bf16[1600]{0:T(1024)(128)(2,1)}, u32[]{:S(2)}) copy-start(bf16[1600]{0:T(1024)(128)(2,1)} %param.29) | copy-start | bytes 9604
  13.5 88.1 %copy-start.14 = (bf16[1,128,1600]{1,2,0:T(8,128)(2,1)S(1)}, bf16[1,128,1600]{1,2,0:T(8,128)(2,1)}, u32[]{:S(2)}) copy-start(bf16[1,128,1600]{1,2,0:T(8,128)(2,1)} %param.18) | copy-start | bytes 1228804
  13.5 89.2 %copy-start.3 = (bf16[400,1600]{1,0:T(8,128)(2,1)S(1)}, bf16[400,1600]{1,0:T(8,128)(2,1)}, u32[]{:S(2)}) copy-start(bf16[400,1600]{1,0:T(8,128)(2,1)} %param.24) | copy-start | bytes 3840004
  102.8 1.1 copy-start.4
  195.3 8.7 %slice-start = ((s8[5324800]{0:T(1024)(128)(4,1)}), s8[4194304]{0:T(1024)(128)(4,1)S(1)}, s32[]{:S(2)}) async-start(s8[5324800]{0:T(1024)(128)(4,1)} %bitcast.52), calls=%async_computation | async-start | bytes 8388608
  197.2 6.8 %slice-start.1 = ((s8[5324800]{0:T(1024)(128)(4,1)}), s8[1130496]{0:T(1024)(128)(4,1)S(1)}, s32[]{:S(2)}) async-start(s8[5324800]{0:T(1024)(128)(4,1)} %bitcast.52), calls=%async_computation.1 | async-start | bytes 2260992
  197.2 6.8 %copy-start.10 = (bf16[4,128,1600]{2,1,0:T(8,128)(2,1)S(1)}, bf16[4,128,1600]{2,1,0:T(8,128)(2,1)}, u32[]{:S(2)}) copy-start(bf16[4,128,1600]{2,1,0:T(8,128)(2,1)} %get-tuple-element.56) | copy-start | bytes 4915204
  203.9 9.8 %copy-start.7 = (bf16[512,1600]{1,0:T(8,128)(2,1)}, bf16[512,1600]{1,0:T(8,128)(2,1)S(1)}, u32[]{:S(2)}) copy-start(bf16[512,1600]{1,0:T(8,128)(2,1)S(1)} %get-tuple-element.156.hidden_ref) | copy-start | bytes 4915204
  204.0 4.2 copy-start.17
  208.1 5.6 copy-start.8
  395.1 5.7 copy-start.1
  395.1 5.6 copy-start.2
  396.7 2.7 copy-start.9
  401.0 4.0 copy-start.11
  401.1 4.0 copy-start.16
  410.1 147.9 %copy-start.6 = (f32[128,1600]{1,0:T(8,128)S(1)}, f32[128,1600]{1,0:T(8,128)}, u32[]{:S(2)}) copy-start(f32[128,1600]{1,0:T(8,128)} %get-tuple-element.53.middle_ref) | copy-start | bytes 2457604
  410.1 147.9 %copy-start.12 = (f32[128,1600]{1,0:T(8,128)S(1)}, f32[128,1600]{1,0:T(8,128)}, u32[]{:S(2)}) copy-start(f32[128,1600]{1,0:T(8,128)} %get-tuple-element.57) | copy-start | bytes 2457604
  410.1 147.9 %copy-start.13 = (f32[128,1600]{1,0:T(8,128)S(1)}, f32[128,1600]{1,0:T(8,128)}, u32[]{:S(2)}) copy-start(f32[128,1600]{1,0:T(8,128)} %get-tuple-element.58) | copy-start | bytes 2457604
  558.0 11.3 %slice-start.4 = ((s8[5120000]{0:T(1024)(128)(4,1)}), s8[925696]{0:T(1024)(128)(4,1)S(1)}, s32[]{:S(2)}) async-start(s8[5120000]{0:T(1024)(128)(4,1)} %bitcast.58), calls=%async_computation.4 | async-start | bytes 1851392
  561.5 3.9 copy-start.5
  562.1 7.2 %slice-start.5 = ((s8[5120000]{0:T(1024)(128)(4,1)}), s8[4194304]{0:T(1024)(128)(4,1)S(1)}, s32[]{:S(2)}) async-start(s8[5120000]{0:T(1024)(128)(4,1)} %bitcast.58), calls=%async_computation.5 | async-start | bytes 8388608
  565.4 8.6 %slice-start.2 = ((s8[5324800]{0:T(1024)(128)(4,1)}), s8[4194304]{0:T(1024)(128)(4,1)S(1)}, s32[]{:S(2)}) async-start(s8[5324800]{0:T(1024)(128)(4,1)} %bitcast.56), calls=%async_computation.2 | async-start | bytes 8388608
  569.3 4.7 slice-start.3

commit v5 on v4

--- a/solution.py
+++ b/solution.py
@@ -113,12 +113,11 @@
 
 
 class RingSpread:
-    def __init__(self, target, place, at, beside, low_x, send, receive):
+    def __init__(self, target, place, at, beside, low_x, alone, send, receive):
         self.target, self.place, self.beside, self.send, self.receive = target, place, beside, send, receive
         self.up, self.down, self.opposite = (place + 1) % 4, (place + 3) % 4, (place + 2) % 4
         self.to = (at(self.up), at(self.down))
         rows = target.shape[1]
-        alone = (rows + 40) // 80 * 16
         ring = rows - alone
         cut = (rows // 32) * 16
         row = lambda start, extent: pl.ds(pl.multiple_of(start, 16), extent)
@@ -145,6 +144,8 @@
     def begin(self):
         for way in range(2):
             self.early(way, self.place).start()
+
+    def go_on(self):
         for way in range(2):
             self.rest(way, self.place).start()
 
@@ -285,7 +286,10 @@
     ]
 
 
-def project(inputs, block_order, vectors, w_qkv, w_fc, collective):
+COLUMNS = -(-3 * SPAN // 128) * 128
+
+
+def project(inputs, block_order, vectors, w_qkv, w_fc, w_out, collective):
     rows, features = inputs.shape
     share = w_qkv.shape[0]
     ff = w_fc.shape[1] // 4
@@ -293,15 +297,16 @@
     chunks = 5
     extent = share // chunks
     low = jnp.bfloat16
-    wide = 3 * SPAN
+    wide = COLUMNS
+    extra = SPAN - share
 
     def kernel(token_ref, order_ref, *refs):
         (
-            vectors_ref, qkv_ref, fc_ref,
-            received_ref, orders_ref, vec_ref, own_ref, normed_ref, fc_out,
+            vectors_ref, qkv_ref, fc_ref, w_out_ref,
+            received_ref, orders_ref, vec_ref, own_ref, normed_ref, fc_out, wide_ref, placed_ref,
             all_ref, small_ref, columns_ref, pieces_ref, parts_ref, sum_ref, turned_ref, blocks_ref,
             gather_send, gather_receive, cross_send, cross_receive, fc_send, fc_receive, near_send, near_receive,
-            head_send, head_receive,
+            head_send, head_receive, edges_ref, edge_send, edge_receive,
         ) = refs
         ctx, wt = lax.axis_index("ctx"), lax.axis_index("wt")
         low_x = ctx % 2
@@ -314,10 +319,18 @@
 
         def columns(slot, owner):
             start = 384 * owner
-            columns_ref[slot, :, :SPAN] = qkv_ref[:, pl.ds(pl.multiple_of(start, 128), SPAN)]
-            keys = qkv_ref[:, pl.ds(pl.multiple_of(features - 64 + start, 128), SPAN + 64)]
-            columns_ref[slot, :, SPAN : 2 * SPAN] = keys[:, 64:]
-            columns_ref[slot, :, 2 * SPAN :] = qkv_ref[:, pl.ds(pl.multiple_of(2 * features + start, 128), SPAN)]
+            queries = qkv_ref[:, pl.ds(pl.multiple_of(start, 128), SPAN)]
+            keys = qkv_ref[:, pl.ds(pl.multiple_of(features - 64 + start, 128), SPAN + 64)][:, 64:]
+            values = qkv_ref[:, pl.ds(pl.multiple_of(2 * features + start, 128), SPAN)]
+            for part, member in enumerate((queries, keys, values)):
+                columns_ref[slot, :, part * SPAN : (part + 1) * SPAN] = member
+            columns_ref[slot, :, 3 * SPAN :] = jnp.zeros((share, wide - 3 * SPAN), low)
+
+        def edge(way):
+            source = (w_out_ref.at[pl.ds(share - extra, extra)], w_out_ref.at[pl.ds(0, extra)])[way]
+            other = ((wt + 1) % 4, (wt + 3) % 4)[way]
+            target = (edges_ref.at[pl.ds(0, extra)], edges_ref.at[pl.ds(extra + share, extra)])[way]
+            return remote(source, target, edge_send.at[way], edge_receive.at[way], (ctx, other))
 
         def piece(target, slot, owner):
             start = pl.multiple_of(128 * ((25 * owner) // 2), 128)
@@ -352,13 +365,15 @@
         pair_fc = lambda: remote(pieces_ref.at[1], fc_out.at[wt], near_send.at[1], near_receive.at[1], near)
 
         columns(0, goes)
-        greet_ctx(ctx, wt, (near, far, across, (ctx ^ 1, comes)))
+        greet_ctx(ctx, wt, (near, far, (ctx, wt ^ 3), across, (ctx ^ 1, comes)))
         for item in range(3):
             gather(item, 0, wt, far).start()
         for index in range(chunks):
             cross(index).start()
         for item in range(3):
             gather(item, 1, wt, near).start()
+        for way in range(2):
+            edge(way).start()
         columns(1, wt ^ 1)
         pair().start()
         columns(2, wt)
@@ -390,9 +405,32 @@
         bias = (vec_ref[2:3, start], jnp.zeros((1, SPAN), jnp.float32), vec_ref[3:4, start])
         for part in range(3):
             sum_ref[:, part * SPAN : (part + 1) * SPAN] = jnp.broadcast_to(bias[part], (4 * rows, SPAN))
+        sum_ref[:, 3 * SPAN :] = jnp.zeros((4 * rows, wide - 3 * SPAN), jnp.float32)
 
         def add(sender):
             sum_ref[...] += jnp.dot(parts_ref[sender], own_ref[sender], preferred_element_type=jnp.float32)
+
+        def to_head(index):
+            return remote(blocks_ref.at[index], received_ref.at[ctx], head_send.at[index], head_receive.at[ctx], (index, wt))
+
+        def heads(sequence, carry):
+            tokens = pl.ds(pl.multiple_of(sequence * rows, rows), rows)
+            turned_ref[...] = sum_ref[tokens].astype(low).T
+            for head in range(GROUP):
+                index = sequence * GROUP + head
+                for part in range(3):
+                    line = part * SPAN + head * HEAD_DIM
+                    blocks_ref[index, part * HEAD_DIM : (part + 1) * HEAD_DIM] = turned_ref[line : line + HEAD_DIM]
+
+                @pl.when(index != ctx)
+                def _():
+                    to_head(index).start()
+
+                @pl.when(index == ctx)
+                def _():
+                    received_ref[index] = blocks_ref[index]
+
+            return carry
 
         add(wt)
         pair().wait_recv()
@@ -406,30 +444,13 @@
         for index in range(chunks):
             onward(index).wait_recv()
         add(goes)
-
-        def to_head(index):
-            return remote(blocks_ref.at[index], received_ref.at[ctx], head_send.at[index], head_receive.at[ctx], (index, wt))
-
-        def heads(sequence, carry):
-            tokens = pl.ds(pl.multiple_of(sequence * rows, rows), rows)
-            turned_ref[...] = sum_ref[tokens].astype(low).T
-            for head in range(GROUP):
-                index = sequence * GROUP + head
-                for part in range(3):
-                    line = part * SPAN + head * HEAD_DIM
-                    blocks_ref[index, part * HEAD_DIM : (part + 1) * HEAD_DIM] = turned_ref[line : line + HEAD_DIM]
-
-                @pl.when(index != ctx)
-                def _():
-                    to_head(index).start()
-
-                @pl.when(index == ctx)
-                def _():
-                    received_ref[index] = blocks_ref[index]
-
-            return carry
-
         lax.fori_loop(0, 4, heads, 0)
+        edges_ref[extra : extra + share] = w_out_ref[...]
+        placed_ref[...] = jnp.zeros((SPAN, features), low)
+        placed_ref[pl.ds(pl.multiple_of(16 * wt, 16), share)] = w_out_ref[...]
+        for way in range(2):
+            edge(way).wait_recv()
+        wide_ref[...] = edges_ref[pl.ds(pl.multiple_of(extra - 16 * wt, 16), SPAN)]
 
         def head_here(step, carry):
             source = (ctx + step) % 32
@@ -455,6 +476,8 @@
             gather(item, 1, wt, near).wait_send()
             gather(item, 2, wt ^ 2, near).wait_send()
         pair().wait_send()
+        for way in range(2):
+            edge(way).wait_send()
         for index in range(chunks):
             cross(index).wait_send()
             onward(index).wait_send()
@@ -472,9 +495,11 @@
             jax.ShapeDtypeStruct((4, share, wide), low),
             jax.ShapeDtypeStruct((4, rows, features), low),
             jax.ShapeDtypeStruct((4, share, ff), low),
+            jax.ShapeDtypeStruct((SPAN, features), low),
+            jax.ShapeDtypeStruct((SPAN, features), low),
         ),
-        in_specs=[vmem] * 5,
-        out_specs=(vmem,) * 6,
+        in_specs=[vmem] * 6,
+        out_specs=(vmem,) * 8,
         scratch_shapes=[
             pltpu.VMEM((4, rows, features), low),
             pltpu.VMEM((4, 16, share), low),
@@ -494,19 +519,22 @@
             pltpu.SemaphoreType.DMA((2,)),
             pltpu.SemaphoreType.DMA((4 * GROUP,)),
             pltpu.SemaphoreType.DMA((32,)),
+            pltpu.VMEM((share + 2 * extra, features), low),
+            pltpu.SemaphoreType.DMA((2,)),
+            pltpu.SemaphoreType.DMA((2,)),
         ],
         compiler_params=pltpu.CompilerParams(
             collective_id=collective, has_side_effects=True, vmem_limit_bytes=56 * 2**20
         ),
         name="project",
-    )(inputs, block_order, vectors, w_qkv, w_fc)
+    )(inputs, block_order, vectors, w_qkv, w_fc, w_out)
 
 
 def attend(received, inverse, place, placed_out, tokens, small, pieces, cotangent, collective):
     parts, wide, rows = received.shape
     dim = wide // 3
     features = tokens.shape[1]
-    block = math.gcd(512, parts * rows)
+    block = math.gcd(1024, parts * rows)
     per = block // rows
     count = parts // per
     chunks = 5
@@ -540,10 +568,6 @@
             onward(index).start()
         upstream(0, cot_ref, wt, far).start()
         upstream(1, cot_ref, wt, near).start()
-        all_cot_ref[wt] = cot_ref[...]
-        for slot in (wt, wt ^ 1, comes):
-            fc_ref[slot] = pieces_ref[slot]
-
         def arrange(index, carry):
             for sub in range(per):
                 piece = in_ref[inverse_ref[index * per + sub]]
@@ -612,6 +636,9 @@
 
         upstream(0, cot_ref, wt ^ 2, far).wait_recv()
         upstream(2, all_cot_ref.at[wt ^ 2], wt ^ 2, near).start()
+        all_cot_ref[wt] = cot_ref[...]
+        for slot in (wt, wt ^ 1, comes):
+            fc_ref[slot] = pieces_ref[slot]
 
         def owner_here(source, carry):
             @pl.when(source != ctx)
@@ -931,8 +958,8 @@
 
     def kernel(
         inverse_ref, hold_ref, off_ref, up_ref, q_ref, kt_ref, k_ref, v_ref, att_ref, lse_ref, fc_ref, proj_ref, qkv_ref,
-        stacked_ref, grad_ref, fc_out, proj_out,
-        up_sorted, up_rows, q_rows, delta_ref, gq_ref, gk_ref, gv_ref, blocks_ref, came_ref, turned_ref, terms_ref, bufs,
+        own_ref, grad_ref, fc_out, proj_out,
+        up_sorted, up_rows, q_rows, delta_ref, gq_ref, gk_ref, gv_ref, blocks_ref, came_ref, turned_ref, plain_ref, terms_ref, bufs,
         head_send, head_receive, term_send, term_receive, *scratch,
     ):
         ctx, wt = lax.axis_index("ctx"), lax.axis_index("wt")
@@ -982,12 +1009,10 @@
             gq_ref[qi] = step(qi, qi, total, True) * dim**-0.5
             return carry
 
-        lax.fori_loop(0, 6, query_block, 0)
+        lax.fori_loop(0, count - 1, query_block, 0)
         for one in steps:
             one.add_inner()
-        lax.fori_loop(6, count, query_block, 0)
-        for one in steps:
-            one.add_beside()
+        lax.fori_loop(count - 1, count, query_block, 0)
 
         def to_owner(index):
             return remote(blocks_ref.at[index], came_ref.at[ctx], head_send.at[index], head_receive.at[ctx], (index, wt))
@@ -1018,6 +1043,9 @@
         def _():
             lax.fori_loop(0, parts, give_back, 0)
 
+        for one in steps:
+            one.add_beside()
+
         def owner_here(source, carry):
             @pl.when(source != ctx)
             def _():
@@ -1031,6 +1059,7 @@
         for one in steps:
             one.collect()
         feature = lax.broadcasted_iota(jnp.int32, (dim, rows), 0)
+        turned_ref[3 * SPAN :] = jnp.zeros((COLUMNS - 3 * SPAN, rows), low)
 
         def make_terms(sequence):
             for head in range(GROUP):
@@ -1038,13 +1067,16 @@
                 place_in = feature + head * dim
                 mine = (place_in >= 16 * wt) & (place_in < 16 * wt + features // 4)
                 for part in range(3):
+                    line = piece[part * dim : (part + 1) * dim]
                     start = part * SPAN + head * dim
-                    turned_ref[start : start + dim] = jnp.where(
-                        mine, piece[part * dim : (part + 1) * dim].astype(jnp.float32), 0.0
-                    ).astype(low)
-            stacked_ref[sequence] = turned_ref[...].T
+                    plain_ref[part, head * dim : (head + 1) * dim] = line
+                    turned_ref[start : start + dim] = jnp.where(mine, line.astype(jnp.float32), 0.0).astype(low)
+            tokens = pl.ds(pl.multiple_of(sequence * rows, rows), rows)
+            for part in range(3):
+                lines = plain_ref[part, pl.ds(pl.multiple_of(16 * wt, 16), features // 4)]
+                own_ref[part * (features // 4) : (part + 1) * (features // 4), tokens] = lines
             terms_ref[...] = lax.dot_general(
-                stacked_ref[sequence], qkv_ref[...], (((1,), (1,)), ((), ())), preferred_element_type=jnp.float32
+                turned_ref[...].T, qkv_ref[...], (((1,), (1,)), ((), ())), preferred_element_type=jnp.float32
             )
 
         def term(index, source, target, peer):
@@ -1090,7 +1122,7 @@
     return pl.pallas_call(
         kernel,
         out_shape=(
-            jax.ShapeDtypeStruct((4, rows, 3 * SPAN), low),
+            jax.ShapeDtypeStruct((3 * features // 4, 4 * rows), low),
             jax.ShapeDtypeStruct((rows, features), jnp.float32),
             jax.ShapeDtypeStruct(window_fc.shape, low),
             jax.ShapeDtypeStruct(window_proj.shape, low),
@@ -1107,7 +1139,8 @@
             pltpu.VMEM((count, block, dim), jnp.float32),
             pltpu.VMEM((parts, 3 * dim, rows), low),
             pltpu.VMEM((parts, 3 * dim, rows), low),
-            pltpu.VMEM((3 * SPAN, rows), low),
+            pltpu.VMEM((COLUMNS, rows), low),
+            pltpu.VMEM((3, SPAN, rows), low),
             pltpu.VMEM((rows, features), jnp.float32),
             pltpu.VMEM((6, rows, features), low),
             pltpu.SemaphoreType.DMA((parts,)),
@@ -1164,17 +1197,21 @@
         ]
         beside = (ctx ^ 1, wt)
         mlp = [
-            RingSpread(fc_out, y, at_y, beside, low_x, mlp_send.at[0], mlp_receive.at[0]),
-            RingSpread(proj_out, z, at_z, beside, low_x, mlp_send.at[1], mlp_receive.at[1]),
+            RingSpread(fc_out, y, at_y, beside, low_x, 144, mlp_send.at[0], mlp_receive.at[0]),
+            RingSpread(proj_out, z, at_z, beside, low_x, 144, mlp_send.at[1], mlp_receive.at[1]),
         ]
+        for load in loads[6:]:
+            load.wait()
+        for one in mlp:
+            one.begin()
         for ring in rings:
             ring.begin()
-        for load in loads[6:]:
-            load.wait()
+        for one in mlp:
+            one.share()
         for ring in rings:
             ring.pass_on()
         for one in mlp:
-            one.begin()
+            one.go_on()
         first_out[y] = rings[0].finish().astype(low)
         second_out[z] = rings[1].finish().astype(low)
         steps = inners(
@@ -1182,8 +1219,6 @@
         )
         for one in steps:
             one.begin()
-        for one in mlp:
-            one.share()
         for one in steps:
             one.add_inner()
         for one in steps:
@@ -1195,11 +1230,12 @@
         for one in steps:
             one.fill()
         spreads = [
-            RingSpread(first_out, y, at_y, beside, low_x, out_send.at[0], out_receive.at[0]),
-            RingSpread(second_out, z, at_z, beside, low_x, out_send.at[1], out_receive.at[1]),
+            RingSpread(first_out, y, at_y, beside, low_x, 32, out_send.at[0], out_receive.at[0]),
+            RingSpread(second_out, z, at_z, beside, low_x, 32, out_send.at[1], out_receive.at[1]),
         ]
         for one in spreads:
             one.begin()
+            one.go_on()
         for one in mlp:
             one.finish()
         for one in spreads:
@@ -1293,22 +1329,16 @@
     shift = 16 * wt
 
     small = jnp.stack([ln1_gain, ln1_bias, bias_q, bias_v, bias_out, ln2_gain, ln2_bias, bias_proj])
-    received, all_order, vectors, own_qkv, normed_one, pieces = project(
-        inputs[0], block_order, small, w_qkv, w_fc, 1
+    received, all_order, vectors, own_qkv, normed_one, pieces, wide_out, placed_out = project(
+        inputs[0], block_order, small, w_qkv, w_fc, w_out, 1
     )
-    own_qkv = own_qkv.reshape(features, 3 * SPAN)
+    own_qkv = own_qkv.reshape(features, COLUMNS)
     normed_one = normed_one.reshape(4 * rows, features)
     gain_one, shift_one, _, _, full_bout, gain_two, shift_two, full_bproj = vectors
     orders = all_order[:, 0, :ctx_count]
     place = lax.dynamic_index_in_dim(orders, jnp.minimum(ctx // GROUP, 3), 0, keepdims=False)
     slots = jnp.arange(ctx_count, dtype=jnp.int32)
     inverse = jnp.sum(jnp.where(place[None, :] == slots[:, None], slots[None, :], 0), axis=1)
-    edge = SPAN - share
-    below = lax.ppermute(w_out[share - edge :], "wt", [(source, (source + 1) % 4) for source in range(4)])
-    above = lax.ppermute(w_out[:edge], "wt", [(source, (source - 1) % 4) for source in range(4)])
-    wide_out = lax.dynamic_slice_in_dim(jnp.concatenate([below, w_out, above]), edge - shift, SPAN, 0)
-    placed_out = lax.dynamic_update_slice_in_dim(jnp.zeros((SPAN, features), w_out.dtype), w_out, shift, 0)
-
     *saved, attended, middle, all_two, own_fc, group_cot = attend(
         received,
         inverse,
@@ -1350,20 +1380,18 @@
     grad_gain_two, grad_shift_two = norm_sums[0], norm_sums[1]
     all_branch = all_branch.reshape(4 * rows, features)
 
-    stacked, normed_one_grad, window_fc, window_proj = attend_back(
+    own_stacked, normed_one_grad, window_fc, window_proj = attend_back(
         upstream, inverse, place, saved, window_fc, window_proj, own_qkv, 8
     )
     unused_first, first_back = jax.vjp(layer_norm, tokens, gain_one, shift_one)
     input_part, grad_gain_one, grad_shift_one = first_back(normed_one_grad)
     input_grad = middle_grad + input_part
 
-    stacked = stacked.reshape(4 * rows, 3, SPAN)
-    own_stacked = lax.dynamic_slice_in_dim(stacked, shift, share, 2).reshape(4 * rows, 3 * share)
     own_attended = lax.dynamic_slice_in_dim(attended.reshape(4 * rows, SPAN), shift, share, 1)
-    grad_qkv = dot(own_stacked, normed_one, 0, 0).astype(low)
+    grad_qkv = dot(own_stacked, normed_one).astype(low)
     grad_out = dot(own_attended, all_branch, 0, 0).astype(low)
     column = lambda value: lax.dynamic_slice_in_dim(value, share * wt, share, 0)
-    sums = jnp.sum(own_stacked.astype(jnp.float32), axis=0).reshape(3, share)
+    sums = jnp.sum(own_stacked.astype(jnp.float32), axis=1).reshape(3, share)
     grad_bout = column(jnp.sum(all_branch.astype(jnp.float32), axis=0))
     grad_bproj = column(jnp.sum(group_cot.astype(jnp.float32), axis=0))
     grad_bfc = jnp.sum(pre_grad.astype(jnp.float32), axis=0)

time: 590 us -> 567 us (0.961)
  Pallas kernels: 491 us -> 477 us
    pallas_call x1, Pallas kernels: 146 us -> 133 us  [finish_gradients(): pl.pallas_call(kernel, out_shape=(jax.ShapeDtypeStruct((share, 3 * featur...]
    pallas_call x1, Pallas kernels: 83.3 us -> 89.6 us  [project(): pl.pallas_call(kernel, out_shape=(jax.ShapeDtypeStruct((32, 3 * HEAD_DIM,...]
  transfers between devices with their start and end apart: 2 -> 0, of which waited for: 0 -> 0; matrix products, arithmetic and copies ran while one was open for 7% -> 0% of each run, Pallas kernels for 30% -> 0%
where the time goes in v5:
time: 567 us; the launch traced here: 559 us
  Pallas kernels  477 us (84%)
  other arithmetic  31.5 us (6%)
  matrix products  30.2 us (5%)
  local copies, waits for them, and re-layouts  18.8 us (3%)
    pallas_call x1, Pallas kernels, finish_gradients(): pl.pallas_call(kernel, out_shape=(jax.ShapeDtypeStruct((share, 3 * featur...  133 us
    pallas_call x1, Pallas kernels, attend_back(): pl.pallas_call(kernel, out_shape=(jax.ShapeDtypeStruct((3 * features // 4...  96.2 us
    pallas_call x1, Pallas kernels, project(): pl.pallas_call(kernel, out_shape=(jax.ShapeDtypeStruct((32, 3 * HEAD_DIM,...  89.6 us
    pallas_call x1, Pallas kernels, attend(): pl.pallas_call(kernel, out_shape=(lane_first, lane_first, row_first, row_...  89 us
    pallas_call x1, Pallas kernels, feed_back(): pl.pallas_call(kernel, out_shape=(jax.ShapeDtypeStruct((rows, features),...  69.3 us
    dot_general x6, matrix products, dot(): lax.dot_general(left, right, (((left_dim,), (right_dim,)), ((), ())), pre...  30.2 us
    convert_element_type x3, other arithmetic, local(): member.astype(jnp.float32)  12.1 us

profile of v5, /device:TPU:1, one launch (start us, length us, event | category | flops | bytes accessed | tf_op | source)
XLA Modules:
  0.0 559.1 jit_solution(4163242435790815176)
XLA Ops:
  6.8 0.7 convert_element_type.71
  7.5 1.2 copy.38
  8.9 2.0 copy.39
  10.8 89.6 %project.1 = (bf16[32,192,128]{2,1,0:T(8,128)(2,1)}, s32[4,8,128]{2,1,0:T(8,128)}, f32[8,1600]{1,0:T(8,128)}, bf16[4,400,1408]{2,1,0:T(8,128)(2,1)}, bf16[4,128,...) custom-call(bf16[128,1600]{1,0:T(8,128)(2,1)} %bitcast.47, ...), custom_call_target="tpu_custom_call" | custom-call | tf_op jit(solution)/shard_map/project/pallas_call | solution.py:489
  100.5 0.7 slice.50
  102.8 1.5 slice_reduce_fusion.1
  104.4 0.8 unstack.37
  105.8 89.0 %attend.1 = (bf16[4,64,1024]{2,1,0:T(8,128)(2,1)}, bf16[4,64,1024]{2,1,0:T(8,128)(2,1)}, bf16[4,1024,64]{2,1,0:T(8,128)(2,1)}, bf16[4,1024,64]{2,1,0:T(8,128)(2,...) custom-call(s32[32]{0:T(128)} %select_reduce_fusion.inverse_ref, ...), custom_call_target="tpu_custom_call" | custom-call | tf_op jit(solution)/shard_map/attend/pallas_call | solution.py:720
  194.9 1.9 convert_reduce_fusion
  196.9 6.7 %multiply_convert_fusion = (bf16[512,1600]{1,0:T(8,128)(2,1)S(1)}, f32[512,1600]{1,0:T(8,128)S(1)}) fusion(f32[1600]{0:T(1024)S(1)} %convert_element_type.71, bf16[512,1600]{1,0:T(8,128)(2,1)} %bitcast.70, bf16[1600,1600]{1,0:T(8,128)(2,1)} %bitcast.51), kind=kOutput, calls=%fused_computation.15 | convolution fusion | flops 2629632000 | bytes 11680000 | tf_op jit(solution)/shard_map/dot_general | solution.py:34
  203.7 4.1 fusion.28
  207.9 5.6 convolution_convert_fusion.2.fc_ref
  213.4 5.6 convolution_convert_fusion.1.proj_ref
  219.0 69.3 %feed_back.1 = (f32[128,1600]{1,0:T(8,128)}, f32[128,1600]{1,0:T(8,128)}, f32[8,1600]{1,0:T(8,128)}, bf16[4,128,1600]{2,1,0:T(8,128)(2,1)}, bf16[32,64,128]{2,1,...) custom-call(bf16[512,1600]{1,0:T(8,128)(2,1)} %copy-done.6, bf16[512,1600]{1,0:T(8,128)(2,1)} %copy-done.7, ...), custom_call_target="tpu_custom_call" | custom-call | tf_op jit(solution)/shard_map/feed_back/pallas_call | solution.py:911
  288.3 96.2 %attend_back.1 = (bf16[1200,512]{1,0:T(8,128)(2,1)}, f32[128,1600]{1,0:T(8,128)}, bf16[400,1600]{1,0:T(8,128)(2,1)}, bf16[400,1600]{1,0:T(8,128)(2,1)}) custom-call(s32[32]{0:T(128)} %select_reduce_fusion.inverse_ref, s32[32]{0:T(128)} %and_select_fusion.1.hold_ref, s32[32]{0:T(128)} %get-tuple-element.126.off_ref, ...), custom_call_target="tpu_custom_call" | custom-call | tf_op jit(solution)/shard_map/attend_back/pallas_call | solution.py:1122
  384.5 1.6 fusion.11
  386.2 1.5 reduce.2
  387.8 1.7 convert_reduce_fusion.1
  389.7 0.8 slice.73
  391.0 1.8 add_bitcast_fusion
  392.9 1.2 copy.44
  394.1 0.7 fusion.23
  394.7 0.9 copy.43
  395.7 3.9 convolution_convert_fusion.3.out_ref
  399.6 4.4 convolution_convert_fusion.qkv_ref
  403.9 133.3 %finish_gradients.1 = (bf16[400,4800]{1,0:T(8,128)(2,1)}, bf16[400,1600]{1,0:T(8,128)(2,1)}, bf16[16,1600]{1,0:T(8,128)(2,1)}, bf16[16,1600]{1,0:T(8,128)(2,1)},...) custom-call(bf16[1200,1600]{1,0:T(8,128)(2,1)} %convolution_convert_fusion.qkv_ref, ...), custom_call_target="tpu_custom_call" | custom-call | tf_op jit(solution)/shard_map/finish_gradients/pallas_call | solution.py:1271
  537.3 0.7 slice_convert_fusion.1
  538.8 1.1 slice_convert_fusion.2
  541.1 3.0 convert_element_type.88
  544.1 4.5 convert_element_type.86
  549.0 4.7 convert_element_type.89
  553.7 5.2 bitcast_convert_fusion
  (65 shorter events, 11.9 us)
Async XLA Ops:
  8.7 2.1 copy-start
  194.9 8.7 %slice-start = ((s8[5324800]{0:T(1024)(128)(4,1)}), s8[4194304]{0:T(1024)(128)(4,1)S(1)}, s32[]{:S(2)}) async-start(s8[5324800]{0:T(1024)(128)(4,1)} %bitcast.49), calls=%async_computation | async-start | bytes 8388608
  196.9 6.8 %slice-start.1 = ((s8[5324800]{0:T(1024)(128)(4,1)}), s8[1130496]{0:T(1024)(128)(4,1)S(1)}, s32[]{:S(2)}) async-start(s8[5324800]{0:T(1024)(128)(4,1)} %bitcast.49), calls=%async_computation.1 | async-start | bytes 2260992
  196.9 6.8 %copy-start.8 = (bf16[4,128,1600]{2,1,0:T(8,128)(2,1)S(1)}, bf16[4,128,1600]{2,1,0:T(8,128)(2,1)}, u32[]{:S(2)}) copy-start(bf16[4,128,1600]{2,1,0:T(8,128)(2,1)} %get-tuple-element.59) | copy-start | bytes 4915204
  203.6 9.8 %copy-start.6 = (bf16[512,1600]{1,0:T(8,128)(2,1)}, bf16[512,1600]{1,0:T(8,128)(2,1)S(1)}, u32[]{:S(2)}) copy-start(bf16[512,1600]{1,0:T(8,128)(2,1)S(1)} %get-tuple-element.141.hidden_ref) | copy-start | bytes 4915204
  203.7 4.2 copy-start.11
  207.8 5.6 %copy-start.7 = (bf16[512,1600]{1,0:T(8,128)(2,1)}, bf16[512,1600]{1,0:T(8,128)(2,1)S(1)}, u32[]{:S(2)}) copy-start(bf16[512,1600]{1,0:T(8,128)(2,1)S(1)} %get-tuple-element.125.pre_ref) | copy-start | bytes 4915204
  288.3 96.2 %copy-start.1 = (bf16[1,128,1600]{2,1,0:T(8,128)(2,1)S(1)}, bf16[1,128,1600]{2,1,0:T(8,128)(2,1)}, u32[]{:S(2)}) copy-start(bf16[1,128,1600]{2,1,0:T(8,128)(2,1)} %copy-done) | copy-start | bytes 1228804
  384.5 6.0 %copy-start.2 = (f32[128,1600]{1,0:T(8,128)S(1)}, f32[128,1600]{1,0:T(8,128)}, u32[]{:S(2)}) copy-start(f32[128,1600]{1,0:T(8,128)} %get-tuple-element.73) | copy-start | bytes 2457604
  384.5 6.5 %copy-start.5 = (f32[128,1600]{1,0:T(8,128)S(1)}, f32[128,1600]{1,0:T(8,128)}, u32[]{:S(2)}) copy-start(f32[128,1600]{1,0:T(8,128)} %get-tuple-element.56.middle_ref) | copy-start | bytes 2457604
  392.8 6.7 %copy-start.9 = (bf16[1200,512]{1,0:T(8,128)(2,1)S(1)}, bf16[1200,512]{1,0:T(8,128)(2,1)}, u32[]{:S(2)}) copy-start(bf16[1200,512]{1,0:T(8,128)(2,1)} %get-tuple-element.74) | copy-start | bytes 3686404
  395.7 3.9 copy-start.10
  538.2 5.9 %copy-start.4 = (bf16[400,4800]{1,0:T(8,128)(2,1)S(1)}, bf16[400,4800]{1,0:T(8,128)(2,1)}, u32[]{:S(2)}) copy-start(bf16[400,4800]{1,0:T(8,128)(2,1)} %get-tuple-element.82) | copy-start | bytes 11520004
  544.1 4.9 copy-start.3
  544.1 9.6 %slice-start.2 = ((s8[5324800]{0:T(1024)(128)(4,1)}), s8[4194304]{0:T(1024)(128)(4,1)S(1)}, s32[]{:S(2)}) async-start(s8[5324800]{0:T(1024)(128)(4,1)} %bitcast.53), calls=%async_computation.2 | async-start | bytes 8388608
  549.0 4.7 slice-start.3

commit v6 on v5

--- a/solution.py
+++ b/solution.py
@@ -378,9 +378,6 @@
         pair().start()
         columns(2, wt)
         own_ref[wt] = columns_ref[2]
-        piece(pieces_ref, 0, goes)
-        piece(pieces_ref, 1, wt ^ 1)
-        piece(fc_out, wt, wt)
         for item in range(3):
             gather(item, 0, wt ^ 2, far).wait_recv()
             gather(item, 2, wt ^ 2, near).start()
@@ -435,6 +432,9 @@
         add(wt)
         pair().wait_recv()
         add(wt ^ 1)
+        piece(pieces_ref, 0, goes)
+        piece(pieces_ref, 1, wt ^ 1)
+        piece(fc_out, wt, wt)
         for index in range(chunks):
             cross(index).wait_recv()
             onward(index).start()

time: 567 us -> 567 us (level)
  no operation moved by 1% of the time
where the time goes in v6:
time: 567 us; the launch traced here: 559 us
  Pallas kernels  477 us (84%)
  other arithmetic  31.5 us (6%)
  matrix products  30.2 us (5%)
  local copies, waits for them, and re-layouts  18.8 us (3%)
    pallas_call x1, Pallas kernels, finish_gradients(): pl.pallas_call(kernel, out_shape=(jax.ShapeDtypeStruct((share, 3 * featur...  133 us
    pallas_call x1, Pallas kernels, attend_back(): pl.pallas_call(kernel, out_shape=(jax.ShapeDtypeStruct((3 * features // 4...  96.4 us
    pallas_call x1, Pallas kernels, project(): pl.pallas_call(kernel, out_shape=(jax.ShapeDtypeStruct((32, 3 * HEAD_DIM,...  89.6 us
    pallas_call x1, Pallas kernels, attend(): pl.pallas_call(kernel, out_shape=(lane_first, lane_first, row_first, row_...  89.1 us
    pallas_call x1, Pallas kernels, feed_back(): pl.pallas_call(kernel, out_shape=(jax.ShapeDtypeStruct((rows, features),...  68.8 us
    dot_general x6, matrix products, dot(): lax.dot_general(left, right, (((left_dim,), (right_dim,)), ((), ())), pre...  30.2 us
    convert_element_type x3, other arithmetic, local(): member.astype(jnp.float32)  12.1 us

profile of v6, /device:TPU:1, one launch (start us, length us, event | category | flops | bytes accessed | tf_op | source)
XLA Modules:
  0.0 559.1 jit_solution(6545976761126298718)
XLA Ops:
  6.8 0.7 convert_element_type.71
  7.5 1.2 copy.38
  8.9 2.0 copy.39
  10.8 89.6 %project.1 = (bf16[32,192,128]{2,1,0:T(8,128)(2,1)}, s32[4,8,128]{2,1,0:T(8,128)}, f32[8,1600]{1,0:T(8,128)}, bf16[4,400,1408]{2,1,0:T(8,128)(2,1)}, bf16[4,128,...) custom-call(bf16[128,1600]{1,0:T(8,128)(2,1)} %bitcast.47, ...), custom_call_target="tpu_custom_call" | custom-call | tf_op jit(solution)/shard_map/project/pallas_call | solution.py:489
  100.5 0.7 slice.50
  102.8 1.5 slice_reduce_fusion.1
  104.4 0.8 unstack.37
  105.8 89.1 %attend.1 = (bf16[4,64,1024]{2,1,0:T(8,128)(2,1)}, bf16[4,64,1024]{2,1,0:T(8,128)(2,1)}, bf16[4,1024,64]{2,1,0:T(8,128)(2,1)}, bf16[4,1024,64]{2,1,0:T(8,128)(2,...) custom-call(s32[32]{0:T(128)} %select_reduce_fusion.inverse_ref, ...), custom_call_target="tpu_custom_call" | custom-call | tf_op jit(solution)/shard_map/attend/pallas_call | solution.py:720
  194.9 1.9 convert_reduce_fusion
  196.9 6.7 %multiply_convert_fusion = (bf16[512,1600]{1,0:T(8,128)(2,1)S(1)}, f32[512,1600]{1,0:T(8,128)S(1)}) fusion(f32[1600]{0:T(1024)S(1)} %convert_element_type.71, bf16[512,1600]{1,0:T(8,128)(2,1)} %bitcast.70, bf16[1600,1600]{1,0:T(8,128)(2,1)} %bitcast.51), kind=kOutput, calls=%fused_computation.15 | convolution fusion | flops 2629632000 | bytes 11680000 | tf_op jit(solution)/shard_map/dot_general | solution.py:34
  203.7 4.1 fusion.28
  207.9 5.6 convolution_convert_fusion.2.fc_ref
  213.4 5.6 convolution_convert_fusion.1.proj_ref
  219.0 68.8 %feed_back.1 = (f32[128,1600]{1,0:T(8,128)}, f32[128,1600]{1,0:T(8,128)}, f32[8,1600]{1,0:T(8,128)}, bf16[4,128,1600]{2,1,0:T(8,128)(2,1)}, bf16[32,64,128]{2,1,...) custom-call(bf16[512,1600]{1,0:T(8,128)(2,1)} %copy-done.6, bf16[512,1600]{1,0:T(8,128)(2,1)} %copy-done.7, ...), custom_call_target="tpu_custom_call" | custom-call | tf_op jit(solution)/shard_map/feed_back/pallas_call | solution.py:911
  287.9 96.4 %attend_back.1 = (bf16[1200,512]{1,0:T(8,128)(2,1)}, f32[128,1600]{1,0:T(8,128)}, bf16[400,1600]{1,0:T(8,128)(2,1)}, bf16[400,1600]{1,0:T(8,128)(2,1)}) custom-call(s32[32]{0:T(128)} %select_reduce_fusion.inverse_ref, s32[32]{0:T(128)} %and_select_fusion.1.hold_ref, s32[32]{0:T(128)} %get-tuple-element.126.off_ref, ...), custom_call_target="tpu_custom_call" | custom-call | tf_op jit(solution)/shard_map/attend_back/pallas_call | solution.py:1122
  384.3 1.6 fusion.11
  385.9 1.5 reduce.2
  387.6 1.7 convert_reduce_fusion.1
  389.5 0.8 slice.73
  390.8 1.8 add_bitcast_fusion
  392.6 1.2 copy.44
  393.8 0.7 fusion.23
  394.5 0.9 copy.43
  395.5 3.9 convolution_convert_fusion.3.out_ref
  399.3 4.4 convolution_convert_fusion.qkv_ref
  403.7 133.5 %finish_gradients.1 = (bf16[400,4800]{1,0:T(8,128)(2,1)}, bf16[400,1600]{1,0:T(8,128)(2,1)}, bf16[16,1600]{1,0:T(8,128)(2,1)}, bf16[16,1600]{1,0:T(8,128)(2,1)},...) custom-call(bf16[1200,1600]{1,0:T(8,128)(2,1)} %convolution_convert_fusion.qkv_ref, ...), custom_call_target="tpu_custom_call" | custom-call | tf_op jit(solution)/shard_map/finish_gradients/pallas_call | solution.py:1271
  537.2 0.7 slice_convert_fusion.1
  538.7 1.1 slice_convert_fusion.2
  541.0 3.0 convert_element_type.88
  544.0 4.5 convert_element_type.86
  549.0 4.7 convert_element_type.89
  553.6 5.2 bitcast_convert_fusion
  (65 shorter events, 11.9 us)
Async XLA Ops:
  8.7 2.1 copy-start
  194.9 8.7 %slice-start = ((s8[5324800]{0:T(1024)(128)(4,1)}), s8[4194304]{0:T(1024)(128)(4,1)S(1)}, s32[]{:S(2)}) async-start(s8[5324800]{0:T(1024)(128)(4,1)} %bitcast.49), calls=%async_computation | async-start | bytes 8388608
  196.9 6.8 %slice-start.1 = ((s8[5324800]{0:T(1024)(128)(4,1)}), s8[1130496]{0:T(1024)(128)(4,1)S(1)}, s32[]{:S(2)}) async-start(s8[5324800]{0:T(1024)(128)(4,1)} %bitcast.49), calls=%async_computation.1 | async-start | bytes 2260992
  196.9 6.8 %copy-start.8 = (bf16[4,128,1600]{2,1,0:T(8,128)(2,1)S(1)}, bf16[4,128,1600]{2,1,0:T(8,128)(2,1)}, u32[]{:S(2)}) copy-start(bf16[4,128,1600]{2,1,0:T(8,128)(2,1)} %get-tuple-element.59) | copy-start | bytes 4915204
  203.6 9.8 %copy-start.6 = (bf16[512,1600]{1,0:T(8,128)(2,1)}, bf16[512,1600]{1,0:T(8,128)(2,1)S(1)}, u32[]{:S(2)}) copy-start(bf16[512,1600]{1,0:T(8,128)(2,1)S(1)} %get-tuple-element.141.hidden_ref) | copy-start | bytes 4915204
  203.7 4.2 copy-start.11
  207.8 5.6 %copy-start.7 = (bf16[512,1600]{1,0:T(8,128)(2,1)}, bf16[512,1600]{1,0:T(8,128)(2,1)S(1)}, u32[]{:S(2)}) copy-start(bf16[512,1600]{1,0:T(8,128)(2,1)S(1)} %get-tuple-element.125.pre_ref) | copy-start | bytes 4915204
  287.8 96.5 %copy-start.1 = (bf16[1,128,1600]{2,1,0:T(8,128)(2,1)S(1)}, bf16[1,128,1600]{2,1,0:T(8,128)(2,1)}, u32[]{:S(2)}) copy-start(bf16[1,128,1600]{2,1,0:T(8,128)(2,1)} %copy-done) | copy-start | bytes 1228804
  384.3 6.0 %copy-start.2 = (f32[128,1600]{1,0:T(8,128)S(1)}, f32[128,1600]{1,0:T(8,128)}, u32[]{:S(2)}) copy-start(f32[128,1600]{1,0:T(8,128)} %get-tuple-element.73) | copy-start | bytes 2457604
  384.3 6.5 %copy-start.5 = (f32[128,1600]{1,0:T(8,128)S(1)}, f32[128,1600]{1,0:T(8,128)}, u32[]{:S(2)}) copy-start(f32[128,1600]{1,0:T(8,128)} %get-tuple-element.56.middle_ref) | copy-start | bytes 2457604
  392.6 6.7 %copy-start.9 = (bf16[1200,512]{1,0:T(8,128)(2,1)S(1)}, bf16[1200,512]{1,0:T(8,128)(2,1)}, u32[]{:S(2)}) copy-start(bf16[1200,512]{1,0:T(8,128)(2,1)} %get-tuple-element.74) | copy-start | bytes 3686404
  395.5 3.9 copy-start.10
  538.1 5.9 %copy-start.4 = (bf16[400,4800]{1,0:T(8,128)(2,1)S(1)}, bf16[400,4800]{1,0:T(8,128)(2,1)}, u32[]{:S(2)}) copy-start(bf16[400,4800]{1,0:T(8,128)(2,1)} %get-tuple-element.82) | copy-start | bytes 11520004
  544.0 4.9 copy-start.3
  544.0 9.6 %slice-start.2 = ((s8[5324800]{0:T(1024)(128)(4,1)}), s8[4194304]{0:T(1024)(128)(4,1)S(1)}, s32[]{:S(2)}) async-start(s8[5324800]{0:T(1024)(128)(4,1)} %bitcast.53), calls=%async_computation.2 | async-start | bytes 8388608
  549.0 4.7 slice-start.3
